TPU v7x, 512 devices: a whole 4x8x8 slice. The times are simulated.
512 devices in a mesh: rep: 64 (over x, z, y_lo), fsdp: 8 (over y_hi, core).
Axes of the slice: x: 4, y: 8 (y_hi: 4, y_lo: 2; y = y_hi * 2 + y_lo), z: 8, core: 2. Of those that a mesh axis runs over, the one named last changes fastest.
Arguments:
- tokens: bfloat16 [64, 2048, 4096], P('rep', 'fsdp'), may hold values from -6 to 6
- targets: bfloat16 [64, 2048, 512], P('rep', 'fsdp'), may hold values from -6 to 6
- anchor: bfloat16 [64, 2048, 512], P('rep', 'fsdp'), may hold values from -6 to 6
- adam_m: bfloat16 [64, 2048, 512], P('rep', 'fsdp'), may hold values from -6 to 6
- adam_v: bfloat16 [64, 2048, 512], P('rep', 'fsdp'), may hold values from 0.25 to 4
- outer_mom: bfloat16 [64, 2048, 512], P('rep', 'fsdp'), may hold values from -4 to 4
- partner: int32 [32], replicated, may hold values from 0 to 31, as said below
Outputs:
- new_anchor: bfloat16 [64, 2048, 512], P('rep', 'fsdp')
- new_m: bfloat16 [64, 2048, 512], P('rep', 'fsdp')
- new_v: bfloat16 [64, 2048, 512], P('rep', 'fsdp')
- new_mom: bfloat16 [64, 2048, 512], P('rep', 'fsdp')
Inputs may be any that keep to these rules, and one draw needn't show every extreme that they name: A matching: partner[partner[r]] = r and partner[r] != r for every replica r.
All inputs are finite; a program needn't handle non-finite values.
Results may differ from a plain program's by a relative error of at most 0.0075.
Values may be sent and summed in bfloat16 or wider, within the bound.
No kernel may reach another device: no remote copies, remote signals or barrier semaphores. Data moves between devices by JAX's collectives and lax.ppermute only.
A program may use at most 64 MiB of HBM per device.

v0:
```python
import jax
import jax.numpy as jnp
from jax import lax
from jax.sharding import PartitionSpec as P

beta_one = 0.9
beta_two = 0.95
epsilon = 1e-08
inner_rate = 0.1
weight_decay = 0.1
outer_rate = 0.7
outer_momentum = 0.9
pull_rate = 0.5


def partner_2(value, axis, distance):
    return lax.ppermute(value, axis, [(i, i ^ 1 << distance) for i in range(lax.axis_size(axis))])


def contract_rows(left, right):
    return lax.dot_general(
        left, right, (((0,), (0,)), ((), ())), preferred_element_type=jnp.float32
    )


def shards(tokens, targets, anchor, adam_m, adam_v, outer_mom, partner):
    side = lax.axis_index("rep") % 2
    inputs = tokens[0]
    wanted = targets[0]
    features = inputs.shape[1]
    half = features // 2
    count_tok = inputs.shape[0]
    outputs = wanted.shape[1]
    own_cols = lax.dynamic_slice_in_dim(inputs, side * half, half, 1)
    far_cols = lax.dynamic_slice_in_dim(inputs, (1 - side) * half, half, 1)
    shard = anchor[0]
    shard_rows = shard.shape[0]
    facing_shard = partner_2(shard, "rep", 0)
    pieces = (
        lax.all_gather(shard, "fsdp", axis=0, tiled=True),
        lax.all_gather(facing_shard, "fsdp", axis=0, tiled=True),
    )
    total = jnp.dot(own_cols, pieces[0], preferred_element_type=jnp.float32)
    keys = total + jnp.dot(far_cols, pieces[1], preferred_element_type=jnp.float32)
    keys = keys * features ** (-0.5)
    residual = (keys - wanted.astype(jnp.float32)).astype(jnp.bfloat16)
    replica_tokens = 2 * lax.axis_size("fsdp") * count_tok
    norm_scale = replica_tokens ** (-0.5)
    own_term = contract_rows(own_cols, residual)
    far_term = contract_rows(far_cols, residual)
    incoming = partner_2(far_term.astype(jnp.bfloat16), "rep", 0).astype(far_term.dtype)
    grad = (
        lax.psum_scatter(own_term + incoming, "fsdp", scatter_dimension=0, tiled=True) * norm_scale
    )
    theta = shard.astype(jnp.float32)
    first = beta_one * adam_m[0].astype(jnp.float32) + (1.0 - beta_one) * grad
    second = beta_two * adam_v[0].astype(jnp.float32) + (1.0 - beta_two) * grad * grad
    delta = inner_rate * (first / (jnp.sqrt(second) + epsilon) + weight_decay * theta)
    groups = lax.axis_size("rep")
    slots = jnp.arange(groups, dtype=jnp.int32)
    facing = 2 * partner[slots // 2] + slots % 2
    sent_flat = delta.astype(jnp.bfloat16).reshape(groups, -1)
    anchor_flat = shard.reshape(groups, -1)
    pieces = (
        lax.all_to_all(sent_flat, "rep", split_axis=0, concat_axis=0, tiled=True),
        lax.all_to_all(anchor_flat, "rep", split_axis=0, concat_axis=0, tiled=True),
    )
    got_delta = lax.all_to_all(pieces[0][facing], "rep", split_axis=0, concat_axis=0, tiled=True)
    got_anchor = lax.all_to_all(pieces[1][facing], "rep", split_axis=0, concat_axis=0, tiled=True)
    partner_delta = got_delta.reshape(shard_rows, outputs).astype(jnp.float32)
    partner_anchor = got_anchor.reshape(shard_rows, outputs).astype(jnp.float32)
    mean_delta = 0.5 * (delta + partner_delta)
    momentum = outer_momentum * outer_mom[0].astype(jnp.float32) + mean_delta
    moved = theta - outer_rate * (mean_delta + outer_momentum * momentum)
    moved = moved - pull_rate * 0.5 * (theta - partner_anchor)
    return (
        moved.astype(jnp.bfloat16)[None],
        first.astype(jnp.bfloat16)[None],
        second.astype(jnp.bfloat16)[None],
        momentum.astype(jnp.bfloat16)[None],
    )


def solution(mesh):
    in_specs = (
        P("rep", "fsdp", None),
        P("rep", "fsdp", None),
        P("rep", "fsdp", None),
        P("rep", "fsdp", None),
        P("rep", "fsdp", None),
        P("rep", "fsdp", None),
        P(),
    )
    out_specs = (
        P("rep", "fsdp", None),
        P("rep", "fsdp", None),
        P("rep", "fsdp", None),
        P("rep", "fsdp", None),
    )
    return jax.shard_map(shards, mesh=mesh, in_specs=in_specs, out_specs=out_specs, check_vma=False)
```

profile of v0, /device:TPU:16, one launch (start us, length us, event | category | flops | bytes accessed | tf_op | source)
XLA Modules:
  0.0 297.0 jit_solution(16303292994599900736)
XLA Ops:
  7.2 0.7 all-gather.6.cloned.1.call-update
  8.0 3.5 %collective-permute-start = (bf16[256,512]{1,0:T(8,128)(2,1)}, bf16[256,512]{1,0:T(8,128)(2,1)S(1)}, u32[]{:S(2)}, u32[]{:S(2)}) collective-permute-start(bf16[256,512]{1,0:T(8,128)(2,1)} %bitcast.75), channel_id=1, source_target_pairs={{0,8},{8,0},{16,24},{24,16},{32,40},{40,32},{48,56},{56,48},{64,72... | collective-permute-start | bytes 786440 | tf_op jit(solution)/shard_map/ppermute | solution.py:17
  11.5 6.7 %collective-permute-done = bf16[256,512]{1,0:T(8,128)(2,1)S(1)} collective-permute-done((bf16[256,512]{1,0:T(8,128)(2,1)}, bf16[256,512]{1,0:T(8,128)(2,1)S(1)}, u32[]{:S(2)}, u32[]{:S(2)}) %collective-permute-start) | collective-permute-done | bytes 262176 | tf_op jit(solution)/shard_map/ppermute | solution.py:17
  18.1 0.7 copy-done.4
  18.8 0.0 reduce-scatter.2.cloned.1.call-start
  18.9 33.9 %all-gather.6.cloned.1.call-done = bf16[1,2048,512]{2,1,0:T(8,128)(2,1)} async-done(((bf16[1,256,512]{2,1,0:T(8,128)(2,1)}), bf16[1,2048,512]{2,1,0:T(8,128)(2,1)}) %all-gather.6.cloned.1.call-update) | async-done | bytes 2097168 | tf_op jit(solution)/shard_map/all_gather | solution.py:40
  52.9 2.3 fusion
  55.2 37.0 %all-gather.4.cloned.1.call-done = bf16[2048,512]{1,0:T(8,128)(2,1)} async-done(((bf16[256,512]{1,0:T(8,128)(2,1)}), bf16[2048,512]{1,0:T(8,128)(2,1)}) %all-gather.4.cloned.1.call-update) | async-done | bytes 2097168 | tf_op jit(solution)/shard_map/all_gather | solution.py:41
  92.1 2.3 fusion.4
  94.5 0.8 convolution_convert_fusion
  95.2 1.9 collective-permute-start.1
  97.2 47.7 %collective-permute-done.1 = bf16[2048,512]{1,0:T(8,128)(2,1)S(1)} collective-permute-done((bf16[2048,512]{1,0:T(8,128)(2,1)S(1)}, bf16[2048,512]{1,0:T(8,128)(2,1)S(1)}, u32[]{:S(2)}, u32[]{:S(2)}) %collective-permute-start.1) | collective-permute-done | bytes 2097184 | tf_op jit(solution)/shard_map/ppermute | solution.py:17
  144.9 2.7 convert_add_fusion
  147.6 0.9 copy-done.2
  148.6 0.2 all_to_all.39
  148.7 0.6 broadcast.171
  149.3 2.2 reduce.6
  151.5 0.9 reshape.150
  152.4 11.2 %all-to-all-start.2 = ((bf16[64,2,1024]{2,1,0:T(2,128)(2,1)}), bf16[64,2,1024]{2,1,0:T(2,128)(2,1)}, u32[]{:S(2)}, u32[]{:S(2)}) async-start(bf16[64,2,1024]{2,1,0:T(2,128)(2,1)} %reshape.150), calls=%async_computation.3 | async-start | bytes 524288 | tf_op jit(solution)/shard_map/all_to_all | solution.py:66
  163.6 45.0 %reduce-scatter.2.cloned.1.call-done = f32[256,512]{1,0:T(8,128)} async-done(((f32[2048,512]{1,0:T(8,128)}), f32[256,512]{1,0:T(8,128)}) %reduce-scatter.2.cloned.1.call-update) | async-done | bytes 524304 | tf_op jit(solution)/shard_map/reduce_scatter | solution.py:53
  208.6 2.3 fusion.33
  210.9 2.0 all_to_all.38
  212.9 3.0 %reduce.4 = bf16[64,2048]{1,0:T(8,128)(2,1)} reduce(bf16[64,1,2048]{2,1,0:T(2,128)(2,1)S(1)} %all_to_all.38, bf16[]{:T(256)} %broadcast.171), dimensions={1}, to_apply=%all_to_all.38.reduce_sub_computation | reduce | bytes 524290 | tf_op jit(solution)/shard_map/all_to_all | solution.py:65
  215.9 1.8 reshape.154
  217.8 11.0 %all-to-all-start = ((bf16[64,2,1024]{2,1,0:T(2,128)(2,1)}), bf16[64,2,1024]{2,1,0:T(2,128)(2,1)}, u32[]{:S(2)}, u32[]{:S(2)}) async-start(bf16[64,2,1024]{2,1,0:T(2,128)(2,1)} %reshape.154), calls=%async_computation.1 | async-start | bytes 524288 | tf_op jit(solution)/shard_map/all_to_all | solution.py:65
  228.9 0.8 gather_fusion
  229.7 2.8 reshape.151
  232.4 1.2 copy.22
  233.6 0.7 gather_fusion.2
  234.4 0.8 reduce.7
  235.2 0.9 reshape.152
  236.1 3.6 %all-to-all-done = bf16[64,2,1024]{2,1,0:T(2,128)(2,1)} async-done(((bf16[64,2,1024]{2,1,0:T(2,128)(2,1)}), bf16[64,2,1024]{2,1,0:T(2,128)(2,1)}, u32[]{:S(2)}, u32[]{:S(2)}) %all-to-all-start) | async-done | bytes 262176 | tf_op jit(solution)/shard_map/all_to_all | solution.py:65
  239.7 8.5 %all-to-all-start.3 = ((bf16[64,2,1024]{2,1,0:T(2,128)(2,1)}), bf16[64,2,1024]{2,1,0:T(2,128)(2,1)}, u32[]{:S(2)}, u32[]{:S(2)}) async-start(bf16[64,2,1024]{2,1,0:T(2,128)(2,1)} %reshape.152), calls=%async_computation.4 | async-start | bytes 524288 | tf_op jit(solution)/shard_map/all_to_all | solution.py:69
  248.2 2.8 reshape.155
  251.0 1.2 copy.23
  252.2 0.7 gather_fusion.1
  252.9 0.8 reduce.5
  253.7 0.9 reshape.156
  254.6 5.1 %all-to-all-done.3 = bf16[64,2,1024]{2,1,0:T(2,128)(2,1)} async-done(((bf16[64,2,1024]{2,1,0:T(2,128)(2,1)}), bf16[64,2,1024]{2,1,0:T(2,128)(2,1)}, u32[]{:S(2)}, u32[]{:S(2)}) %all-to-all-start.3) | async-done | bytes 262176 | tf_op jit(solution)/shard_map/all_to_all | solution.py:69
  259.7 8.0 %all-to-all-start.1 = ((bf16[64,2,1024]{2,1,0:T(2,128)(2,1)}), bf16[64,2,1024]{2,1,0:T(2,128)(2,1)}, u32[]{:S(2)}, u32[]{:S(2)}) async-start(bf16[64,2,1024]{2,1,0:T(2,128)(2,1)} %reshape.156), calls=%async_computation.2 | async-start | bytes 524288 | tf_op jit(solution)/shard_map/all_to_all | solution.py:68
  267.7 2.1 reshape.153
  269.9 2.2 convert_reduce_fusion
  272.1 1.2 reshape.122
  273.3 7.0 %all-to-all-done.1 = bf16[64,2,1024]{2,1,0:T(2,128)(2,1)} async-done(((bf16[64,2,1024]{2,1,0:T(2,128)(2,1)}), bf16[64,2,1024]{2,1,0:T(2,128)(2,1)}, u32[]{:S(2)}, u32[]{:S(2)}) %all-to-all-start.1) | async-done | bytes 262176 | tf_op jit(solution)/shard_map/all_to_all | solution.py:68
  280.3 2.8 reshape.157
  283.1 3.3 %convert_reduce_fusion.1 = f32[64,2048]{1,0:T(8,128)} fusion(bf16[64,1,2048]{2,1,0:T(2,128)(2,1)} %reshape.157), kind=kLoop, calls=%fused_computation.32 | loop fusion | flops 131072 | bytes 786432 | tf_op jit(solution)/shard_map/convert_element_type | solution.py:70
  286.4 2.0 reshape.121
  288.3 2.2 fusion.24
  (19 shorter events, 0.2 us)
Async XLA Ops:
  7.2 45.7 %copy-start = (bf16[1,256,4096]{2,1,0:T(8,128)(2,1)S(1)}, bf16[1,256,4096]{2,1,0:T(8,128)(2,1)}, u32[]{:S(2)}) copy-start(bf16[1,256,4096]{2,1,0:T(8,128)(2,1)} %param.7) | copy-start | bytes 6291460
  7.2 85.0 %copy-start.5 = (bf16[1,256,512]{2,1,0:T(8,128)(2,1)S(1)}, bf16[1,256,512]{2,1,0:T(8,128)(2,1)}, u32[]{:S(2)}) copy-start(bf16[1,256,512]{2,1,0:T(8,128)(2,1)} %param.8) | copy-start | bytes 786436
  7.2 45.7 %all-gather.6.cloned.1.call-start = ((), (), s32[]{:S(2)}) async-start(), calls=%async_computation.7 | async-start | bytes 2359296 | tf_op jit(solution)/shard_map/all_gather | solution.py:40
  7.9 84.2 %all-gather.4.cloned.1.call-start = ((), (), s32[]{:S(2)}) async-start(), calls=%async_computation.5 | async-start | bytes 2359296 | tf_op jit(solution)/shard_map/all_gather | solution.py:41
  8.0 10.2 %collective-permute-start = (bf16[256,512]{1,0:T(8,128)(2,1)}, bf16[256,512]{1,0:T(8,128)(2,1)S(1)}, u32[]{:S(2)}, u32[]{:S(2)}) collective-permute-start(bf16[256,512]{1,0:T(8,128)(2,1)} %bitcast.75), channel_id=1, source_target_pairs={{0,8},{8,0},{16,24},{24,16},{32,40},{40,32},{48,56},{56,48},{64,72... | collective-permute-start | bytes 786440 | tf_op jit(solution)/shard_map/ppermute | solution.py:17
  18.1 0.7 copy-start.4
  18.8 189.7 %reduce-scatter.2.cloned.1.call-start = ((), (), s32[]{:S(2)}) async-start(), calls=%async_computation.6 | async-start | bytes 4718592 | tf_op jit(solution)/shard_map/reduce_scatter | solution.py:53
  95.2 49.7 %collective-permute-start.1 = (bf16[2048,512]{1,0:T(8,128)(2,1)S(1)}, bf16[2048,512]{1,0:T(8,128)(2,1)S(1)}, u32[]{:S(2)}, u32[]{:S(2)}) collective-permute-start(bf16[2048,512]{1,0:T(8,128)(2,1)S(1)} %convolution_convert_fusion), channel_id=1, source_target_pairs={{0,8},{8,0},{16,24},{24,16},{32,40},{40,32},{48,56},{56,48},{64,72... | collective-permute-start | bytes 6291464 | tf_op jit(solution)/shard_map/ppermute | solution.py:17
  147.6 0.9 copy-start.2
  148.6 60.0 %copy-start.3 = (bf16[1,256,512]{2,1,0:T(8,128)(2,1)S(1)}, bf16[1,256,512]{2,1,0:T(8,128)(2,1)}, u32[]{:S(2)}) copy-start(bf16[1,256,512]{2,1,0:T(8,128)(2,1)} %param.11) | copy-start | bytes 786436
  152.4 65.4 %all-to-all-start.2 = ((bf16[64,2,1024]{2,1,0:T(2,128)(2,1)}), bf16[64,2,1024]{2,1,0:T(2,128)(2,1)}, u32[]{:S(2)}, u32[]{:S(2)}) async-start(bf16[64,2,1024]{2,1,0:T(2,128)(2,1)} %reshape.150), calls=%async_computation.3 | async-start | bytes 524288 | tf_op jit(solution)/shard_map/all_to_all | solution.py:66
  163.6 65.3 %copy-start.1 = (s32[32]{0:T(128)S(1)}, s32[32]{0:T(128)}, u32[]{:S(2)}) copy-start(s32[32]{0:T(128)} %param.13) | copy-start | bytes 388
  217.8 21.9 %all-to-all-start = ((bf16[64,2,1024]{2,1,0:T(2,128)(2,1)}), bf16[64,2,1024]{2,1,0:T(2,128)(2,1)}, u32[]{:S(2)}, u32[]{:S(2)}) async-start(bf16[64,2,1024]{2,1,0:T(2,128)(2,1)} %reshape.154), calls=%async_computation.1 | async-start | bytes 524288 | tf_op jit(solution)/shard_map/all_to_all | solution.py:65
  239.7 20.0 %all-to-all-start.3 = ((bf16[64,2,1024]{2,1,0:T(2,128)(2,1)}), bf16[64,2,1024]{2,1,0:T(2,128)(2,1)}, u32[]{:S(2)}, u32[]{:S(2)}) async-start(bf16[64,2,1024]{2,1,0:T(2,128)(2,1)} %reshape.152), calls=%async_computation.4 | async-start | bytes 524288 | tf_op jit(solution)/shard_map/all_to_all | solution.py:69
  259.7 20.6 %all-to-all-start.1 = ((bf16[64,2,1024]{2,1,0:T(2,128)(2,1)}), bf16[64,2,1024]{2,1,0:T(2,128)(2,1)}, u32[]{:S(2)}, u32[]{:S(2)}) async-start(bf16[64,2,1024]{2,1,0:T(2,128)(2,1)} %reshape.156), calls=%async_computation.2 | async-start | bytes 524288 | tf_op jit(solution)/shard_map/all_to_all | solution.py:68
Sparse Core Ops, SparseCore 0:
  10.2 42.6 all-gather.5
  55.6 36.5 all-gather.3
  147.8 60.7 reduce-scatter.1
where the time goes:
time: 298 us; the launch traced here: 297 us
  waiting for transfers between devices  187 us (63%)
  starting transfers between devices  44.3 us (15%)
  local copies, waits for them, and re-layouts  27.2 us (9%)
  other arithmetic  16.9 us (6%)
  between operations  13.9 us (5%)
  matrix products  8.08 us (3%)
    ppermute x2, waiting for transfers between devices, partner_2(): lax.ppermute(value, axis, [(i, i ^ 1 << distance) for i in range(lax.axis...  54.4 us
    reduce_scatter x1, waiting for transfers between devices, shards(): lax.psum_scatter(own_term + incoming, 'fsdp', scatter_dimension=0, tiled=...  45 us
    all_gather x1, waiting for transfers between devices, shards(): lax.all_gather(facing_shard, 'fsdp', axis=0, tiled=True)  37 us
    all_gather x1, waiting for transfers between devices, shards(): lax.all_gather(shard, 'fsdp', axis=0, tiled=True)  33.9 us
    unnamed x22, local copies, waits for them, and re-layouts  19 us
    all_to_all x1, starting transfers between devices, shards(): lax.all_to_all(anchor_flat, 'rep', split_axis=0, concat_axis=0, tiled=True)  11.2 us
    all_to_all x1, starting transfers between devices, shards(): lax.all_to_all(sent_flat, 'rep', split_axis=0, concat_axis=0, tiled=True)  11 us
    all_to_all x1, starting transfers between devices, shards(): lax.all_to_all(pieces[1][facing], 'rep', split_axis=0, concat_axis=0, til...  8.52 us
  transfers between devices with their start and end apart: 9, of which 8 were waited for; matrix products, arithmetic and copies ran while one was open for 11% of the time, Pallas kernels for 0%

commit v1 on v0

v1 whole, which is shorter than its diff:
```python
import functools

import jax
import jax.numpy as jnp
from jax import lax
from jax.experimental import pallas as pl
from jax.experimental.pallas import tpu as pltpu
from jax.sharding import Mesh, PartitionSpec as P

beta_one = 0.9
beta_two = 0.95
epsilon = 1e-08
inner_rate = 0.1
weight_decay = 0.1
outer_rate = 0.7
outer_momentum = 0.9
pull_rate = 0.5

RING = ("hi", "lo")
STRIP = 128


def swap_core(value):
    return lax.ppermute(value, "core", [(0, 1), (1, 0)])


def contract_rows(left, right):
    return lax.dot_general(
        left, right, (((0,), (0,)), ((), ())), preferred_element_type=jnp.float32
    )


def arrange_kernel(n_hi, n_lo, core_ref, own_ref, beside_ref, out_ref):
    rows, features = own_ref.shape
    width = features // (n_hi * n_lo * 2)
    for core in range(2):

        @pl.when(core_ref[0] == core)
        def _():
            for place in range(n_hi * n_lo):
                block = (place % n_lo * n_hi + place // n_lo) * 2 + core
                source = pl.ds(block * width, width)
                target = pl.ds(place * width, width)
                out_ref[:rows, target] = own_ref[:, source]
                out_ref[rows:, target] = beside_ref[:, source]


def arrange(core, own, beside, n_hi, n_lo):
    rows, features = own.shape
    vmem = pl.BlockSpec(memory_space=pltpu.VMEM)
    return pl.pallas_call(
        functools.partial(arrange_kernel, n_hi, n_lo),
        out_shape=jax.ShapeDtypeStruct((2 * rows, features // 2), own.dtype),
        in_specs=[pl.BlockSpec(memory_space=pltpu.SMEM), vmem, vmem],
        out_specs=vmem,
        compiler_params=pltpu.CompilerParams(vmem_limit_bytes=16 * 2**20),
        cost_estimate=pl.CostEstimate(
            flops=0, bytes_accessed=4 * rows * features, transcendentals=0
        ),
        name="arrange",
    )(core.reshape(1).astype(jnp.int32), own, beside)


def scatter_pieces(value):
    columns = lax.axis_size("col")
    pieces = value.reshape(columns, value.shape[0] // columns, value.shape[1])
    return lax.all_to_all(pieces, "col", split_axis=0, concat_axis=0, tiled=True)


def deliver_pieces(pieces, partner):
    turned = pieces.at[partner].get(mode="promise_in_bounds")
    got = lax.all_to_all(turned, "col", split_axis=0, concat_axis=0, tiled=True)
    return got.reshape(got.shape[0] * got.shape[1], got.shape[2])


def gather_strips(shard):
    pieces, strips = shard, []
    for start in range(shard.shape[1] // 2, shard.shape[1], STRIP):
        strip = shard[:, start : start + STRIP]
        if strips:
            strip, pieces, _ = lax.optimization_barrier((strip, pieces, strips[-1]))
        if len(strips) == 1:
            pieces = scatter_pieces(pieces)
        strips.append(lax.all_gather(strip, RING, axis=0, tiled=True))
    return strips, pieces


def sum_direct(term, ring):
    pieces = term.reshape(ring, term.shape[0] // ring, term.shape[1])
    got = lax.all_to_all(pieces, RING, split_axis=0, concat_axis=0, tiled=True)
    return jnp.sum(got.astype(jnp.float32), axis=0)


def shards(tokens, targets, anchor, adam_m, adam_v, outer_mom, partner):
    core = lax.axis_index("core")
    n_hi, n_lo = lax.axis_size("hi"), lax.axis_size("lo")
    ring = n_hi * n_lo
    shard = anchor[0]
    features = tokens.shape[2]
    norm_scale = (2 * ring * tokens.shape[1]) ** (-0.5)
    cut = shard.shape[1] // 2
    left, right = slice(0, cut), slice(cut, None)

    shard_left, own = lax.optimization_barrier((shard[:, left], tokens[0]))
    weight_left = lax.all_gather(shard_left, RING, axis=0, tiled=True)
    beside = swap_core(own)
    goals = jnp.concatenate([targets[0], swap_core(targets[0])], axis=0)
    strips, anchor_pieces = gather_strips(shard)
    inputs = arrange(core, own, beside, n_hi, n_lo)

    def residual_of(part, cols):
        other = swap_core(part.astype(jnp.bfloat16)).astype(jnp.float32)
        rows = part.shape[0] // 2
        keys = part + jnp.concatenate([other[rows:], other[:rows]], axis=0)
        keys = keys * features ** (-0.5)
        return (keys - goals[:, cols].astype(jnp.float32)).astype(jnp.bfloat16)

    part = jnp.concatenate(
        [jnp.dot(inputs, strip, preferred_element_type=jnp.float32) for strip in strips], axis=1
    )
    residual_right = residual_of(part, right)
    term = contract_rows(inputs, residual_right[:, -STRIP:]).astype(jnp.bfloat16)
    tied, anchor_pieces = lax.optimization_barrier((term, anchor_pieces))
    sum_right = sum_direct(tied, ring)

    weight_left, _ = lax.optimization_barrier((weight_left, term))
    part = jnp.dot(inputs, weight_left, preferred_element_type=jnp.float32)
    residual_left = residual_of(part, left)
    residual = jnp.concatenate([residual_left, residual_right[:, :-STRIP]], axis=1)
    term = contract_rows(inputs, residual).astype(jnp.bfloat16)
    sum_left = lax.psum_scatter(term, RING, scatter_dimension=0, tiled=True)

    partner_anchor = deliver_pieces(
        lax.optimization_barrier((anchor_pieces, sum_right))[0], partner
    )
    sum_left, partner_anchor = lax.optimization_barrier((sum_left, partner_anchor))

    grad = jnp.concatenate([sum_left.astype(jnp.float32), sum_right], axis=1) * norm_scale
    theta = shard.astype(jnp.float32)
    first = beta_one * adam_m[0].astype(jnp.float32) + (1.0 - beta_one) * grad
    second = beta_two * adam_v[0].astype(jnp.float32) + (1.0 - beta_two) * grad * grad
    delta = inner_rate * (first / (jnp.sqrt(second) + epsilon) + weight_decay * theta)
    new_m, new_v = first.astype(jnp.bfloat16), second.astype(jnp.bfloat16)
    sent, delta, new_m, new_v = lax.optimization_barrier(
        (delta.astype(jnp.bfloat16), delta, new_m, new_v)
    )
    partner_delta = deliver_pieces(scatter_pieces(sent), partner)
    mean_delta = 0.5 * (delta + partner_delta.astype(jnp.float32))
    momentum = outer_momentum * outer_mom[0].astype(jnp.float32) + mean_delta
    moved = theta - outer_rate * (mean_delta + outer_momentum * momentum)
    moved = moved - pull_rate * 0.5 * (theta - partner_anchor.astype(jnp.float32))
    moved, momentum = moved.astype(jnp.bfloat16), momentum.astype(jnp.bfloat16)
    return moved[None], new_m[None], new_v[None], momentum[None]


def solution(mesh):
    n_rep, n_fsdp = mesh.devices.shape
    ring_mesh = Mesh(
        mesh.devices.reshape(n_rep // 2, 2, n_fsdp // 2, 2), ("col", "lo", "hi", "core")
    )
    rows = P(("col", "lo"), ("hi", "core"), None)
    return jax.shard_map(
        shards,
        mesh=ring_mesh,
        in_specs=(rows,) * 6 + (P(),),
        out_specs=(rows,) * 4,
        check_vma=False,
    )
```

time: 298 us -> 200 us (0.67)
  the two profiles are of different devices: /device:TPU:16 before, /device:TPU:64 now
where the time goes in v1:
time: 200 us
  blocking collectives  127 us (64%)
  waiting for transfers between devices  23.7 us (12%)
  between operations  14.3 us (7%)
  starting transfers between devices  14 us (7%)
  local copies, waits for them, and re-layouts  8.37 us (4%)
  matrix products  7.68 us (4%)
  other arithmetic  4.29 us (2%)
    all_gather x2, blocking collectives, gather_strips(): strips.append(lax.all_gather(strip, RING, axis=0, tiled=True))  53 us
    all_to_all x2, blocking collectives, scatter_pieces(): lax.all_to_all(pieces, 'col', split_axis=0, concat_axis=0, tiled=True)  41.3 us
    all_to_all x2, blocking collectives, deliver_pieces(): got = lax.all_to_all(turned, 'col', split_axis=0, concat_axis=0, tiled=True)  32.7 us
    all_to_all x1, waiting for transfers between devices, sum_direct(): got = lax.all_to_all(pieces, RING, split_axis=0, concat_axis=0, tiled=True)  21.4 us
    ppermute x4, starting transfers between devices, swap_core(): return lax.ppermute(value, 'core', [(0, 1), (1, 0)])  8.5 us
    all_to_all x1, starting transfers between devices, sum_direct(): got = lax.all_to_all(pieces, RING, split_axis=0, concat_axis=0, tiled=True)  5.41 us
    unnamed x21, local copies, waits for them, and re-layouts  4.7 us
    dot_general x2, matrix products, contract_rows(): lax.dot_general(left, right, (((0,), (0,)), ((), ())), preferred_element_...  4.04 us
  transfers between devices with their start and end apart: 7, of which 3 were waited for; matrix products, arithmetic and copies ran while one was open for 3% of the time, Pallas kernels for 0%

profile of v1, /device:TPU:64, one launch (start us, length us, event | category | flops | bytes accessed | tf_op | source)
XLA Modules:
  0.0 199.5 jit_solution(1810148674331807828)
XLA Ops:
  7.2 0.0 all-gather.2.cloned.1.call-start
  7.2 1.6 slice.48
  8.8 1.9 collective-permute-start
  10.7 0.0 all-gather.2.cloned.1.call-update
  10.7 0.0 reduce-scatter.2.cloned.1.call-start
  10.8 0.9 fusion.28
  11.7 27.0 %all_gather.10 = bf16[2048,128]{1,0:T(8,128)(2,1)S(1)} all-gather(bf16[256,128]{1,0:T(8,128)(2,1)S(1)} %get-tuple-element.42), channel_id=1, replica_groups=mesh['col'=32,'lo'=2,'hi'=4,'core'=2] {'hi','lo'}, dimensions={0}, use_global_device_ids=true | all-gather | bytes 589824 | tf_op jit(solution)/shard_map/all_gather | solution.py:84
  38.7 26.0 %all_gather.11 = bf16[2048,128]{1,0:T(8,128)(2,1)S(1)} all-gather(bf16[256,128]{1,0:T(8,128)(2,1)S(1)} %get-tuple-element.20), channel_id=1, replica_groups=mesh['col'=32,'lo'=2,'hi'=4,'core'=2] {'hi','lo'}, dimensions={0}, use_global_device_ids=true | all-gather | bytes 589824 | tf_op jit(solution)/shard_map/all_gather | solution.py:84
  64.7 0.0 collective-permute-done.beside_ref
  64.7 1.3 copy-done.1
  66.0 1.6 copy-done
  67.6 1.6 copy-done.2
  69.2 0.2 arrange.1
  69.4 0.8 fusion.30
  70.3 0.0 copy-start.7
  70.3 0.8 fusion.31
  71.1 0.7 fusion.13
  71.8 1.9 collective-permute-start.1
  73.8 0.1 copy.11
  73.9 2.4 %collective-permute-start.2 = (bf16[256,512]{0,1:T(8,128)(2,1)S(1)}, bf16[256,512]{0,1:T(8,128)(2,1)S(1)}, u32[]{:S(2)}, u32[]{:S(2)}) collective-permute-start(bf16[256,512]{0,1:T(8,128)(2,1)S(1)} %bitcast.60), channel_id=1, source_target_pairs={{0,1},{1,0},{2,3},{3,2},{4,5},{5,4},{6,7},{7,6},{8,9},{9,8},{10,11... | collective-permute-start | bytes 786440 | tf_op jit(solution)/shard_map/ppermute | solution.py:24
  76.3 0.0 collective-permute-done.1
  76.4 1.1 collective-permute-done.2
  77.5 0.1 fusion.7
  77.6 0.0 copy-start.4
  77.6 1.6 convolution_convert_fusion.1
  79.2 2.0 fusion.29
  81.1 2.3 %collective-permute-start.3 = (bf16[512,256]{0,1:T(8,128)(2,1)S(1)}, bf16[512,256]{0,1:T(8,128)(2,1)S(1)}, u32[]{:S(2)}, u32[]{:S(2)}) collective-permute-start(bf16[512,256]{0,1:T(8,128)(2,1)S(1)} %get-tuple-element.44), channel_id=1, source_target_pairs={{0,1},{1,0},{2,3},{3,2},{4,5},{5,4},{6,7},{7,6},{8,9},{9,8},{10,11... | collective-permute-start | bytes 786440 | tf_op jit(solution)/shard_map/ppermute | solution.py:24
  83.4 0.0 slice-start
  83.5 1.1 collective-permute-done.3
  84.6 0.1 fusion.10
  84.8 0.0 copy-start.3
  84.8 2.5 %convolution_convert_fusion = bf16[2048,384]{1,0:T(8,128)(2,1)} fusion(bf16[512,2048]{1,0:T(8,128)(2,1)S(1)} %arrange.1, bf16[512,128]{0,1:T(8,128)(2,1)S(1)} %slice-done, bf16[512,256]{0,1:T(8,128)(2,1)S(1)} %fusion.10), kind=kOutput, calls=%fused_computation.2 | convolution fusion | flops 806879232 | bytes 4063232 | tf_op jit(solution)/shard_map/dot_general | solution.py:28
  87.2 0.0 reduce-scatter.2.cloned.1.call-update
  87.3 0.0 copy-start.5
  87.3 0.0 copy-start.6
  87.3 25.9 %all_to_all.25 = bf16[32,8,512]{2,1,0:T(8,128)(2,1)S(1)} all-to-all(bf16[32,8,512]{2,1,0:T(8,128)(2,1)S(1)} %bitcast.59), channel_id=1, replica_groups=mesh['col'=32,'lo'=2,'hi'=4,'core'=2] {'col'}, dimensions={0} | all-to-all | bytes 524288 | tf_op jit(solution)/shard_map/all_to_all | solution.py:67
  113.2 5.4 %all-to-all-start.1 = ((bf16[8,256,128]{2,1,0:T(8,128)(2,1)}), bf16[8,256,128]{2,1,0:T(8,128)(2,1)S(1)}, u32[]{:S(2)}, u32[]{:S(2)}) async-start(bf16[8,256,128]{2,1,0:T(8,128)(2,1)} %bitcast.6), calls=%async_computation.2 | async-start | bytes 1048576 | tf_op jit(solution)/shard_map/all_to_all | solution.py:90
  118.7 21.4 %all-to-all-done.1 = bf16[8,256,128]{2,1,0:T(8,128)(2,1)S(1)} async-done(((bf16[8,256,128]{2,1,0:T(8,128)(2,1)}), bf16[8,256,128]{2,1,0:T(8,128)(2,1)S(1)}, u32[]{:S(2)}, u32[]{:S(2)}) %all-to-all-start.1) | async-done | bytes 524320 | tf_op jit(solution)/shard_map/all_to_all | solution.py:90
  140.1 0.1 convert_reduce_fusion
  140.1 0.6 gather_fusion
  140.7 17.4 %all_to_all.26 = bf16[32,8,512]{2,1,0:T(8,128)(2,1)S(1)} all-to-all(bf16[32,8,512]{2,1,0:T(8,128)(2,1)S(1)} %gather_fusion), channel_id=1, replica_groups=mesh['col'=32,'lo'=2,'hi'=4,'core'=2] {'col'}, dimensions={0} | all-to-all | bytes 524288 | tf_op jit(solution)/shard_map/all_to_all | solution.py:72
  158.2 1.0 convert_element_type.88
  159.1 0.0 copy-start.8
  159.2 1.2 fusion.24
  160.4 15.4 %all_to_all.27 = bf16[32,8,512]{2,1,0:T(8,128)(2,1)S(1)} all-to-all(bf16[32,8,512]{2,1,0:T(8,128)(2,1)S(1)} %bitcast.63), channel_id=1, replica_groups=mesh['col'=32,'lo'=2,'hi'=4,'core'=2] {'col'}, dimensions={0} | all-to-all | bytes 524288 | tf_op jit(solution)/shard_map/all_to_all | solution.py:67
  175.8 0.6 gather_fusion.1
  176.3 15.3 %all_to_all.28 = bf16[32,8,512]{2,1,0:T(8,128)(2,1)S(1)} all-to-all(bf16[32,8,512]{2,1,0:T(8,128)(2,1)S(1)} %gather_fusion.1), channel_id=1, replica_groups=mesh['col'=32,'lo'=2,'hi'=4,'core'=2] {'col'}, dimensions={0} | all-to-all | bytes 524288 | tf_op jit(solution)/shard_map/all_to_all | solution.py:72
  191.6 1.1 fusion.17
  (18 shorter events, 0.1 us)
Async XLA Ops:
  7.2 72.0 %all-gather.2.cloned.1.call-start = ((), (), s32[]{:S(2)}) async-start(), calls=%async_computation.6 | async-start | bytes 1179648 | tf_op jit(solution)/shard_map/all_gather | solution.py:105
  8.8 55.9 %collective-permute-start = (bf16[256,4096]{1,0:T(8,128)(2,1)}, bf16[256,4096]{1,0:T(8,128)(2,1)S(1)}, u32[]{:S(2)}, u32[]{:S(2)}) collective-permute-start(bf16[256,4096]{1,0:T(8,128)(2,1)} %bitcast.55), channel_id=1, source_target_pairs={{0,1},{1,0},{2,3},{3,2},{4,5},{5,4},{6,7},{7,6},{8,9},{9,8},{10,11... | collective-permute-start | bytes 6291464 | tf_op jit(solution)/shard_map/ppermute | solution.py:24
  10.7 147.4 %reduce-scatter.2.cloned.1.call-start = ((), (), s32[]{:S(2)}) async-start(), calls=%async_computation.7 | async-start | bytes 1769472 | tf_op jit(solution)/shard_map/reduce_scatter | solution.py:131
  64.7 1.3 copy-start.1
  66.0 1.6 copy-start
  67.6 1.6 copy-start.2
  70.3 3.5 %copy-start.7 = (bf16[1,256,512]{2,1,0:T(8,128)(2,1)S(1)}, bf16[1,256,512]{2,1,0:T(8,128)(2,1)}, u32[]{:S(2)}) copy-start(bf16[1,256,512]{2,1,0:T(8,128)(2,1)} %param.8) | copy-start | bytes 786436
  71.8 4.5 %collective-permute-start.1 = (bf16[512,256]{0,1:T(8,128)(2,1)}, bf16[512,256]{0,1:T(8,128)(2,1)S(1)}, u32[]{:S(2)}, u32[]{:S(2)}) collective-permute-start(bf16[512,256]{0,1:T(8,128)(2,1)} %fusion.13), channel_id=1, source_target_pairs={{0,1},{1,0},{2,3},{3,2},{4,5},{5,4},{6,7},{7,6},{8,9},{9,8},{10,11... | collective-permute-start | bytes 786440 | tf_op jit(solution)/shard_map/ppermute | solution.py:24
  73.9 3.6 %collective-permute-start.2 = (bf16[256,512]{0,1:T(8,128)(2,1)S(1)}, bf16[256,512]{0,1:T(8,128)(2,1)S(1)}, u32[]{:S(2)}, u32[]{:S(2)}) collective-permute-start(bf16[256,512]{0,1:T(8,128)(2,1)S(1)} %bitcast.60), channel_id=1, source_target_pairs={{0,1},{1,0},{2,3},{3,2},{4,5},{5,4},{6,7},{7,6},{8,9},{9,8},{10,11... | collective-permute-start | bytes 786440 | tf_op jit(solution)/shard_map/ppermute | solution.py:24
  77.6 5.9 %copy-start.4 = (bf16[512,256]{0,1:T(8,128)(2,1)}, bf16[512,256]{0,1:T(8,128)(2,1)S(1)}, u32[]{:S(2)}) copy-start(bf16[512,256]{0,1:T(8,128)(2,1)S(1)} %fusion.7) | copy-start | bytes 786436
  81.1 3.4 %collective-permute-start.3 = (bf16[512,256]{0,1:T(8,128)(2,1)S(1)}, bf16[512,256]{0,1:T(8,128)(2,1)S(1)}, u32[]{:S(2)}, u32[]{:S(2)}) collective-permute-start(bf16[512,256]{0,1:T(8,128)(2,1)S(1)} %get-tuple-element.44), channel_id=1, source_target_pairs={{0,1},{1,0},{2,3},{3,2},{4,5},{5,4},{6,7},{7,6},{8,9},{9,8},{10,11... | collective-permute-start | bytes 786440 | tf_op jit(solution)/shard_map/ppermute | solution.py:24
  83.4 1.3 slice-start
  84.8 2.5 %copy-start.3 = (bf16[1,256,512]{2,1,0:T(8,128)(2,1)S(1)}, bf16[1,256,512]{2,1,0:T(8,128)(2,1)}, u32[]{:S(2)}) copy-start(bf16[1,256,512]{2,1,0:T(8,128)(2,1)} %param.9) | copy-start | bytes 786436
  87.2 31.4 %copy-start.9 = (s32[32]{0:T(128)S(1)}, s32[32]{0:T(128)}, u32[]{:S(2)}) copy-start(s32[32]{0:T(128)} %param.13) | copy-start | bytes 388
  87.3 71.9 %copy-start.5 = (bf16[1,256,512]{2,1,0:T(8,128)(2,1)S(1)}, bf16[1,256,512]{2,1,0:T(8,128)(2,1)}, u32[]{:S(2)}) copy-start(bf16[1,256,512]{2,1,0:T(8,128)(2,1)} %param.11) | copy-start | bytes 786436
  87.3 71.9 %copy-start.6 = (bf16[1,256,512]{2,1,0:T(8,128)(2,1)S(1)}, bf16[1,256,512]{2,1,0:T(8,128)(2,1)}, u32[]{:S(2)}) copy-start(bf16[1,256,512]{2,1,0:T(8,128)(2,1)} %param.10) | copy-start | bytes 786436
  113.2 26.9 %all-to-all-start.1 = ((bf16[8,256,128]{2,1,0:T(8,128)(2,1)}), bf16[8,256,128]{2,1,0:T(8,128)(2,1)S(1)}, u32[]{:S(2)}, u32[]{:S(2)}) async-start(bf16[8,256,128]{2,1,0:T(8,128)(2,1)} %bitcast.6), calls=%async_computation.2 | async-start | bytes 1048576 | tf_op jit(solution)/shard_map/all_to_all | solution.py:90
  159.1 32.5 %copy-start.8 = (bf16[1,256,512]{2,1,0:T(8,128)(2,1)S(1)}, bf16[1,256,512]{2,1,0:T(8,128)(2,1)}, u32[]{:S(2)}) copy-start(bf16[1,256,512]{2,1,0:T(8,128)(2,1)} %param.12) | copy-start | bytes 786436
Sparse Core Ops, SparseCore 0:
  10.8 45.7 all-gather.1
  87.4 51.9 reduce-scatter.1

commit v2 on v1

v2 whole, which is shorter than its diff:
```python
import functools

import jax
import jax.numpy as jnp
from jax import lax
from jax.experimental import pallas as pl
from jax.experimental.pallas import tpu as pltpu
from jax.sharding import Mesh, PartitionSpec as P

beta_one = 0.9
beta_two = 0.95
epsilon = 1e-08
inner_rate = 0.1
weight_decay = 0.1
outer_rate = 0.7
outer_momentum = 0.9
pull_rate = 0.5

REPLICA = ("lo", "hi", "core")


def swap_core(value):
    return lax.ppermute(value, "core", [(0, 1), (1, 0)])


def hop(value, ring, outward, cross):
    pairs = []
    for y in range(ring):
        for core in range(2):
            end = core ^ 1 if cross else core
            up = end == 0 if outward else core == 1
            to = (y + (1 if up else -1)) % ring
            pairs.append((place_of(y, core, ring), place_of(to, end, ring)))
    return lax.ppermute(value, REPLICA, pairs)


def place_of(y, core, ring):
    return (y % 2 * (ring // 2) + y // 2) * 2 + core


def contract_rows(left, right):
    return lax.dot_general(
        left, right, (((0,), (0,)), ((), ())), preferred_element_type=jnp.float32
    )


def arrange_kernel(width, count, starts_ref, own_ref, beside_ref, out_ref):
    rows = own_ref.shape[0]
    for place in range(count):
        source = pl.ds(pl.multiple_of(starts_ref[place], width), width)
        target = pl.ds(place * width, width)
        out_ref[:rows, target] = own_ref[:, source]
        out_ref[rows:, target] = beside_ref[:, source]


def arrange(own, beside, starts, width):
    rows, count = own.shape[0], starts.shape[0]
    vmem = pl.BlockSpec(memory_space=pltpu.VMEM)
    return pl.pallas_call(
        functools.partial(arrange_kernel, width, count),
        out_shape=jax.ShapeDtypeStruct((2 * rows, count * width), own.dtype),
        in_specs=[pl.BlockSpec(memory_space=pltpu.SMEM), vmem, vmem],
        out_specs=vmem,
        compiler_params=pltpu.CompilerParams(vmem_limit_bytes=8 * 2**20),
        cost_estimate=pl.CostEstimate(
            flops=0, bytes_accessed=8 * rows * count * width, transcendentals=0
        ),
        name="arrange",
    )(starts, own, beside)


def scatter_pieces(value):
    columns = lax.axis_size("col")
    pieces = value.reshape(columns, value.shape[0] // columns, value.shape[1])
    return lax.all_to_all(pieces, "col", split_axis=0, concat_axis=0, tiled=True)


def deliver_pieces(pieces, partner):
    turned = pieces.at[partner].get(mode="promise_in_bounds")
    got = lax.all_to_all(turned, "col", split_axis=0, concat_axis=0, tiled=True)
    return got.reshape(got.shape[0] * got.shape[1], got.shape[2])


def shards(tokens, targets, anchor, adam_m, adam_v, outer_mom, partner):
    core = lax.axis_index("core")
    n_hi, n_lo = lax.axis_size("hi"), lax.axis_size("lo")
    ring = n_hi * n_lo
    half = ring // 2
    chip = 2 * lax.axis_index("hi") + lax.axis_index("lo")
    shard = anchor[0]
    rows = shard.shape[0]
    features = tokens.shape[2]
    norm_scale = (2 * ring * tokens.shape[1]) ** (-0.5)

    beside = swap_core(tokens[0])
    a, b = hop(shard, ring, True, False), hop(shard, ring, True, True)
    blocks, places = [shard, a, b], [(0, 0), (1, 0), (1, 1)]
    for k in range(2, half + 1):
        places += [(k, 0), (k, 1)] if k < half else [(k, 0)]

    away = jnp.array([k for k, _ in places], jnp.int32)
    other = jnp.array([o for _, o in places], jnp.int32)
    source = (chip + jnp.where(core == 0, -away, away)) % ring
    starts = ((source % 2 * half + source // 2) * 2 + (core + other) % 2) * rows
    inputs = arrange(tokens[0], beside, starts.astype(jnp.int32), rows)

    for k in range(2, half + 1):
        if k == half - 1:
            a, inputs, shard_behind = lax.optimization_barrier((a, inputs, shard))
            anchor_pieces = scatter_pieces(shard_behind)
        if k == half:
            a, goals_beside = lax.optimization_barrier((a, goals_beside))
        a = hop(a, ring, True, False)
        blocks.append(a)
        if k < half:
            b = hop(b, ring, True, False)
            blocks.append(b)
        if k == 2:
            a, goals_own = lax.optimization_barrier((a, targets[0]))
            goals_beside = swap_core(goals_own)
    goals = jnp.concatenate([targets[0], goals_beside], axis=0)

    part = None
    for index, block in enumerate(blocks):
        columns = inputs[:, index * rows : (index + 1) * rows]
        term = jnp.dot(columns, block, preferred_element_type=jnp.float32)
        part = term if part is None else part + term
    part, anchor_pieces = lax.optimization_barrier((part, anchor_pieces))
    tokens_dev = part.shape[0] // 2
    swapped = swap_core(part.astype(jnp.bfloat16)).astype(jnp.float32)
    keys = part + jnp.concatenate([swapped[tokens_dev:], swapped[:tokens_dev]], axis=0)
    keys = keys * features ** (-0.5)
    residual = (keys - goals.astype(jnp.float32)).astype(jnp.bfloat16)

    last = (ring - 2) * rows
    far_terms = contract_rows(inputs[:, last:], residual)
    residual, anchor_pieces, _ = lax.optimization_barrier((residual, anchor_pieces, far_terms))
    near_terms = contract_rows(inputs[:, :last], residual)
    partner_anchor = deliver_pieces(anchor_pieces, partner)

    def term_of(k, stream):
        start = places.index((k, stream)) * rows
        terms, start = (far_terms, start - last) if start >= last else (near_terms, start)
        return terms[start : start + rows]

    a = hop(term_of(half, 0).astype(jnp.bfloat16), ring, False, False)
    b = hop(term_of(half - 1, 1).astype(jnp.bfloat16), ring, False, half == 2)
    for k in range(half - 1, 0, -1):
        if k == 1:
            a, partner_anchor = lax.optimization_barrier((a, partner_anchor))
        a = hop((term_of(k, 0) + a.astype(jnp.float32)).astype(jnp.bfloat16), ring, False, False)
        if k > 1:
            b = hop((term_of(k - 1, 1) + b.astype(jnp.float32)).astype(jnp.bfloat16), ring, False, k == 2)
    grad = (term_of(0, 0) + a.astype(jnp.float32) + b.astype(jnp.float32)) * norm_scale

    theta = shard.astype(jnp.float32)
    first = beta_one * adam_m[0].astype(jnp.float32) + (1.0 - beta_one) * grad
    second = beta_two * adam_v[0].astype(jnp.float32) + (1.0 - beta_two) * grad * grad
    delta = inner_rate * (first / (jnp.sqrt(second) + epsilon) + weight_decay * theta)
    new_m, new_v = first.astype(jnp.bfloat16), second.astype(jnp.bfloat16)
    sent, delta, new_m, new_v = lax.optimization_barrier(
        (delta.astype(jnp.bfloat16), delta, new_m, new_v)
    )
    partner_delta = deliver_pieces(scatter_pieces(sent), partner)
    mean_delta = 0.5 * (delta + partner_delta.astype(jnp.float32))
    momentum = outer_momentum * outer_mom[0].astype(jnp.float32) + mean_delta
    moved = theta - outer_rate * (mean_delta + outer_momentum * momentum)
    moved = moved - pull_rate * 0.5 * (theta - partner_anchor.astype(jnp.float32))
    moved, momentum = moved.astype(jnp.bfloat16), momentum.astype(jnp.bfloat16)
    return moved[None], new_m[None], new_v[None], momentum[None]


def solution(mesh):
    n_rep, n_fsdp = mesh.devices.shape
    ring_mesh = Mesh(
        mesh.devices.reshape(n_rep // 2, 2, n_fsdp // 2, 2), ("col", "lo", "hi", "core")
    )
    rows = P(("col", "lo"), ("hi", "core"), None)
    return jax.shard_map(
        shards,
        mesh=ring_mesh,
        in_specs=(rows,) * 6 + (P(),),
        out_specs=(rows,) * 4,
        check_vma=False,
    )
```

time: 200 us -> 172 us (0.86)
  the two profiles are of different devices: /device:TPU:64 before, /device:TPU:16 now
where the time goes in v2:
time: 172 us; the launch traced here: 171 us
  starting transfers between devices  73.3 us (43%)
  blocking collectives  40.1 us (23%)
  waiting for transfers between devices  29 us (17%)
  other arithmetic  10.2 us (6%)
  matrix products  9.65 us (6%)
  local copies, waits for them, and re-layouts  6.58 us (4%)
    ppermute x14, starting transfers between devices, hop(): return lax.ppermute(value, REPLICA, pairs)  44.6 us
    ppermute x14, waiting for transfers between devices, hop(): return lax.ppermute(value, REPLICA, pairs)  22.2 us
    all_to_all x1, blocking collectives, scatter_pieces(): lax.all_to_all(pieces, 'col', split_axis=0, concat_axis=0, tiled=True)  21.4 us
    all_to_all x1, blocking collectives, deliver_pieces(): got = lax.all_to_all(turned, 'col', split_axis=0, concat_axis=0, tiled=True)  18.7 us
    all_to_all x1, starting transfers between devices, scatter_pieces(): lax.all_to_all(pieces, 'col', split_axis=0, concat_axis=0, tiled=True)  13.2 us
    all_to_all x1, starting transfers between devices, deliver_pieces(): got = lax.all_to_all(turned, 'col', split_axis=0, concat_axis=0, tiled=True)  9.78 us
    dot_general x8, matrix products, shards(): term = jnp.dot(columns, block, preferred_element_type=jnp.float32)  8.13 us
    ppermute x3, starting transfers between devices, swap_core(): return lax.ppermute(value, 'core', [(0, 1), (1, 0)])  5.76 us
  transfers between devices with their start and end apart: 19, of which 10 were waited for; matrix products, arithmetic and copies ran while one was open for 8% of the time, Pallas kernels for 0%

profile of v2, /device:TPU:16, one launch (start us, length us, event | category | flops | bytes accessed | tf_op | source)
XLA Modules:
  0.0 170.7 jit_solution(13655327160947908137)
XLA Ops:
  0.6 1.9 %collective-permute-start.2 = (bf16[256,4096]{1,0:T(8,128)(2,1)}, bf16[256,4096]{1,0:T(8,128)(2,1)S(1)}, u32[]{:S(2)}, u32[]{:S(2)}) collective-permute-start(bf16[256,4096]{1,0:T(8,128)(2,1)} %bitcast.56), channel_id=1, source_target_pairs={{0,1},{1,0},{2,3},{3,2},{4,5},{5,4},{6,7},{7,6},{8,9},{9,8},{10,11... | collective-permute-start | bytes 6291464 | tf_op jit(solution)/shard_map/ppermute | solution.py:23
  2.6 3.5 %collective-permute-start = (bf16[256,512]{1,0:T(8,128)(2,1)}, bf16[256,512]{1,0:T(8,128)(2,1)S(1)}, u32[]{:S(2)}, u32[]{:S(2)}) collective-permute-start(bf16[256,512]{1,0:T(8,128)(2,1)} %bitcast), channel_id=1, source_target_pairs={{0,8},{1,15},{8,2},{9,1},{2,10},{3,9},{10,4},{11,3},{4,12},{5,11},... | collective-permute-start | bytes 786440 | tf_op jit(solution)/shard_map/ppermute | solution.py:34
  6.1 6.4 %collective-permute-start.3 = (bf16[256,512]{1,0:T(8,128)(2,1)}, bf16[256,512]{1,0:T(8,128)(2,1)S(1)}, u32[]{:S(2)}, u32[]{:S(2)}) collective-permute-start(bf16[256,512]{1,0:T(8,128)(2,1)} %bitcast), channel_id=1, source_target_pairs={{0,15},{1,8},{8,1},{9,2},{2,9},{3,10},{10,3},{11,4},{4,11},{5,12},... | collective-permute-start | bytes 786440 | tf_op jit(solution)/shard_map/ppermute | solution.py:34
  12.5 3.1 %collective-permute-start.1 = (bf16[256,512]{1,0:T(8,128)(2,1)S(1)}, bf16[256,512]{1,0:T(8,128)(2,1)}, u32[]{:S(2)}, u32[]{:S(2)}) collective-permute-start(bf16[256,512]{1,0:T(8,128)(2,1)S(1)} %collective-permute-done), channel_id=1, source_target_pairs={{0,8},{1,15},{8,2},{9,1},{2,10},{3,9},{10,4},{11,3},{4,12},{5,11},... | collective-permute-start | bytes 786440 | tf_op jit(solution)/shard_map/ppermute | solution.py:34
  15.7 1.1 collective-permute-done.3
  16.7 4.4 %collective-permute-start.4 = (bf16[256,512]{1,0:T(8,128)(2,1)S(1)}, bf16[256,512]{1,0:T(8,128)(2,1)}, u32[]{:S(2)}, u32[]{:S(2)}) collective-permute-start(bf16[256,512]{1,0:T(8,128)(2,1)S(1)} %collective-permute-done.3), channel_id=1, source_target_pairs={{0,8},{1,15},{8,2},{9,1},{2,10},{3,9},{10,4},{11,3},{4,12},{5,11},... | collective-permute-start | bytes 786440 | tf_op jit(solution)/shard_map/ppermute | solution.py:34
  21.9 0.8 collective-permute-done.1
  22.7 1.9 %collective-permute-start.7 = (bf16[256,512]{1,0:T(8,128)(2,1)}, bf16[256,512]{1,0:T(8,128)(2,1)}, u32[]{:S(2)}, u32[]{:S(2)}) collective-permute-start(bf16[256,512]{1,0:T(8,128)(2,1)} %bitcast.60), channel_id=1, source_target_pairs={{0,1},{1,0},{2,3},{3,2},{4,5},{5,4},{6,7},{7,6},{8,9},{9,8},{10,11... | collective-permute-start | bytes 786440 | tf_op jit(solution)/shard_map/ppermute | solution.py:23
  24.6 0.9 collective-permute-done.4
  25.5 4.1 %collective-permute-start.6 = (bf16[256,512]{1,0:T(8,128)(2,1)}, bf16[256,512]{1,0:T(8,128)(2,1)}, u32[]{:S(2)}, u32[]{:S(2)}) collective-permute-start(bf16[256,512]{1,0:T(8,128)(2,1)} %collective-permute-done.4), channel_id=1, source_target_pairs={{0,8},{1,15},{8,2},{9,1},{2,10},{3,9},{10,4},{11,3},{4,12},{5,11},... | collective-permute-start | bytes 786440 | tf_op jit(solution)/shard_map/ppermute | solution.py:34
  29.6 1.3 copy-done.1
  30.9 1.6 copy-done
  32.5 1.6 copy-done.2
  34.1 0.8 arrange.1
  34.9 1.2 fusion.36
  36.2 4.0 %collective-permute-start.5 = (bf16[256,512]{1,0:T(8,128)(2,1)}, bf16[256,512]{1,0:T(8,128)(2,1)}, u32[]{:S(2)}, u32[]{:S(2)}) collective-permute-start(bf16[256,512]{1,0:T(8,128)(2,1)} %collective-permute-done.1), channel_id=1, source_target_pairs={{0,8},{1,15},{8,2},{9,1},{2,10},{3,9},{10,4},{11,3},{4,12},{5,11},... | collective-permute-start | bytes 786440 | tf_op jit(solution)/shard_map/ppermute | solution.py:34
  40.2 13.2 %all-to-all-start = ((bf16[32,8,512]{2,1,0:T(8,128)(2,1)}), bf16[32,8,512]{2,1,0:T(8,128)(2,1)S(1)}, u32[]{:S(2)}, u32[]{:S(2)}) async-start(bf16[32,8,512]{2,1,0:T(8,128)(2,1)} %bitcast.4), calls=%async_computation | async-start | bytes 524288 | tf_op jit(solution)/shard_map/all_to_all | solution.py:75
  53.4 1.3 convolution_add_fusion.3
  55.0 1.2 fusion.31
  56.3 1.9 %collective-permute-start.8 = (bf16[256,512]{1,0:T(8,128)(2,1)}, bf16[256,512]{1,0:T(8,128)(2,1)S(1)}, u32[]{:S(2)}, u32[]{:S(2)}) collective-permute-start(bf16[256,512]{1,0:T(8,128)(2,1)} %collective-permute-done.5), channel_id=1, source_target_pairs={{0,8},{1,15},{8,2},{9,1},{2,10},{3,9},{10,4},{11,3},{4,12},{5,11},... | collective-permute-start | bytes 786440 | tf_op jit(solution)/shard_map/ppermute | solution.py:34
  58.2 1.3 fusion.29
  59.5 1.2 fusion.4
  60.7 4.0 %collective-permute-done.8 = bf16[256,512]{1,0:T(8,128)(2,1)S(1)} collective-permute-done((bf16[256,512]{1,0:T(8,128)(2,1)}, bf16[256,512]{1,0:T(8,128)(2,1)S(1)}, u32[]{:S(2)}, u32[]{:S(2)}) %collective-permute-start.8) | collective-permute-done | bytes 262176 | tf_op jit(solution)/shard_map/ppermute | solution.py:34
  65.0 1.2 fusion.2
  66.4 1.9 %collective-permute-start.9 = (bf16[512,512]{1,0:T(8,128)(2,1)S(1)}, bf16[512,512]{1,0:T(8,128)(2,1)S(1)}, u32[]{:S(2)}, u32[]{:S(2)}) collective-permute-start(bf16[512,512]{1,0:T(8,128)(2,1)S(1)} %convert_element_type.91), channel_id=1, source_target_pairs={{0,1},{1,0},{2,3},{3,2},{4,5},{5,4},{6,7},{7,6},{8,9},{9,8},{10,11... | collective-permute-start | bytes 1572872 | tf_op jit(solution)/shard_map/ppermute | solution.py:23
  68.3 1.9 %collective-permute-done.9 = bf16[512,512]{1,0:T(8,128)(2,1)S(1)} collective-permute-done((bf16[512,512]{1,0:T(8,128)(2,1)S(1)}, bf16[512,512]{1,0:T(8,128)(2,1)S(1)}, u32[]{:S(2)}, u32[]{:S(2)}) %collective-permute-start.9) | collective-permute-done | bytes 524320 | tf_op jit(solution)/shard_map/ppermute | solution.py:23
  70.3 1.3 fusion.7
  72.2 1.9 %collective-permute-start.10 = (bf16[256,512]{1,0:T(8,128)(2,1)S(1)}, bf16[256,512]{1,0:T(8,128)(2,1)S(1)}, u32[]{:S(2)}, u32[]{:S(2)}) collective-permute-start(bf16[256,512]{1,0:T(8,128)(2,1)S(1)} %get-tuple-element.47), channel_id=1, source_target_pairs={{0,14},{1,9},{8,0},{9,3},{2,8},{3,11},{10,2},{11,5},{4,10},{5,13},... | collective-permute-start | bytes 786440 | tf_op jit(solution)/shard_map/ppermute | solution.py:34
  74.1 1.0 fusion
  75.2 5.3 %collective-permute-done.10 = bf16[256,512]{1,0:T(8,128)(2,1)S(1)} collective-permute-done((bf16[256,512]{1,0:T(8,128)(2,1)S(1)}, bf16[256,512]{1,0:T(8,128)(2,1)S(1)}, u32[]{:S(2)}, u32[]{:S(2)}) %collective-permute-start.10) | collective-permute-done | bytes 262176 | tf_op jit(solution)/shard_map/ppermute | solution.py:34
  80.5 1.9 %collective-permute-start.11 = (bf16[256,512]{1,0:T(8,128)(2,1)S(1)}, bf16[256,512]{1,0:T(8,128)(2,1)S(1)}, u32[]{:S(2)}, u32[]{:S(2)}) collective-permute-start(bf16[256,512]{1,0:T(8,128)(2,1)S(1)} %fusion.15), channel_id=1, source_target_pairs={{0,14},{1,9},{8,0},{9,3},{2,8},{3,11},{10,2},{11,5},{4,10},{5,13},... | collective-permute-start | bytes 786440 | tf_op jit(solution)/shard_map/ppermute | solution.py:34
  82.5 1.3 gather_fusion
  83.8 9.8 %all-to-all-start.1 = ((bf16[32,8,512]{2,1,0:T(8,128)(2,1)}), bf16[32,8,512]{2,1,0:T(8,128)(2,1)S(1)}, u32[]{:S(2)}, u32[]{:S(2)}) async-start(bf16[32,8,512]{2,1,0:T(8,128)(2,1)} %gather_fusion), calls=%async_computation.1 | async-start | bytes 524288 | tf_op jit(solution)/shard_map/all_to_all | solution.py:80
  93.6 1.2 fusion.16
  94.8 2.5 %collective-permute-start.12 = (bf16[256,512]{1,0:T(8,128)(2,1)S(1)}, bf16[256,512]{1,0:T(8,128)(2,1)S(1)}, u32[]{:S(2)}, u32[]{:S(2)}) collective-permute-start(bf16[256,512]{1,0:T(8,128)(2,1)S(1)} %fusion.16), channel_id=1, source_target_pairs={{0,14},{1,9},{8,0},{9,3},{2,8},{3,11},{10,2},{11,5},{4,10},{5,13},... | collective-permute-start | bytes 786440 | tf_op jit(solution)/shard_map/ppermute | solution.py:34
  97.2 3.1 %collective-permute-start.14 = (bf16[256,512]{1,0:T(8,128)(2,1)S(1)}, bf16[256,512]{1,0:T(8,128)(2,1)S(1)}, u32[]{:S(2)}, u32[]{:S(2)}) collective-permute-start(bf16[256,512]{1,0:T(8,128)(2,1)S(1)} %get-tuple-element.46), channel_id=1, source_target_pairs={{0,14},{1,9},{8,0},{9,3},{2,8},{3,11},{10,2},{11,5},{4,10},{5,13},... | collective-permute-start | bytes 786440 | tf_op jit(solution)/shard_map/ppermute | solution.py:34
  100.4 5.0 %all-to-all-done.1 = bf16[32,8,512]{2,1,0:T(8,128)(2,1)S(1)} async-done(((bf16[32,8,512]{2,1,0:T(8,128)(2,1)}), bf16[32,8,512]{2,1,0:T(8,128)(2,1)S(1)}, u32[]{:S(2)}, u32[]{:S(2)}) %all-to-all-start.1) | async-done | bytes 262176 | tf_op jit(solution)/shard_map/all_to_all | solution.py:80
  105.8 1.4 fusion.17
  107.2 2.8 %collective-permute-start.15 = (bf16[256,512]{1,0:T(8,128)(2,1)S(1)}, bf16[256,512]{1,0:T(8,128)(2,1)S(1)}, u32[]{:S(2)}, u32[]{:S(2)}) collective-permute-start(bf16[256,512]{1,0:T(8,128)(2,1)S(1)} %get-tuple-element.43), channel_id=1, source_target_pairs={{0,14},{1,9},{8,0},{9,3},{2,8},{3,11},{10,2},{11,5},{4,10},{5,13},... | collective-permute-start | bytes 786440 | tf_op jit(solution)/shard_map/ppermute | solution.py:34
  110.0 2.8 %collective-permute-start.13 = (bf16[256,512]{1,0:T(8,128)(2,1)S(1)}, bf16[256,512]{1,0:T(8,128)(2,1)S(1)}, u32[]{:S(2)}, u32[]{:S(2)}) collective-permute-start(bf16[256,512]{1,0:T(8,128)(2,1)S(1)} %get-tuple-element.42), channel_id=1, source_target_pairs={{0,14},{1,9},{8,0},{9,3},{2,8},{3,11},{10,2},{11,5},{4,10},{5,13},... | collective-permute-start | bytes 786440 | tf_op jit(solution)/shard_map/ppermute | solution.py:34
  112.8 3.9 %collective-permute-done.15 = bf16[256,512]{1,0:T(8,128)(2,1)S(1)} collective-permute-done((bf16[256,512]{1,0:T(8,128)(2,1)S(1)}, bf16[256,512]{1,0:T(8,128)(2,1)S(1)}, u32[]{:S(2)}, u32[]{:S(2)}) %collective-permute-start.15) | collective-permute-done | bytes 262176 | tf_op jit(solution)/shard_map/ppermute | solution.py:34
  116.7 1.1 fusion.14
  117.8 2.1 %collective-permute-start.16 = (bf16[256,512]{1,0:T(8,128)(2,1)S(1)}, bf16[256,512]{1,0:T(8,128)(2,1)S(1)}, u32[]{:S(2)}, u32[]{:S(2)}) collective-permute-start(bf16[256,512]{1,0:T(8,128)(2,1)S(1)} %fusion.14), channel_id=1, source_target_pairs={{0,15},{1,8},{8,1},{9,2},{2,9},{3,10},{10,3},{11,4},{4,11},{5,12},... | collective-permute-start | bytes 786440 | tf_op jit(solution)/shard_map/ppermute | solution.py:34
  119.9 5.8 %collective-permute-done.16 = bf16[256,512]{1,0:T(8,128)(2,1)S(1)} collective-permute-done((bf16[256,512]{1,0:T(8,128)(2,1)S(1)}, bf16[256,512]{1,0:T(8,128)(2,1)S(1)}, u32[]{:S(2)}, u32[]{:S(2)}) %collective-permute-start.16) | collective-permute-done | bytes 262176 | tf_op jit(solution)/shard_map/ppermute | solution.py:34
  125.6 2.4 %fusion.47 = (bf16[256,512]{1,0:T(8,128)(2,1)S(1)}, f32[256,512]{1,0:T(8,128)S(1)}, bf16[256,512]{1,0:T(8,128)(2,1)}, bf16[256,512]{1,0:T(8,128)(2,1)}) fusion(bf16[1,256,512]{2,1,0:T(8,128)(2,1)} %param.11, bf16[1,256,512]{2,1,0:T(8,128)(2,1)S(1)} %copy-done.5, bf16[256,512]{1,0:T(8,128)(2,1)S(1)} %collective-permute-done.16, ...), kind=kLoop, calls=%fused_computation.81 | loop fusion | flops 3014656 | bytes 3145728 | tf_op jit(solution)/shard_map/convert_element_type | solution.py:162
  128.0 21.4 %all_to_all.20 = bf16[32,8,512]{2,1,0:T(8,128)(2,1)S(1)} all-to-all(bf16[32,8,512]{2,1,0:T(8,128)(2,1)S(1)} %bitcast.58), channel_id=1, replica_groups=mesh['col'=32,'lo'=2,'hi'=4,'core'=2] {'col'}, dimensions={0} | all-to-all | bytes 524288 | tf_op jit(solution)/shard_map/all_to_all | solution.py:75
  150.0 18.7 %all_to_all.21 = bf16[32,8,512]{2,1,0:T(8,128)(2,1)S(1)} all-to-all(bf16[32,8,512]{2,1,0:T(8,128)(2,1)S(1)} %gather_fusion.1), channel_id=1, replica_groups=mesh['col'=32,'lo'=2,'hi'=4,'core'=2] {'col'}, dimensions={0} | all-to-all | bytes 524288 | tf_op jit(solution)/shard_map/all_to_all | solution.py:80
  168.7 2.0 %fusion.24 = (bf16[1,256,512]{2,1,0:T(8,128)(2,1)}, bf16[1,256,512]{2,1,0:T(8,128)(2,1)}) fusion(f32[256,512]{1,0:T(8,128)S(1)} %get-tuple-element.33, bf16[1,256,512]{2,1,0:T(8,128)(2,1)S(1)} %copy-done.10, bf16[32,8,512]{2,1,0:T(8,128)(2,1)S(1)} %all_to_all.21, bf16[256,512]{1,0:T(8,128)(2,1)S(1)} %bitcast.59, bf16[1,256,512]{2,1,0:T(8,128)(2,1)} %param.11), kind=kLoop, calls=%fused_computation.44 | loop fusion | flops 2228224 | bytes 2097152 | tf_op jit(solution)/shard_map/broadcast_in_dim | solution.py:170
  (42 shorter events, 3.2 us)
Async XLA Ops:
  0.6 28.9 %collective-permute-start.2 = (bf16[256,4096]{1,0:T(8,128)(2,1)}, bf16[256,4096]{1,0:T(8,128)(2,1)S(1)}, u32[]{:S(2)}, u32[]{:S(2)}) collective-permute-start(bf16[256,4096]{1,0:T(8,128)(2,1)} %bitcast.56), channel_id=1, source_target_pairs={{0,1},{1,0},{2,3},{3,2},{4,5},{5,4},{6,7},{7,6},{8,9},{9,8},{10,11... | collective-permute-start | bytes 6291464 | tf_op jit(solution)/shard_map/ppermute | solution.py:23
  2.6 9.9 %collective-permute-start = (bf16[256,512]{1,0:T(8,128)(2,1)}, bf16[256,512]{1,0:T(8,128)(2,1)S(1)}, u32[]{:S(2)}, u32[]{:S(2)}) collective-permute-start(bf16[256,512]{1,0:T(8,128)(2,1)} %bitcast), channel_id=1, source_target_pairs={{0,8},{1,15},{8,2},{9,1},{2,10},{3,9},{10,4},{11,3},{4,12},{5,11},... | collective-permute-start | bytes 786440 | tf_op jit(solution)/shard_map/ppermute | solution.py:34
  6.1 10.7 %collective-permute-start.3 = (bf16[256,512]{1,0:T(8,128)(2,1)}, bf16[256,512]{1,0:T(8,128)(2,1)S(1)}, u32[]{:S(2)}, u32[]{:S(2)}) collective-permute-start(bf16[256,512]{1,0:T(8,128)(2,1)} %bitcast), channel_id=1, source_target_pairs={{0,15},{1,8},{8,1},{9,2},{2,9},{3,10},{10,3},{11,4},{4,11},{5,12},... | collective-permute-start | bytes 786440 | tf_op jit(solution)/shard_map/ppermute | solution.py:34
  12.5 27.7 %copy-start.7 = (bf16[256,512]{1,0:T(8,128)(2,1)}, bf16[256,512]{1,0:T(8,128)(2,1)S(1)}, u32[]{:S(2)}) copy-start(bf16[256,512]{1,0:T(8,128)(2,1)S(1)} %collective-permute-done) | copy-start | bytes 786436
  12.5 10.1 %collective-permute-start.1 = (bf16[256,512]{1,0:T(8,128)(2,1)S(1)}, bf16[256,512]{1,0:T(8,128)(2,1)}, u32[]{:S(2)}, u32[]{:S(2)}) collective-permute-start(bf16[256,512]{1,0:T(8,128)(2,1)S(1)} %collective-permute-done), channel_id=1, source_target_pairs={{0,8},{1,15},{8,2},{9,1},{2,10},{3,9},{10,4},{11,3},{4,12},{5,11},... | collective-permute-start | bytes 786440 | tf_op jit(solution)/shard_map/ppermute | solution.py:34
  16.7 12.8 %copy-start.8 = (bf16[256,512]{1,0:T(8,128)(2,1)}, bf16[256,512]{1,0:T(8,128)(2,1)S(1)}, u32[]{:S(2)}) copy-start(bf16[256,512]{1,0:T(8,128)(2,1)S(1)} %collective-permute-done.3) | copy-start | bytes 786436
  16.7 8.7 %collective-permute-start.4 = (bf16[256,512]{1,0:T(8,128)(2,1)S(1)}, bf16[256,512]{1,0:T(8,128)(2,1)}, u32[]{:S(2)}, u32[]{:S(2)}) collective-permute-start(bf16[256,512]{1,0:T(8,128)(2,1)S(1)} %collective-permute-done.3), channel_id=1, source_target_pairs={{0,8},{1,15},{8,2},{9,1},{2,10},{3,9},{10,4},{11,3},{4,12},{5,11},... | collective-permute-start | bytes 786440 | tf_op jit(solution)/shard_map/ppermute | solution.py:34
  22.7 33.6 %collective-permute-start.7 = (bf16[256,512]{1,0:T(8,128)(2,1)}, bf16[256,512]{1,0:T(8,128)(2,1)}, u32[]{:S(2)}, u32[]{:S(2)}) collective-permute-start(bf16[256,512]{1,0:T(8,128)(2,1)} %bitcast.60), channel_id=1, source_target_pairs={{0,1},{1,0},{2,3},{3,2},{4,5},{5,4},{6,7},{7,6},{8,9},{9,8},{10,11... | collective-permute-start | bytes 786440 | tf_op jit(solution)/shard_map/ppermute | solution.py:23
  25.5 39.6 %collective-permute-start.6 = (bf16[256,512]{1,0:T(8,128)(2,1)}, bf16[256,512]{1,0:T(8,128)(2,1)}, u32[]{:S(2)}, u32[]{:S(2)}) collective-permute-start(bf16[256,512]{1,0:T(8,128)(2,1)} %collective-permute-done.4), channel_id=1, source_target_pairs={{0,8},{1,15},{8,2},{9,1},{2,10},{3,9},{10,4},{11,3},{4,12},{5,11},... | collective-permute-start | bytes 786440 | tf_op jit(solution)/shard_map/ppermute | solution.py:34
  29.6 1.4 copy-start.1
  30.9 1.6 copy-start
  32.5 1.6 copy-start.2
  36.2 20.1 %collective-permute-start.5 = (bf16[256,512]{1,0:T(8,128)(2,1)}, bf16[256,512]{1,0:T(8,128)(2,1)}, u32[]{:S(2)}, u32[]{:S(2)}) collective-permute-start(bf16[256,512]{1,0:T(8,128)(2,1)} %collective-permute-done.1), channel_id=1, source_target_pairs={{0,8},{1,15},{8,2},{9,1},{2,10},{3,9},{10,4},{11,3},{4,12},{5,11},... | collective-permute-start | bytes 786440 | tf_op jit(solution)/shard_map/ppermute | solution.py:34
  40.2 26.1 %all-to-all-start = ((bf16[32,8,512]{2,1,0:T(8,128)(2,1)}), bf16[32,8,512]{2,1,0:T(8,128)(2,1)S(1)}, u32[]{:S(2)}, u32[]{:S(2)}) async-start(bf16[32,8,512]{2,1,0:T(8,128)(2,1)} %bitcast.4), calls=%async_computation | async-start | bytes 524288 | tf_op jit(solution)/shard_map/all_to_all | solution.py:75
  53.4 1.3 copy-start.9
  56.3 8.5 %collective-permute-start.8 = (bf16[256,512]{1,0:T(8,128)(2,1)}, bf16[256,512]{1,0:T(8,128)(2,1)S(1)}, u32[]{:S(2)}, u32[]{:S(2)}) collective-permute-start(bf16[256,512]{1,0:T(8,128)(2,1)} %collective-permute-done.5), channel_id=1, source_target_pairs={{0,8},{1,15},{8,2},{9,1},{2,10},{3,9},{10,4},{11,3},{4,12},{5,11},... | collective-permute-start | bytes 786440 | tf_op jit(solution)/shard_map/ppermute | solution.py:34
  66.3 4.0 %copy-start.4 = (bf16[1,256,512]{2,1,0:T(8,128)(2,1)S(1)}, bf16[1,256,512]{2,1,0:T(8,128)(2,1)}, u32[]{:S(2)}) copy-start(bf16[1,256,512]{2,1,0:T(8,128)(2,1)} %param.10) | copy-start | bytes 786436
  66.4 3.8 %collective-permute-start.9 = (bf16[512,512]{1,0:T(8,128)(2,1)S(1)}, bf16[512,512]{1,0:T(8,128)(2,1)S(1)}, u32[]{:S(2)}, u32[]{:S(2)}) collective-permute-start(bf16[512,512]{1,0:T(8,128)(2,1)S(1)} %convert_element_type.91), channel_id=1, source_target_pairs={{0,1},{1,0},{2,3},{3,2},{4,5},{5,4},{6,7},{7,6},{8,9},{9,8},{10,11... | collective-permute-start | bytes 1572872 | tf_op jit(solution)/shard_map/ppermute | solution.py:23
  72.2 10.3 %copy-start.11 = (s32[32]{0:T(128)S(1)}, s32[32]{0:T(128)}, u32[]{:S(2)}) copy-start(s32[32]{0:T(128)} %param.15) | copy-start | bytes 388
  72.2 8.3 %collective-permute-start.10 = (bf16[256,512]{1,0:T(8,128)(2,1)S(1)}, bf16[256,512]{1,0:T(8,128)(2,1)S(1)}, u32[]{:S(2)}, u32[]{:S(2)}) collective-permute-start(bf16[256,512]{1,0:T(8,128)(2,1)S(1)} %get-tuple-element.47), channel_id=1, source_target_pairs={{0,14},{1,9},{8,0},{9,3},{2,8},{3,11},{10,2},{11,5},{4,10},{5,13},... | collective-permute-start | bytes 786440 | tf_op jit(solution)/shard_map/ppermute | solution.py:34
  75.1 5.3 %copy-start.3 = (f32[1536,512]{1,0:T(8,128)}, f32[1536,512]{1,0:T(8,128)S(1)}, u32[]{:S(2)}) copy-start(f32[1536,512]{1,0:T(8,128)S(1)} %fusion) | copy-start | bytes 9437188
  80.5 13.1 %collective-permute-start.11 = (bf16[256,512]{1,0:T(8,128)(2,1)S(1)}, bf16[256,512]{1,0:T(8,128)(2,1)S(1)}, u32[]{:S(2)}, u32[]{:S(2)}) collective-permute-start(bf16[256,512]{1,0:T(8,128)(2,1)S(1)} %fusion.15), channel_id=1, source_target_pairs={{0,14},{1,9},{8,0},{9,3},{2,8},{3,11},{10,2},{11,5},{4,10},{5,13},... | collective-permute-start | bytes 786440 | tf_op jit(solution)/shard_map/ppermute | solution.py:34
  83.8 21.6 %all-to-all-start.1 = ((bf16[32,8,512]{2,1,0:T(8,128)(2,1)}), bf16[32,8,512]{2,1,0:T(8,128)(2,1)S(1)}, u32[]{:S(2)}, u32[]{:S(2)}) async-start(bf16[32,8,512]{2,1,0:T(8,128)(2,1)} %gather_fusion), calls=%async_computation.1 | async-start | bytes 524288 | tf_op jit(solution)/shard_map/all_to_all | solution.py:80
  93.6 32.1 %copy-start.5 = (bf16[1,256,512]{2,1,0:T(8,128)(2,1)S(1)}, bf16[1,256,512]{2,1,0:T(8,128)(2,1)}, u32[]{:S(2)}) copy-start(bf16[1,256,512]{2,1,0:T(8,128)(2,1)} %param.13) | copy-start | bytes 786436
  93.6 32.1 %copy-start.6 = (bf16[1,256,512]{2,1,0:T(8,128)(2,1)S(1)}, bf16[1,256,512]{2,1,0:T(8,128)(2,1)}, u32[]{:S(2)}) copy-start(bf16[1,256,512]{2,1,0:T(8,128)(2,1)} %param.12) | copy-start | bytes 786436
  94.8 10.6 %collective-permute-start.12 = (bf16[256,512]{1,0:T(8,128)(2,1)S(1)}, bf16[256,512]{1,0:T(8,128)(2,1)S(1)}, u32[]{:S(2)}, u32[]{:S(2)}) collective-permute-start(bf16[256,512]{1,0:T(8,128)(2,1)S(1)} %fusion.16), channel_id=1, source_target_pairs={{0,14},{1,9},{8,0},{9,3},{2,8},{3,11},{10,2},{11,5},{4,10},{5,13},... | collective-permute-start | bytes 786440 | tf_op jit(solution)/shard_map/ppermute | solution.py:34
  97.2 8.6 %collective-permute-start.14 = (bf16[256,512]{1,0:T(8,128)(2,1)S(1)}, bf16[256,512]{1,0:T(8,128)(2,1)S(1)}, u32[]{:S(2)}, u32[]{:S(2)}) collective-permute-start(bf16[256,512]{1,0:T(8,128)(2,1)S(1)} %get-tuple-element.46), channel_id=1, source_target_pairs={{0,14},{1,9},{8,0},{9,3},{2,8},{3,11},{10,2},{11,5},{4,10},{5,13},... | collective-permute-start | bytes 786440 | tf_op jit(solution)/shard_map/ppermute | solution.py:34
  107.2 9.5 %collective-permute-start.15 = (bf16[256,512]{1,0:T(8,128)(2,1)S(1)}, bf16[256,512]{1,0:T(8,128)(2,1)S(1)}, u32[]{:S(2)}, u32[]{:S(2)}) collective-permute-start(bf16[256,512]{1,0:T(8,128)(2,1)S(1)} %get-tuple-element.43), channel_id=1, source_target_pairs={{0,14},{1,9},{8,0},{9,3},{2,8},{3,11},{10,2},{11,5},{4,10},{5,13},... | collective-permute-start | bytes 786440 | tf_op jit(solution)/shard_map/ppermute | solution.py:34
  110.0 9.9 %collective-permute-start.13 = (bf16[256,512]{1,0:T(8,128)(2,1)S(1)}, bf16[256,512]{1,0:T(8,128)(2,1)S(1)}, u32[]{:S(2)}, u32[]{:S(2)}) collective-permute-start(bf16[256,512]{1,0:T(8,128)(2,1)S(1)} %get-tuple-element.42), channel_id=1, source_target_pairs={{0,14},{1,9},{8,0},{9,3},{2,8},{3,11},{10,2},{11,5},{4,10},{5,13},... | collective-permute-start | bytes 786440 | tf_op jit(solution)/shard_map/ppermute | solution.py:34
  117.8 50.9 %copy-start.10 = (bf16[1,256,512]{2,1,0:T(8,128)(2,1)S(1)}, bf16[1,256,512]{2,1,0:T(8,128)(2,1)}, u32[]{:S(2)}) copy-start(bf16[1,256,512]{2,1,0:T(8,128)(2,1)} %param.14) | copy-start | bytes 786436
  117.8 7.8 %collective-permute-start.16 = (bf16[256,512]{1,0:T(8,128)(2,1)S(1)}, bf16[256,512]{1,0:T(8,128)(2,1)S(1)}, u32[]{:S(2)}, u32[]{:S(2)}) collective-permute-start(bf16[256,512]{1,0:T(8,128)(2,1)S(1)} %fusion.14), channel_id=1, source_target_pairs={{0,15},{1,8},{8,1},{9,2},{2,9},{3,10},{10,3},{11,4},{4,11},{5,12},... | collective-permute-start | bytes 786440 | tf_op jit(solution)/shard_map/ppermute | solution.py:34

commit v3 on v2

--- a/solution.py
+++ b/solution.py
@@ -92,6 +92,7 @@
     features = tokens.shape[2]
     norm_scale = (2 * ring * tokens.shape[1]) ** (-0.5)
 
+    everyone = lax.all_gather(shard, "col")
     beside = swap_core(tokens[0])
     a, b = hop(shard, ring, True, False), hop(shard, ring, True, True)
     blocks, places = [shard, a, b], [(0, 0), (1, 0), (1, 1)]
@@ -105,11 +106,6 @@
     inputs = arrange(tokens[0], beside, starts.astype(jnp.int32), rows)
 
     for k in range(2, half + 1):
-        if k == half - 1:
-            a, inputs, shard_behind = lax.optimization_barrier((a, inputs, shard))
-            anchor_pieces = scatter_pieces(shard_behind)
-        if k == half:
-            a, goals_beside = lax.optimization_barrier((a, goals_beside))
         a = hop(a, ring, True, False)
         blocks.append(a)
         if k < half:
@@ -118,6 +114,8 @@
         if k == 2:
             a, goals_own = lax.optimization_barrier((a, targets[0]))
             goals_beside = swap_core(goals_own)
+        if k == half - 1:
+            a, goals_beside, inputs = lax.optimization_barrier((a, goals_beside, inputs))
     goals = jnp.concatenate([targets[0], goals_beside], axis=0)
 
     part = None
@@ -125,7 +123,6 @@
         columns = inputs[:, index * rows : (index + 1) * rows]
         term = jnp.dot(columns, block, preferred_element_type=jnp.float32)
         part = term if part is None else part + term
-    part, anchor_pieces = lax.optimization_barrier((part, anchor_pieces))
     tokens_dev = part.shape[0] // 2
     swapped = swap_core(part.astype(jnp.bfloat16)).astype(jnp.float32)
     keys = part + jnp.concatenate([swapped[tokens_dev:], swapped[:tokens_dev]], axis=0)
@@ -134,9 +131,9 @@
 
     last = (ring - 2) * rows
     far_terms = contract_rows(inputs[:, last:], residual)
-    residual, anchor_pieces, _ = lax.optimization_barrier((residual, anchor_pieces, far_terms))
-    near_terms = contract_rows(inputs[:, :last], residual)
-    partner_anchor = deliver_pieces(anchor_pieces, partner)
+    near_terms = contract_rows(
+        inputs[:, :last], lax.optimization_barrier((residual, far_terms))[0]
+    )
 
     def term_of(k, stream):
         start = places.index((k, stream)) * rows
@@ -146,8 +143,6 @@
     a = hop(term_of(half, 0).astype(jnp.bfloat16), ring, False, False)
     b = hop(term_of(half - 1, 1).astype(jnp.bfloat16), ring, False, half == 2)
     for k in range(half - 1, 0, -1):
-        if k == 1:
-            a, partner_anchor = lax.optimization_barrier((a, partner_anchor))
         a = hop((term_of(k, 0) + a.astype(jnp.float32)).astype(jnp.bfloat16), ring, False, False)
         if k > 1:
             b = hop((term_of(k - 1, 1) + b.astype(jnp.float32)).astype(jnp.bfloat16), ring, False, k == 2)
@@ -162,6 +157,9 @@
         (delta.astype(jnp.bfloat16), delta, new_m, new_v)
     )
     partner_delta = deliver_pieces(scatter_pieces(sent), partner)
+    partner_anchor = lax.dynamic_index_in_dim(
+        everyone, partner[lax.axis_index("col")], 0, keepdims=False
+    )
     mean_delta = 0.5 * (delta + partner_delta.astype(jnp.float32))
     momentum = outer_momentum * outer_mom[0].astype(jnp.float32) + mean_delta
     moved = theta - outer_rate * (mean_delta + outer_momentum * momentum)

time: 172 us -> 157 us (0.913)
  blocking collectives: 40.1 us -> 0 us
  between operations: 1.1 us -> 16.4 us
  waiting for transfers between devices: 29 us -> 41.6 us
  starting transfers between devices: 73.3 us -> 84 us
  other arithmetic: 10.2 us -> 4.79 us
  matrix products: 9.65 us -> 4.85 us
  local copies, waits for them, and re-layouts: 6.58 us -> 3.64 us
    all_to_all x2 -> x0, blocking collectives: 40.1 us -> none  [the longest x1 21.4 us: scatter_pieces(): lax.all_to_all(pieces, 'col', split_axis=0, concat_axis=0, tiled=True)]
    ppermute x14, starting transfers between devices: 44.6 us -> 58 us  [hop(): return lax.ppermute(value, REPLICA, pairs)]
    all_to_all x1, waiting for transfers between devices: 0.01 us -> 11.4 us  [scatter_pieces(): lax.all_to_all(pieces, 'col', split_axis=0, concat_axis=0, tiled=True)]
    all_to_all x1, waiting for transfers between devices: 4.95 us -> 10.2 us  [deliver_pieces(): got = lax.all_to_all(turned, 'col', split_axis=0, concat_axis=0, tiled=True)]
    dot_general x8, matrix products: 8.13 us -> 3.36 us  [shards(): term = jnp.dot(columns, block, preferred_element_type=jnp.float32)]
    ppermute x14, waiting for transfers between devices: 22.2 us -> 17.4 us  [hop(): return lax.ppermute(value, REPLICA, pairs)]
    all_to_all x1, starting transfers between devices: 9.78 us -> 6.5 us  [deliver_pieces(): got = lax.all_to_all(turned, 'col', split_axis=0, concat_axis=0, tiled=True)]
    unnamed x24 -> x14, local copies, waits for them, and re-layouts: 4.58 us -> 1.62 us
  transfers between devices with their start and end apart: 19 -> 20, of which waited for: 10 -> 11; matrix products, arithmetic and copies ran while one was open for 8% -> 6% of each run, Pallas kernels for 0% -> 1%
where the time goes in v3:
time: 157 us; the launch traced here: 156 us
  starting transfers between devices  84 us (54%)
  waiting for transfers between devices  41.6 us (26%)
  between operations  16.4 us (10%)
  matrix products  4.85 us (3%)
  other arithmetic  4.79 us (3%)
  local copies, waits for them, and re-layouts  3.64 us (2%)
    ppermute x14, starting transfers between devices, hop(): return lax.ppermute(value, REPLICA, pairs)  58 us
    ppermute x14, waiting for transfers between devices, hop(): return lax.ppermute(value, REPLICA, pairs)  17.4 us
    all_to_all x1, starting transfers between devices, scatter_pieces(): lax.all_to_all(pieces, 'col', split_axis=0, concat_axis=0, tiled=True)  13.5 us
    all_to_all x1, waiting for transfers between devices, scatter_pieces(): lax.all_to_all(pieces, 'col', split_axis=0, concat_axis=0, tiled=True)  11.4 us
    all_to_all x1, waiting for transfers between devices, deliver_pieces(): got = lax.all_to_all(turned, 'col', split_axis=0, concat_axis=0, tiled=True)  10.2 us
    all_to_all x1, starting transfers between devices, deliver_pieces(): got = lax.all_to_all(turned, 'col', split_axis=0, concat_axis=0, tiled=True)  6.5 us
    ppermute x3, starting transfers between devices, swap_core(): return lax.ppermute(value, 'core', [(0, 1), (1, 0)])  5.9 us
    dot_general x8, matrix products, shards(): term = jnp.dot(columns, block, preferred_element_type=jnp.float32)  3.36 us
  transfers between devices with their start and end apart: 20, of which 11 were waited for; matrix products, arithmetic and copies ran while one was open for 6% of the time, Pallas kernels for 1%

profile of v3, /device:TPU:16, one launch (start us, length us, event | category | flops | bytes accessed | tf_op | source)
XLA Modules:
  0.0 156.1 jit_solution(14595411957822153147)
XLA Ops:
  7.2 0.7 all-gather.2.cloned.1.call-update
  7.9 1.9 %collective-permute-start.4 = (bf16[256,4096]{1,0:T(8,128)(2,1)}, bf16[256,4096]{1,0:T(8,128)(2,1)S(1)}, u32[]{:S(2)}, u32[]{:S(2)}) collective-permute-start(bf16[256,4096]{1,0:T(8,128)(2,1)} %bitcast.60), channel_id=1, source_target_pairs={{0,1},{1,0},{2,3},{3,2},{4,5},{5,4},{6,7},{7,6},{8,9},{9,8},{10,11... | collective-permute-start | bytes 6291464 | tf_op jit(solution)/shard_map/ppermute | solution.py:23
  9.8 3.5 %collective-permute-start = (bf16[256,512]{1,0:T(8,128)(2,1)}, bf16[256,512]{1,0:T(8,128)(2,1)S(1)}, u32[]{:S(2)}, u32[]{:S(2)}) collective-permute-start(bf16[256,512]{1,0:T(8,128)(2,1)} %bitcast.62), channel_id=1, source_target_pairs={{0,8},{1,15},{8,2},{9,1},{2,10},{3,9},{10,4},{11,3},{4,12},{5,11},... | collective-permute-start | bytes 786440 | tf_op jit(solution)/shard_map/ppermute | solution.py:34
  13.3 6.4 %collective-permute-start.5 = (bf16[256,512]{1,0:T(8,128)(2,1)}, bf16[256,512]{1,0:T(8,128)(2,1)S(1)}, u32[]{:S(2)}, u32[]{:S(2)}) collective-permute-start(bf16[256,512]{1,0:T(8,128)(2,1)} %bitcast.63), channel_id=1, source_target_pairs={{0,15},{1,8},{8,1},{9,2},{2,9},{3,10},{10,3},{11,4},{4,11},{5,12},... | collective-permute-start | bytes 786440 | tf_op jit(solution)/shard_map/ppermute | solution.py:34
  19.8 3.1 %collective-permute-start.1 = (bf16[256,512]{1,0:T(8,128)(2,1)S(1)}, bf16[256,512]{1,0:T(8,128)(2,1)S(1)}, u32[]{:S(2)}, u32[]{:S(2)}) collective-permute-start(bf16[256,512]{1,0:T(8,128)(2,1)S(1)} %collective-permute-done), channel_id=1, source_target_pairs={{0,8},{1,15},{8,2},{9,1},{2,10},{3,9},{10,4},{11,3},{4,12},{5,11},... | collective-permute-start | bytes 786440 | tf_op jit(solution)/shard_map/ppermute | solution.py:34
  22.9 1.1 collective-permute-done.5
  24.0 4.4 %collective-permute-start.6 = (bf16[256,512]{1,0:T(8,128)(2,1)S(1)}, bf16[256,512]{1,0:T(8,128)(2,1)S(1)}, u32[]{:S(2)}, u32[]{:S(2)}) collective-permute-start(bf16[256,512]{1,0:T(8,128)(2,1)S(1)} %collective-permute-done.5), channel_id=1, source_target_pairs={{0,8},{1,15},{8,2},{9,1},{2,10},{3,9},{10,4},{11,3},{4,12},{5,11},... | collective-permute-start | bytes 786440 | tf_op jit(solution)/shard_map/ppermute | solution.py:34
  28.4 1.4 collective-permute-done.1
  29.8 2.5 %collective-permute-start.2 = (bf16[256,512]{1,0:T(8,128)(2,1)S(1)}, bf16[256,512]{1,0:T(8,128)(2,1)}, u32[]{:S(2)}, u32[]{:S(2)}) collective-permute-start(bf16[256,512]{1,0:T(8,128)(2,1)S(1)} %collective-permute-done.1), channel_id=1, source_target_pairs={{0,8},{1,15},{8,2},{9,1},{2,10},{3,9},{10,4},{11,3},{4,12},{5,11},... | collective-permute-start | bytes 786440 | tf_op jit(solution)/shard_map/ppermute | solution.py:34
  32.3 1.9 %collective-permute-start.3 = (bf16[256,512]{1,0:T(8,128)(2,1)}, bf16[256,512]{1,0:T(8,128)(2,1)S(1)}, u32[]{:S(2)}, u32[]{:S(2)}) collective-permute-start(bf16[256,512]{1,0:T(8,128)(2,1)} %bitcast.64), channel_id=1, source_target_pairs={{0,1},{1,0},{2,3},{3,2},{4,5},{5,4},{6,7},{7,6},{8,9},{9,8},{10,11... | collective-permute-start | bytes 786440 | tf_op jit(solution)/shard_map/ppermute | solution.py:23
  34.2 0.7 fusion.41.starts_ref
  34.9 5.6 %collective-permute-start.7 = (bf16[256,512]{1,0:T(8,128)(2,1)S(1)}, bf16[256,512]{1,0:T(8,128)(2,1)S(1)}, u32[]{:S(2)}, u32[]{:S(2)}) collective-permute-start(bf16[256,512]{1,0:T(8,128)(2,1)S(1)} %collective-permute-done.6), channel_id=1, source_target_pairs={{0,8},{1,15},{8,2},{9,1},{2,10},{3,9},{10,4},{11,3},{4,12},{5,11},... | collective-permute-start | bytes 786440 | tf_op jit(solution)/shard_map/ppermute | solution.py:34
  40.6 1.6 %copy-done = bf16[1,256,4096]{2,1,0:T(8,128)(2,1)S(1)} copy-done((bf16[1,256,4096]{2,1,0:T(8,128)(2,1)S(1)}, bf16[1,256,4096]{2,1,0:T(8,128)(2,1)}, u32[]{:S(2)}) %copy-start) | copy-done | bytes 2097176
  42.1 0.9 arrange.1
  43.0 2.1 %collective-permute-start.8 = (bf16[256,512]{1,0:T(8,128)(2,1)}, bf16[256,512]{1,0:T(8,128)(2,1)S(1)}, u32[]{:S(2)}, u32[]{:S(2)}) collective-permute-start(bf16[256,512]{1,0:T(8,128)(2,1)} %collective-permute-done.2), channel_id=1, source_target_pairs={{0,8},{1,15},{8,2},{9,1},{2,10},{3,9},{10,4},{11,3},{4,12},{5,11},... | collective-permute-start | bytes 786440 | tf_op jit(solution)/shard_map/ppermute | solution.py:34
  45.1 0.3 fusion.35
  45.4 1.2 fusion.29
  46.7 0.3 fusion.31
  47.0 0.3 convolution_add_fusion.3
  47.3 0.3 convolution_add_fusion.2
  47.6 0.3 fusion.4
  47.9 3.8 %collective-permute-done.8 = bf16[256,512]{1,0:T(8,128)(2,1)S(1)} collective-permute-done((bf16[256,512]{1,0:T(8,128)(2,1)}, bf16[256,512]{1,0:T(8,128)(2,1)S(1)}, u32[]{:S(2)}, u32[]{:S(2)}) %collective-permute-start.8) | collective-permute-done | bytes 262176 | tf_op jit(solution)/shard_map/ppermute | solution.py:34
  51.7 0.3 fusion.26
  52.0 0.3 fusion.51
  52.3 2.1 %collective-permute-start.9 = (bf16[512,512]{1,0:T(8,128)(2,1)S(1)}, bf16[512,512]{1,0:T(8,128)(2,1)S(1)}, u32[]{:S(2)}, u32[]{:S(2)}) collective-permute-start(bf16[512,512]{1,0:T(8,128)(2,1)S(1)} %get-tuple-element.36), channel_id=1, source_target_pairs={{0,1},{1,0},{2,3},{3,2},{4,5},{5,4},{6,7},{7,6},{8,9},{9,8},{10,11... | collective-permute-start | bytes 1572872 | tf_op jit(solution)/shard_map/ppermute | solution.py:23
  54.4 1.9 %collective-permute-done.9 = bf16[512,512]{1,0:T(8,128)(2,1)S(1)} collective-permute-done((bf16[512,512]{1,0:T(8,128)(2,1)S(1)}, bf16[512,512]{1,0:T(8,128)(2,1)S(1)}, u32[]{:S(2)}, u32[]{:S(2)}) %collective-permute-start.9) | collective-permute-done | bytes 524320 | tf_op jit(solution)/shard_map/ppermute | solution.py:23
  56.4 0.3 fusion.7
  56.7 0.5 fusion.21
  57.2 4.3 %collective-permute-start.10 = (bf16[256,512]{1,0:T(8,128)(2,1)S(1)}, bf16[256,512]{1,0:T(8,128)(2,1)S(1)}, u32[]{:S(2)}, u32[]{:S(2)}) collective-permute-start(bf16[256,512]{1,0:T(8,128)(2,1)S(1)} %get-tuple-element.32), channel_id=1, source_target_pairs={{0,14},{1,9},{8,0},{9,3},{2,8},{3,11},{10,2},{11,5},{4,10},{5,13},... | collective-permute-start | bytes 786440 | tf_op jit(solution)/shard_map/ppermute | solution.py:34
  61.5 1.0 fusion
  62.6 2.9 %collective-permute-done.10 = bf16[256,512]{1,0:T(8,128)(2,1)S(1)} collective-permute-done((bf16[256,512]{1,0:T(8,128)(2,1)S(1)}, bf16[256,512]{1,0:T(8,128)(2,1)S(1)}, u32[]{:S(2)}, u32[]{:S(2)}) %collective-permute-start.10) | collective-permute-done | bytes 262176 | tf_op jit(solution)/shard_map/ppermute | solution.py:34
  65.6 4.3 %collective-permute-start.11 = (bf16[256,512]{1,0:T(8,128)(2,1)S(1)}, bf16[256,512]{1,0:T(8,128)(2,1)S(1)}, u32[]{:S(2)}, u32[]{:S(2)}) collective-permute-start(bf16[256,512]{1,0:T(8,128)(2,1)S(1)} %fusion.15), channel_id=1, source_target_pairs={{0,14},{1,9},{8,0},{9,3},{2,8},{3,11},{10,2},{11,5},{4,10},{5,13},... | collective-permute-start | bytes 786440 | tf_op jit(solution)/shard_map/ppermute | solution.py:34
  69.9 4.5 %collective-permute-start.14 = (bf16[256,512]{1,0:T(8,128)(2,1)S(1)}, bf16[256,512]{1,0:T(8,128)(2,1)S(1)}, u32[]{:S(2)}, u32[]{:S(2)}) collective-permute-start(bf16[256,512]{1,0:T(8,128)(2,1)S(1)} %get-tuple-element.33), channel_id=1, source_target_pairs={{0,14},{1,9},{8,0},{9,3},{2,8},{3,11},{10,2},{11,5},{4,10},{5,13},... | collective-permute-start | bytes 786440 | tf_op jit(solution)/shard_map/ppermute | solution.py:34
  74.5 4.5 %collective-permute-start.12 = (bf16[256,512]{1,0:T(8,128)(2,1)S(1)}, bf16[256,512]{1,0:T(8,128)(2,1)S(1)}, u32[]{:S(2)}, u32[]{:S(2)}) collective-permute-start(bf16[256,512]{1,0:T(8,128)(2,1)S(1)} %fusion.16), channel_id=1, source_target_pairs={{0,14},{1,9},{8,0},{9,3},{2,8},{3,11},{10,2},{11,5},{4,10},{5,13},... | collective-permute-start | bytes 786440 | tf_op jit(solution)/shard_map/ppermute | solution.py:34
  79.0 3.9 %collective-permute-done.12 = bf16[256,512]{1,0:T(8,128)(2,1)S(1)} collective-permute-done((bf16[256,512]{1,0:T(8,128)(2,1)S(1)}, bf16[256,512]{1,0:T(8,128)(2,1)S(1)}, u32[]{:S(2)}, u32[]{:S(2)}) %collective-permute-start.12) | collective-permute-done | bytes 262176 | tf_op jit(solution)/shard_map/ppermute | solution.py:34
  82.9 0.2 fusion.17
  83.1 4.4 %collective-permute-start.15 = (bf16[256,512]{1,0:T(8,128)(2,1)S(1)}, bf16[256,512]{1,0:T(8,128)(2,1)S(1)}, u32[]{:S(2)}, u32[]{:S(2)}) collective-permute-start(bf16[256,512]{1,0:T(8,128)(2,1)S(1)} %get-tuple-element.29), channel_id=1, source_target_pairs={{0,14},{1,9},{8,0},{9,3},{2,8},{3,11},{10,2},{11,5},{4,10},{5,13},... | collective-permute-start | bytes 786440 | tf_op jit(solution)/shard_map/ppermute | solution.py:34
  87.5 4.9 %collective-permute-start.13 = (bf16[256,512]{1,0:T(8,128)(2,1)S(1)}, bf16[256,512]{1,0:T(8,128)(2,1)S(1)}, u32[]{:S(2)}, u32[]{:S(2)}) collective-permute-start(bf16[256,512]{1,0:T(8,128)(2,1)S(1)} %get-tuple-element.28), channel_id=1, source_target_pairs={{0,14},{1,9},{8,0},{9,3},{2,8},{3,11},{10,2},{11,5},{4,10},{5,13},... | collective-permute-start | bytes 786440 | tf_op jit(solution)/shard_map/ppermute | solution.py:34
  92.6 3.6 %collective-permute-start.16 = (bf16[256,512]{1,0:T(8,128)(2,1)S(1)}, bf16[256,512]{1,0:T(8,128)(2,1)S(1)}, u32[]{:S(2)}, u32[]{:S(2)}) collective-permute-start(bf16[256,512]{1,0:T(8,128)(2,1)S(1)} %fusion.14), channel_id=1, source_target_pairs={{0,15},{1,8},{8,1},{9,2},{2,9},{3,10},{10,3},{11,4},{4,11},{5,12},... | collective-permute-start | bytes 786440 | tf_op jit(solution)/shard_map/ppermute | solution.py:34
  96.2 4.2 %collective-permute-done.16 = bf16[256,512]{1,0:T(8,128)(2,1)S(1)} collective-permute-done((bf16[256,512]{1,0:T(8,128)(2,1)S(1)}, bf16[256,512]{1,0:T(8,128)(2,1)S(1)}, u32[]{:S(2)}, u32[]{:S(2)}) %collective-permute-start.16) | collective-permute-done | bytes 262176 | tf_op jit(solution)/shard_map/ppermute | solution.py:34
  100.4 1.3 fusion.47
  101.7 13.5 %all-to-all-start = ((bf16[32,8,512]{2,1,0:T(8,128)(2,1)}), bf16[32,8,512]{2,1,0:T(8,128)(2,1)S(1)}, u32[]{:S(2)}, u32[]{:S(2)}) async-start(bf16[32,8,512]{2,1,0:T(8,128)(2,1)} %bitcast.5), calls=%async_computation | async-start | bytes 524288 | tf_op jit(solution)/shard_map/all_to_all | solution.py:75
  115.3 11.4 %all-to-all-done = bf16[32,8,512]{2,1,0:T(8,128)(2,1)S(1)} async-done(((bf16[32,8,512]{2,1,0:T(8,128)(2,1)}), bf16[32,8,512]{2,1,0:T(8,128)(2,1)S(1)}, u32[]{:S(2)}, u32[]{:S(2)}) %all-to-all-start) | async-done | bytes 262176 | tf_op jit(solution)/shard_map/all_to_all | solution.py:75
  126.7 1.3 gather_fusion
  128.0 6.5 %all-to-all-start.1 = ((bf16[32,8,512]{2,1,0:T(8,128)(2,1)}), bf16[32,8,512]{2,1,0:T(8,128)(2,1)S(1)}, u32[]{:S(2)}, u32[]{:S(2)}) async-start(bf16[32,8,512]{2,1,0:T(8,128)(2,1)} %gather_fusion), calls=%async_computation.1 | async-start | bytes 524288 | tf_op jit(solution)/shard_map/all_to_all | solution.py:80
  134.5 0.6 dynamic_slice.7
  137.0 10.2 %all-to-all-done.1 = bf16[32,8,512]{2,1,0:T(8,128)(2,1)S(1)} async-done(((bf16[32,8,512]{2,1,0:T(8,128)(2,1)}), bf16[32,8,512]{2,1,0:T(8,128)(2,1)S(1)}, u32[]{:S(2)}, u32[]{:S(2)}) %all-to-all-start.1) | async-done | bytes 262176 | tf_op jit(solution)/shard_map/all_to_all | solution.py:80
  147.2 2.0 %fusion.24 = (bf16[1,256,512]{2,1,0:T(8,128)(2,1)}, bf16[1,256,512]{2,1,0:T(8,128)(2,1)}) fusion(f32[256,512]{1,0:T(8,128)S(1)} %get-tuple-element.20, bf16[1,256,512]{2,1,0:T(8,128)(2,1)S(1)} %copy-done.5, bf16[32,8,512]{2,1,0:T(8,128)(2,1)S(1)} %all-to-all-done.1, bf16[32,256,512]{2,1,0:T(8,128)(2,1)} %all-gather.2.cloned.1.call-done, s32[]{:T(128)S(6)} %select_n.46, ...), kind=kLoop, calls=%fused_computation.43 | loop fusion | flops 2228224 | bytes 2097156 | tf_op jit(solution)/shard_map/broadcast_in_dim | solution.py:168
  (32 shorter events, 0.7 us)
Async XLA Ops:
  7.2 140.1 %all-gather.2.cloned.1.call-start = ((), (), s32[]{:S(2)}) async-start(), calls=%async_computation.2 | async-start | bytes 8650752 | tf_op jit(solution)/shard_map/all_gather | solution.py:95
  7.9 32.6 %collective-permute-start.4 = (bf16[256,4096]{1,0:T(8,128)(2,1)}, bf16[256,4096]{1,0:T(8,128)(2,1)S(1)}, u32[]{:S(2)}, u32[]{:S(2)}) collective-permute-start(bf16[256,4096]{1,0:T(8,128)(2,1)} %bitcast.60), channel_id=1, source_target_pairs={{0,1},{1,0},{2,3},{3,2},{4,5},{5,4},{6,7},{7,6},{8,9},{9,8},{10,11... | collective-permute-start | bytes 6291464 | tf_op jit(solution)/shard_map/ppermute | solution.py:23
  9.8 9.9 %collective-permute-start = (bf16[256,512]{1,0:T(8,128)(2,1)}, bf16[256,512]{1,0:T(8,128)(2,1)S(1)}, u32[]{:S(2)}, u32[]{:S(2)}) collective-permute-start(bf16[256,512]{1,0:T(8,128)(2,1)} %bitcast.62), channel_id=1, source_target_pairs={{0,8},{1,15},{8,2},{9,1},{2,10},{3,9},{10,4},{11,3},{4,12},{5,11},... | collective-permute-start | bytes 786440 | tf_op jit(solution)/shard_map/ppermute | solution.py:34
  13.3 10.7 %collective-permute-start.5 = (bf16[256,512]{1,0:T(8,128)(2,1)}, bf16[256,512]{1,0:T(8,128)(2,1)S(1)}, u32[]{:S(2)}, u32[]{:S(2)}) collective-permute-start(bf16[256,512]{1,0:T(8,128)(2,1)} %bitcast.63), channel_id=1, source_target_pairs={{0,15},{1,8},{8,1},{9,2},{2,9},{3,10},{10,3},{11,4},{4,11},{5,12},... | collective-permute-start | bytes 786440 | tf_op jit(solution)/shard_map/ppermute | solution.py:34
  19.8 10.0 %collective-permute-start.1 = (bf16[256,512]{1,0:T(8,128)(2,1)S(1)}, bf16[256,512]{1,0:T(8,128)(2,1)S(1)}, u32[]{:S(2)}, u32[]{:S(2)}) collective-permute-start(bf16[256,512]{1,0:T(8,128)(2,1)S(1)} %collective-permute-done), channel_id=1, source_target_pairs={{0,8},{1,15},{8,2},{9,1},{2,10},{3,9},{10,4},{11,3},{4,12},{5,11},... | collective-permute-start | bytes 786440 | tf_op jit(solution)/shard_map/ppermute | solution.py:34
  24.0 10.9 %collective-permute-start.6 = (bf16[256,512]{1,0:T(8,128)(2,1)S(1)}, bf16[256,512]{1,0:T(8,128)(2,1)S(1)}, u32[]{:S(2)}, u32[]{:S(2)}) collective-permute-start(bf16[256,512]{1,0:T(8,128)(2,1)S(1)} %collective-permute-done.5), channel_id=1, source_target_pairs={{0,8},{1,15},{8,2},{9,1},{2,10},{3,9},{10,4},{11,3},{4,12},{5,11},... | collective-permute-start | bytes 786440 | tf_op jit(solution)/shard_map/ppermute | solution.py:34
  29.8 13.2 %collective-permute-start.2 = (bf16[256,512]{1,0:T(8,128)(2,1)S(1)}, bf16[256,512]{1,0:T(8,128)(2,1)}, u32[]{:S(2)}, u32[]{:S(2)}) collective-permute-start(bf16[256,512]{1,0:T(8,128)(2,1)S(1)} %collective-permute-done.1), channel_id=1, source_target_pairs={{0,8},{1,15},{8,2},{9,1},{2,10},{3,9},{10,4},{11,3},{4,12},{5,11},... | collective-permute-start | bytes 786440 | tf_op jit(solution)/shard_map/ppermute | solution.py:34
  32.3 10.8 %collective-permute-start.3 = (bf16[256,512]{1,0:T(8,128)(2,1)}, bf16[256,512]{1,0:T(8,128)(2,1)S(1)}, u32[]{:S(2)}, u32[]{:S(2)}) collective-permute-start(bf16[256,512]{1,0:T(8,128)(2,1)} %bitcast.64), channel_id=1, source_target_pairs={{0,1},{1,0},{2,3},{3,2},{4,5},{5,4},{6,7},{7,6},{8,9},{9,8},{10,11... | collective-permute-start | bytes 786440 | tf_op jit(solution)/shard_map/ppermute | solution.py:23
  34.9 17.0 %collective-permute-start.7 = (bf16[256,512]{1,0:T(8,128)(2,1)S(1)}, bf16[256,512]{1,0:T(8,128)(2,1)S(1)}, u32[]{:S(2)}, u32[]{:S(2)}) collective-permute-start(bf16[256,512]{1,0:T(8,128)(2,1)S(1)} %collective-permute-done.6), channel_id=1, source_target_pairs={{0,8},{1,15},{8,2},{9,1},{2,10},{3,9},{10,4},{11,3},{4,12},{5,11},... | collective-permute-start | bytes 786440 | tf_op jit(solution)/shard_map/ppermute | solution.py:34
  40.5 1.6 %copy-start = (bf16[1,256,4096]{2,1,0:T(8,128)(2,1)S(1)}, bf16[1,256,4096]{2,1,0:T(8,128)(2,1)}, u32[]{:S(2)}) copy-start(bf16[1,256,4096]{2,1,0:T(8,128)(2,1)} %param.9) | copy-start | bytes 6291460
  43.0 3.9 %copy-start.1 = (bf16[1,256,512]{2,1,0:T(8,128)(2,1)S(1)}, bf16[1,256,512]{2,1,0:T(8,128)(2,1)}, u32[]{:S(2)}) copy-start(bf16[1,256,512]{2,1,0:T(8,128)(2,1)} %param.11) | copy-start | bytes 786436
  43.0 8.6 %collective-permute-start.8 = (bf16[256,512]{1,0:T(8,128)(2,1)}, bf16[256,512]{1,0:T(8,128)(2,1)S(1)}, u32[]{:S(2)}, u32[]{:S(2)}) collective-permute-start(bf16[256,512]{1,0:T(8,128)(2,1)} %collective-permute-done.2), channel_id=1, source_target_pairs={{0,8},{1,15},{8,2},{9,1},{2,10},{3,9},{10,4},{11,3},{4,12},{5,11},... | collective-permute-start | bytes 786440 | tf_op jit(solution)/shard_map/ppermute | solution.py:34
  52.3 4.1 %copy-start.2 = (bf16[1,256,512]{2,1,0:T(8,128)(2,1)S(1)}, bf16[1,256,512]{2,1,0:T(8,128)(2,1)}, u32[]{:S(2)}) copy-start(bf16[1,256,512]{2,1,0:T(8,128)(2,1)} %param.10) | copy-start | bytes 786436
  52.3 3.9 %collective-permute-start.9 = (bf16[512,512]{1,0:T(8,128)(2,1)S(1)}, bf16[512,512]{1,0:T(8,128)(2,1)S(1)}, u32[]{:S(2)}, u32[]{:S(2)}) collective-permute-start(bf16[512,512]{1,0:T(8,128)(2,1)S(1)} %get-tuple-element.36), channel_id=1, source_target_pairs={{0,1},{1,0},{2,3},{3,2},{4,5},{5,4},{6,7},{7,6},{8,9},{9,8},{10,11... | collective-permute-start | bytes 1572872 | tf_op jit(solution)/shard_map/ppermute | solution.py:23
  57.2 8.3 %collective-permute-start.10 = (bf16[256,512]{1,0:T(8,128)(2,1)S(1)}, bf16[256,512]{1,0:T(8,128)(2,1)S(1)}, u32[]{:S(2)}, u32[]{:S(2)}) collective-permute-start(bf16[256,512]{1,0:T(8,128)(2,1)S(1)} %get-tuple-element.32), channel_id=1, source_target_pairs={{0,14},{1,9},{8,0},{9,3},{2,8},{3,11},{10,2},{11,5},{4,10},{5,13},... | collective-permute-start | bytes 786440 | tf_op jit(solution)/shard_map/ppermute | solution.py:34
  65.6 8.9 %collective-permute-start.11 = (bf16[256,512]{1,0:T(8,128)(2,1)S(1)}, bf16[256,512]{1,0:T(8,128)(2,1)S(1)}, u32[]{:S(2)}, u32[]{:S(2)}) collective-permute-start(bf16[256,512]{1,0:T(8,128)(2,1)S(1)} %fusion.15), channel_id=1, source_target_pairs={{0,14},{1,9},{8,0},{9,3},{2,8},{3,11},{10,2},{11,5},{4,10},{5,13},... | collective-permute-start | bytes 786440 | tf_op jit(solution)/shard_map/ppermute | solution.py:34
  69.9 30.5 %copy-start.3 = (bf16[1,256,512]{2,1,0:T(8,128)(2,1)S(1)}, bf16[1,256,512]{2,1,0:T(8,128)(2,1)}, u32[]{:S(2)}) copy-start(bf16[1,256,512]{2,1,0:T(8,128)(2,1)} %param.13) | copy-start | bytes 786436
  69.9 30.5 %copy-start.4 = (bf16[1,256,512]{2,1,0:T(8,128)(2,1)S(1)}, bf16[1,256,512]{2,1,0:T(8,128)(2,1)}, u32[]{:S(2)}) copy-start(bf16[1,256,512]{2,1,0:T(8,128)(2,1)} %param.12) | copy-start | bytes 786436
  69.9 9.1 %collective-permute-start.14 = (bf16[256,512]{1,0:T(8,128)(2,1)S(1)}, bf16[256,512]{1,0:T(8,128)(2,1)S(1)}, u32[]{:S(2)}, u32[]{:S(2)}) collective-permute-start(bf16[256,512]{1,0:T(8,128)(2,1)S(1)} %get-tuple-element.33), channel_id=1, source_target_pairs={{0,14},{1,9},{8,0},{9,3},{2,8},{3,11},{10,2},{11,5},{4,10},{5,13},... | collective-permute-start | bytes 786440 | tf_op jit(solution)/shard_map/ppermute | solution.py:34
  74.5 8.3 %collective-permute-start.12 = (bf16[256,512]{1,0:T(8,128)(2,1)S(1)}, bf16[256,512]{1,0:T(8,128)(2,1)S(1)}, u32[]{:S(2)}, u32[]{:S(2)}) collective-permute-start(bf16[256,512]{1,0:T(8,128)(2,1)S(1)} %fusion.16), channel_id=1, source_target_pairs={{0,14},{1,9},{8,0},{9,3},{2,8},{3,11},{10,2},{11,5},{4,10},{5,13},... | collective-permute-start | bytes 786440 | tf_op jit(solution)/shard_map/ppermute | solution.py:34
  83.1 9.4 %collective-permute-start.15 = (bf16[256,512]{1,0:T(8,128)(2,1)S(1)}, bf16[256,512]{1,0:T(8,128)(2,1)S(1)}, u32[]{:S(2)}, u32[]{:S(2)}) collective-permute-start(bf16[256,512]{1,0:T(8,128)(2,1)S(1)} %get-tuple-element.29), channel_id=1, source_target_pairs={{0,14},{1,9},{8,0},{9,3},{2,8},{3,11},{10,2},{11,5},{4,10},{5,13},... | collective-permute-start | bytes 786440 | tf_op jit(solution)/shard_map/ppermute | solution.py:34
  87.5 8.8 %collective-permute-start.13 = (bf16[256,512]{1,0:T(8,128)(2,1)S(1)}, bf16[256,512]{1,0:T(8,128)(2,1)S(1)}, u32[]{:S(2)}, u32[]{:S(2)}) collective-permute-start(bf16[256,512]{1,0:T(8,128)(2,1)S(1)} %get-tuple-element.28), channel_id=1, source_target_pairs={{0,14},{1,9},{8,0},{9,3},{2,8},{3,11},{10,2},{11,5},{4,10},{5,13},... | collective-permute-start | bytes 786440 | tf_op jit(solution)/shard_map/ppermute | solution.py:34
  92.6 22.7 %copy-start.6 = (s32[32]{0:T(128)S(1)}, s32[32]{0:T(128)}, u32[]{:S(2)}) copy-start(s32[32]{0:T(128)} %param.15) | copy-start | bytes 388
  92.6 54.6 %copy-start.5 = (bf16[1,256,512]{2,1,0:T(8,128)(2,1)S(1)}, bf16[1,256,512]{2,1,0:T(8,128)(2,1)}, u32[]{:S(2)}) copy-start(bf16[1,256,512]{2,1,0:T(8,128)(2,1)} %param.14) | copy-start | bytes 786436
  92.6 7.8 %collective-permute-start.16 = (bf16[256,512]{1,0:T(8,128)(2,1)S(1)}, bf16[256,512]{1,0:T(8,128)(2,1)S(1)}, u32[]{:S(2)}, u32[]{:S(2)}) collective-permute-start(bf16[256,512]{1,0:T(8,128)(2,1)S(1)} %fusion.14), channel_id=1, source_target_pairs={{0,15},{1,8},{8,1},{9,2},{2,9},{3,10},{10,3},{11,4},{4,11},{5,12},... | collective-permute-start | bytes 786440 | tf_op jit(solution)/shard_map/ppermute | solution.py:34
  101.7 25.0 %all-to-all-start = ((bf16[32,8,512]{2,1,0:T(8,128)(2,1)}), bf16[32,8,512]{2,1,0:T(8,128)(2,1)S(1)}, u32[]{:S(2)}, u32[]{:S(2)}) async-start(bf16[32,8,512]{2,1,0:T(8,128)(2,1)} %bitcast.5), calls=%async_computation | async-start | bytes 524288 | tf_op jit(solution)/shard_map/all_to_all | solution.py:75
  128.0 19.2 %all-to-all-start.1 = ((bf16[32,8,512]{2,1,0:T(8,128)(2,1)}), bf16[32,8,512]{2,1,0:T(8,128)(2,1)S(1)}, u32[]{:S(2)}, u32[]{:S(2)}) async-start(bf16[32,8,512]{2,1,0:T(8,128)(2,1)} %gather_fusion), calls=%async_computation.1 | async-start | bytes 524288 | tf_op jit(solution)/shard_map/all_to_all | solution.py:80
Sparse Core Ops, SparseCore 0:
  11.2 108.9 all-gather.1

commit v4 on v3

--- a/solution.py
+++ b/solution.py
@@ -23,13 +23,13 @@
     return lax.ppermute(value, "core", [(0, 1), (1, 0)])
 
 
-def hop(value, ring, outward, cross):
+def hop(value, ring, outward, cross=False, chips=1):
     pairs = []
     for y in range(ring):
         for core in range(2):
             end = core ^ 1 if cross else core
             up = end == 0 if outward else core == 1
-            to = (y + (1 if up else -1)) % ring
+            to = (y + (chips if up else -chips)) % ring
             pairs.append((place_of(y, core, ring), place_of(to, end, ring)))
     return lax.ppermute(value, REPLICA, pairs)
 
@@ -75,8 +75,24 @@
     return lax.all_to_all(pieces, "col", split_axis=0, concat_axis=0, tiled=True)
 
 
+def turn_kernel(partner_ref, pieces_ref, out_ref):
+    for column in range(out_ref.shape[0]):
+        out_ref[column] = pieces_ref[partner_ref[column]]
+
+
 def deliver_pieces(pieces, partner):
-    turned = pieces.at[partner].get(mode="promise_in_bounds")
+    vmem = pl.BlockSpec(memory_space=pltpu.VMEM)
+    turned = pl.pallas_call(
+        turn_kernel,
+        out_shape=jax.ShapeDtypeStruct(pieces.shape, pieces.dtype),
+        in_specs=[pl.BlockSpec(memory_space=pltpu.SMEM), vmem],
+        out_specs=vmem,
+        compiler_params=pltpu.CompilerParams(vmem_limit_bytes=4 * 2**20),
+        cost_estimate=pl.CostEstimate(
+            flops=0, bytes_accessed=4 * pieces.size, transcendentals=0
+        ),
+        name="turn",
+    )(partner, pieces)
     got = lax.all_to_all(turned, "col", split_axis=0, concat_axis=0, tiled=True)
     return got.reshape(got.shape[0] * got.shape[1], got.shape[2])
 
@@ -94,29 +110,21 @@
 
     everyone = lax.all_gather(shard, "col")
     beside = swap_core(tokens[0])
-    a, b = hop(shard, ring, True, False), hop(shard, ring, True, True)
-    blocks, places = [shard, a, b], [(0, 0), (1, 0), (1, 1)]
-    for k in range(2, half + 1):
-        places += [(k, 0), (k, 1)] if k < half else [(k, 0)]
-
+    a1, b1 = hop(shard, ring, True), hop(shard, ring, True, cross=True)
+    a3, b2, a2 = hop(a1, ring, True, chips=2), hop(b1, ring, True), hop(a1, ring, True)
+    b2, goals_own = lax.optimization_barrier((b2, targets[0]))
+    goals_beside = swap_core(goals_own)
+
+    places = [(0, 0), (1, 0), (1, 1), (3, 0), (2, 1), (2, 0), (3, 1), (4, 0)]
     away = jnp.array([k for k, _ in places], jnp.int32)
     other = jnp.array([o for _, o in places], jnp.int32)
     source = (chip + jnp.where(core == 0, -away, away)) % ring
     starts = ((source % 2 * half + source // 2) * 2 + (core + other) % 2) * rows
     inputs = arrange(tokens[0], beside, starts.astype(jnp.int32), rows)
 
-    for k in range(2, half + 1):
-        a = hop(a, ring, True, False)
-        blocks.append(a)
-        if k < half:
-            b = hop(b, ring, True, False)
-            blocks.append(b)
-        if k == 2:
-            a, goals_own = lax.optimization_barrier((a, targets[0]))
-            goals_beside = swap_core(goals_own)
-        if k == half - 1:
-            a, goals_beside, inputs = lax.optimization_barrier((a, goals_beside, inputs))
+    a3, goals_beside, inputs = lax.optimization_barrier((a3, goals_beside, inputs))
     goals = jnp.concatenate([targets[0], goals_beside], axis=0)
+    blocks = [shard, a1, b1, a3, b2, a2, hop(b2, ring, True), hop(a3, ring, True)]
 
     part = None
     for index, block in enumerate(blocks):
@@ -140,13 +148,20 @@
         terms, start = (far_terms, start - last) if start >= last else (near_terms, start)
         return terms[start : start + rows]
 
-    a = hop(term_of(half, 0).astype(jnp.bfloat16), ring, False, False)
-    b = hop(term_of(half - 1, 1).astype(jnp.bfloat16), ring, False, half == 2)
-    for k in range(half - 1, 0, -1):
-        a = hop((term_of(k, 0) + a.astype(jnp.float32)).astype(jnp.bfloat16), ring, False, False)
-        if k > 1:
-            b = hop((term_of(k - 1, 1) + b.astype(jnp.float32)).astype(jnp.bfloat16), ring, False, k == 2)
-    grad = (term_of(0, 0) + a.astype(jnp.float32) + b.astype(jnp.float32)) * norm_scale
+    def send(value, **way):
+        return hop(value, ring, False, **way).astype(jnp.float32)
+
+    def both(first, second):
+        return lax.optimization_barrier((first.astype(jnp.bfloat16), second.astype(jnp.bfloat16)))
+
+    four, three = both(term_of(4, 0), term_of(3, 1))
+    four, three = send(four), send(three)
+    two = send(term_of(2, 0).astype(jnp.bfloat16))
+    four, three = both(term_of(3, 0) + four, term_of(2, 1) + three)
+    four, three = send(four, chips=2), send(three)
+    one, crossed = both(term_of(1, 0) + two + four, term_of(1, 1) + three)
+    from_one, crossed = send(one), send(crossed, cross=True)
+    grad = (term_of(0, 0) + from_one + crossed) * norm_scale
 
     theta = shard.astype(jnp.float32)
     first = beta_one * adam_m[0].astype(jnp.float32) + (1.0 - beta_one) * grad
@@ -157,15 +172,17 @@
         (delta.astype(jnp.bfloat16), delta, new_m, new_v)
     )
     partner_delta = deliver_pieces(scatter_pieces(sent), partner)
-    partner_anchor = lax.dynamic_index_in_dim(
-        everyone, partner[lax.axis_index("col")], 0, keepdims=False
-    )
     mean_delta = 0.5 * (delta + partner_delta.astype(jnp.float32))
     momentum = outer_momentum * outer_mom[0].astype(jnp.float32) + mean_delta
     moved = theta - outer_rate * (mean_delta + outer_momentum * momentum)
+    moved, new_mom, everyone = lax.optimization_barrier(
+        (moved, momentum.astype(jnp.bfloat16), everyone)
+    )
+    partner_anchor = lax.dynamic_index_in_dim(
+        everyone, partner[lax.axis_index("col")], 0, keepdims=False
+    )
     moved = moved - pull_rate * 0.5 * (theta - partner_anchor.astype(jnp.float32))
-    moved, momentum = moved.astype(jnp.bfloat16), momentum.astype(jnp.bfloat16)
-    return moved[None], new_m[None], new_v[None], momentum[None]
+    return moved.astype(jnp.bfloat16)[None], new_m[None], new_v[None], new_mom[None]
 
 
 def solution(mesh):

time: 157 us -> 152 us (0.968)
  the two profiles are of different devices: /device:TPU:16 before, /device:TPU:64 now
where the time goes in v4:
time: 152 us; the launch traced here: 151 us
  starting transfers between devices  55 us (36%)
  waiting for transfers between devices  38.1 us (25%)
  blocking collectives  26.4 us (17%)
  between operations  16.3 us (11%)
  other arithmetic  5.42 us (4%)
  matrix products  4.96 us (3%)
  local copies, waits for them, and re-layouts  2.4 us (2%)
  Pallas kernels  2.11 us (1%)
    ppermute x14, starting transfers between devices, hop(): return lax.ppermute(value, REPLICA, pairs)  43.8 us
    ppermute x14, waiting for transfers between devices, hop(): return lax.ppermute(value, REPLICA, pairs)  27 us
    all_to_all x1, blocking collectives, scatter_pieces(): lax.all_to_all(pieces, 'col', split_axis=0, concat_axis=0, tiled=True)  26.4 us
    all_to_all x1, waiting for transfers between devices, deliver_pieces(): got = lax.all_to_all(turned, 'col', split_axis=0, concat_axis=0, tiled=True)  8.52 us
    ppermute x3, starting transfers between devices, swap_core(): return lax.ppermute(value, 'core', [(0, 1), (1, 0)])  5.89 us
    all_to_all x1, starting transfers between devices, deliver_pieces(): got = lax.all_to_all(turned, 'col', split_axis=0, concat_axis=0, tiled=True)  5.34 us
    dot_general x8, matrix products, shards(): term = jnp.dot(columns, block, preferred_element_type=jnp.float32)  3.48 us
  transfers between devices with their start and end apart: 19, of which 11 were waited for; matrix products, arithmetic and copies ran while one was open for 6% of the time, Pallas kernels for 1%

profile of v4, /device:TPU:64, one launch (start us, length us, event | category | flops | bytes accessed | tf_op | source)
XLA Modules:
  0.0 150.7 jit_solution(16951857996723434983)
XLA Ops:
  7.2 0.7 all-gather.2.cloned.1.call-update
  7.9 1.9 %collective-permute-start.5 = (bf16[256,4096]{1,0:T(8,128)(2,1)}, bf16[256,4096]{1,0:T(8,128)(2,1)S(1)}, u32[]{:S(2)}, u32[]{:S(2)}) collective-permute-start(bf16[256,4096]{1,0:T(8,128)(2,1)} %bitcast.52), channel_id=1, source_target_pairs={{0,1},{1,0},{2,3},{3,2},{4,5},{5,4},{6,7},{7,6},{8,9},{9,8},{10,11... | collective-permute-start | bytes 6291464 | tf_op jit(solution)/shard_map/ppermute | solution.py:23
  9.8 5.5 %collective-permute-start.2 = (bf16[256,512]{1,0:T(8,128)(2,1)}, bf16[256,512]{1,0:T(8,128)(2,1)S(1)}, u32[]{:S(2)}, u32[]{:S(2)}) collective-permute-start(bf16[256,512]{1,0:T(8,128)(2,1)} %bitcast.54), channel_id=1, source_target_pairs={{0,15},{1,8},{8,1},{9,2},{2,9},{3,10},{10,3},{11,4},{4,11},{5,12},... | collective-permute-start | bytes 786440 | tf_op jit(solution)/shard_map/ppermute | solution.py:34
  15.3 1.9 %collective-permute-start = (bf16[256,512]{1,0:T(8,128)(2,1)}, bf16[256,512]{1,0:T(8,128)(2,1)S(1)}, u32[]{:S(2)}, u32[]{:S(2)}) collective-permute-start(bf16[256,512]{1,0:T(8,128)(2,1)} %bitcast.55), channel_id=1, source_target_pairs={{0,8},{1,15},{8,2},{9,1},{2,10},{3,9},{10,4},{11,3},{4,12},{5,11},... | collective-permute-start | bytes 786440 | tf_op jit(solution)/shard_map/ppermute | solution.py:34
  17.2 3.7 %collective-permute-done.2 = bf16[256,512]{1,0:T(8,128)(2,1)S(1)} collective-permute-done((bf16[256,512]{1,0:T(8,128)(2,1)}, bf16[256,512]{1,0:T(8,128)(2,1)S(1)}, u32[]{:S(2)}, u32[]{:S(2)}) %collective-permute-start.2) | collective-permute-done | bytes 262176 | tf_op jit(solution)/shard_map/ppermute | solution.py:34
  20.9 1.9 %collective-permute-start.3 = (bf16[256,512]{1,0:T(8,128)(2,1)S(1)}, bf16[256,512]{1,0:T(8,128)(2,1)}, u32[]{:S(2)}, u32[]{:S(2)}) collective-permute-start(bf16[256,512]{1,0:T(8,128)(2,1)S(1)} %collective-permute-done.2), channel_id=1, source_target_pairs={{0,8},{1,15},{8,2},{9,1},{2,10},{3,9},{10,4},{11,3},{4,12},{5,11},... | collective-permute-start | bytes 786440 | tf_op jit(solution)/shard_map/ppermute | solution.py:34
  22.8 2.2 %collective-permute-done = bf16[256,512]{1,0:T(8,128)(2,1)S(1)} collective-permute-done((bf16[256,512]{1,0:T(8,128)(2,1)}, bf16[256,512]{1,0:T(8,128)(2,1)S(1)}, u32[]{:S(2)}, u32[]{:S(2)}) %collective-permute-start) | collective-permute-done | bytes 262176 | tf_op jit(solution)/shard_map/ppermute | solution.py:34
  25.0 1.9 %collective-permute-start.1 = (bf16[256,512]{1,0:T(8,128)(2,1)S(1)}, bf16[256,512]{1,0:T(8,128)(2,1)S(1)}, u32[]{:S(2)}, u32[]{:S(2)}) collective-permute-start(bf16[256,512]{1,0:T(8,128)(2,1)S(1)} %collective-permute-done), channel_id=1, source_target_pairs={{0,2},{1,7},{8,10},{9,15},{2,4},{3,1},{10,12},{11,9},{4,6},{5,3},{... | collective-permute-start | bytes 786440 | tf_op jit(solution)/shard_map/ppermute | solution.py:34
  26.9 3.5 %collective-permute-done.3 = bf16[256,512]{1,0:T(8,128)(2,1)} collective-permute-done((bf16[256,512]{1,0:T(8,128)(2,1)S(1)}, bf16[256,512]{1,0:T(8,128)(2,1)}, u32[]{:S(2)}, u32[]{:S(2)}) %collective-permute-start.3) | collective-permute-done | bytes 262176 | tf_op jit(solution)/shard_map/ppermute | solution.py:34
  30.5 1.9 %collective-permute-start.4 = (bf16[256,512]{1,0:T(8,128)(2,1)}, bf16[256,512]{1,0:T(8,128)(2,1)S(1)}, u32[]{:S(2)}, u32[]{:S(2)}) collective-permute-start(bf16[256,512]{1,0:T(8,128)(2,1)} %bitcast.57), channel_id=1, source_target_pairs={{0,1},{1,0},{2,3},{3,2},{4,5},{5,4},{6,7},{7,6},{8,9},{9,8},{10,11... | collective-permute-start | bytes 786440 | tf_op jit(solution)/shard_map/ppermute | solution.py:23
  32.4 0.7 fusion.42.starts_ref
  33.1 1.9 %collective-permute-start.6 = (bf16[256,512]{1,0:T(8,128)(2,1)S(1)}, bf16[256,512]{1,0:T(8,128)(2,1)S(1)}, u32[]{:S(2)}, u32[]{:S(2)}) collective-permute-start(bf16[256,512]{1,0:T(8,128)(2,1)S(1)} %collective-permute-done), channel_id=1, source_target_pairs={{0,8},{1,15},{8,2},{9,1},{2,10},{3,9},{10,4},{11,3},{4,12},{5,11},... | collective-permute-start | bytes 786440 | tf_op jit(solution)/shard_map/ppermute | solution.py:34
  35.0 2.5 %collective-permute-start.7 = (bf16[256,512]{1,0:T(8,128)(2,1)}, bf16[256,512]{1,0:T(8,128)(2,1)S(1)}, u32[]{:S(2)}, u32[]{:S(2)}) collective-permute-start(bf16[256,512]{1,0:T(8,128)(2,1)} %collective-permute-done.3), channel_id=1, source_target_pairs={{0,8},{1,15},{8,2},{9,1},{2,10},{3,9},{10,4},{11,3},{4,12},{5,11},... | collective-permute-start | bytes 786440 | tf_op jit(solution)/shard_map/ppermute | solution.py:34
  37.6 1.6 %copy-done = bf16[1,256,4096]{2,1,0:T(8,128)(2,1)S(1)} copy-done((bf16[1,256,4096]{2,1,0:T(8,128)(2,1)S(1)}, bf16[1,256,4096]{2,1,0:T(8,128)(2,1)}, u32[]{:S(2)}) %copy-start) | copy-done | bytes 2097176
  39.2 0.8 arrange.1
  40.0 3.5 %collective-permute-start.8 = (bf16[256,512]{1,0:T(8,128)(2,1)S(1)}, bf16[256,512]{1,0:T(8,128)(2,1)S(1)}, u32[]{:S(2)}, u32[]{:S(2)}) collective-permute-start(bf16[256,512]{1,0:T(8,128)(2,1)S(1)} %collective-permute-done.1), channel_id=1, source_target_pairs={{0,8},{1,15},{8,2},{9,1},{2,10},{3,9},{10,4},{11,3},{4,12},{5,11},... | collective-permute-start | bytes 786440 | tf_op jit(solution)/shard_map/ppermute | solution.py:34
  43.5 0.3 fusion.37
  43.8 0.3 convolution_add_fusion.2
  44.1 0.3 convolution_add_fusion.1
  44.4 1.3 fusion.33
  46.0 0.3 fusion.31
  46.3 3.2 %collective-permute-done.8 = bf16[256,512]{1,0:T(8,128)(2,1)S(1)} collective-permute-done((bf16[256,512]{1,0:T(8,128)(2,1)S(1)}, bf16[256,512]{1,0:T(8,128)(2,1)S(1)}, u32[]{:S(2)}, u32[]{:S(2)}) %collective-permute-start.8) | collective-permute-done | bytes 262176 | tf_op jit(solution)/shard_map/ppermute | solution.py:34
  49.5 0.3 fusion.27
  49.8 0.4 fusion.52
  50.2 2.1 %collective-permute-start.9 = (bf16[512,512]{1,0:T(8,128)(2,1)S(1)}, bf16[512,512]{1,0:T(8,128)(2,1)S(1)}, u32[]{:S(2)}, u32[]{:S(2)}) collective-permute-start(bf16[512,512]{1,0:T(8,128)(2,1)S(1)} %get-tuple-element.56), channel_id=1, source_target_pairs={{0,1},{1,0},{2,3},{3,2},{4,5},{5,4},{6,7},{7,6},{8,9},{9,8},{10,11... | collective-permute-start | bytes 1572872 | tf_op jit(solution)/shard_map/ppermute | solution.py:23
  52.3 1.9 %collective-permute-done.9 = bf16[512,512]{1,0:T(8,128)(2,1)S(1)} collective-permute-done((bf16[512,512]{1,0:T(8,128)(2,1)S(1)}, bf16[512,512]{1,0:T(8,128)(2,1)S(1)}, u32[]{:S(2)}, u32[]{:S(2)}) %collective-permute-start.9) | collective-permute-done | bytes 524320 | tf_op jit(solution)/shard_map/ppermute | solution.py:23
  54.3 0.3 fusion.8
  54.6 0.5 fusion.22
  55.2 3.4 %collective-permute-start.11 = (bf16[256,512]{1,0:T(8,128)(2,1)S(1)}, bf16[256,512]{1,0:T(8,128)(2,1)S(1)}, u32[]{:S(2)}, u32[]{:S(2)}) collective-permute-start(bf16[256,512]{1,0:T(8,128)(2,1)S(1)} %get-tuple-element.29), channel_id=1, source_target_pairs={{0,14},{1,9},{8,0},{9,3},{2,8},{3,11},{10,2},{11,5},{4,10},{5,13},... | collective-permute-start | bytes 786440 | tf_op jit(solution)/shard_map/ppermute | solution.py:34
  58.5 3.9 %collective-permute-start.12 = (bf16[256,512]{1,0:T(8,128)(2,1)S(1)}, bf16[256,512]{1,0:T(8,128)(2,1)S(1)}, u32[]{:S(2)}, u32[]{:S(2)}) collective-permute-start(bf16[256,512]{1,0:T(8,128)(2,1)S(1)} %get-tuple-element.30), channel_id=1, source_target_pairs={{0,14},{1,9},{8,0},{9,3},{2,8},{3,11},{10,2},{11,5},{4,10},{5,13},... | collective-permute-start | bytes 786440 | tf_op jit(solution)/shard_map/ppermute | solution.py:34
  62.5 1.0 fusion
  63.5 3.1 %collective-permute-start.10 = (bf16[256,512]{1,0:T(8,128)(2,1)S(1)}, bf16[256,512]{1,0:T(8,128)(2,1)S(1)}, u32[]{:S(2)}, u32[]{:S(2)}) collective-permute-start(bf16[256,512]{1,0:T(8,128)(2,1)S(1)} %slice.137), channel_id=1, source_target_pairs={{0,14},{1,9},{8,0},{9,3},{2,8},{3,11},{10,2},{11,5},{4,10},{5,13},... | collective-permute-start | bytes 786440 | tf_op jit(solution)/shard_map/ppermute | solution.py:34
  67.0 4.4 %collective-permute-start.13 = (bf16[256,512]{1,0:T(8,128)(2,1)S(1)}, bf16[256,512]{1,0:T(8,128)(2,1)S(1)}, u32[]{:S(2)}, u32[]{:S(2)}) collective-permute-start(bf16[256,512]{1,0:T(8,128)(2,1)S(1)} %get-tuple-element.31), channel_id=1, source_target_pairs={{0,6},{1,3},{8,14},{9,11},{2,0},{3,5},{10,8},{11,13},{4,2},{5,7},{... | collective-permute-start | bytes 786440 | tf_op jit(solution)/shard_map/ppermute | solution.py:34
  71.4 3.2 %collective-permute-start.14 = (bf16[256,512]{1,0:T(8,128)(2,1)S(1)}, bf16[256,512]{1,0:T(8,128)(2,1)S(1)}, u32[]{:S(2)}, u32[]{:S(2)}) collective-permute-start(bf16[256,512]{1,0:T(8,128)(2,1)S(1)} %get-tuple-element.32), channel_id=1, source_target_pairs={{0,14},{1,9},{8,0},{9,3},{2,8},{3,11},{10,2},{11,5},{4,10},{5,13},... | collective-permute-start | bytes 786440 | tf_op jit(solution)/shard_map/ppermute | solution.py:34
  74.7 3.4 %collective-permute-done.13 = bf16[256,512]{1,0:T(8,128)(2,1)S(1)} collective-permute-done((bf16[256,512]{1,0:T(8,128)(2,1)S(1)}, bf16[256,512]{1,0:T(8,128)(2,1)S(1)}, u32[]{:S(2)}, u32[]{:S(2)}) %collective-permute-start.13) | collective-permute-done | bytes 262176 | tf_op jit(solution)/shard_map/ppermute | solution.py:34
  78.1 3.9 %collective-permute-done.14 = bf16[256,512]{1,0:T(8,128)(2,1)S(1)} collective-permute-done((bf16[256,512]{1,0:T(8,128)(2,1)S(1)}, bf16[256,512]{1,0:T(8,128)(2,1)S(1)}, u32[]{:S(2)}, u32[]{:S(2)}) %collective-permute-start.14) | collective-permute-done | bytes 262176 | tf_op jit(solution)/shard_map/ppermute | solution.py:34
  82.2 4.7 %collective-permute-start.15 = (bf16[256,512]{1,0:T(8,128)(2,1)S(1)}, bf16[256,512]{1,0:T(8,128)(2,1)S(1)}, u32[]{:S(2)}, u32[]{:S(2)}) collective-permute-start(bf16[256,512]{1,0:T(8,128)(2,1)S(1)} %get-tuple-element.33), channel_id=1, source_target_pairs={{0,14},{1,9},{8,0},{9,3},{2,8},{3,11},{10,2},{11,5},{4,10},{5,13},... | collective-permute-start | bytes 786440 | tf_op jit(solution)/shard_map/ppermute | solution.py:34
  86.9 1.9 %collective-permute-start.16 = (bf16[256,512]{1,0:T(8,128)(2,1)S(1)}, bf16[256,512]{1,0:T(8,128)(2,1)S(1)}, u32[]{:S(2)}, u32[]{:S(2)}) collective-permute-start(bf16[256,512]{1,0:T(8,128)(2,1)S(1)} %get-tuple-element.34), channel_id=1, source_target_pairs={{0,15},{1,8},{8,1},{9,2},{2,9},{3,10},{10,3},{11,4},{4,11},{5,12},... | collective-permute-start | bytes 786440 | tf_op jit(solution)/shard_map/ppermute | solution.py:34
  88.8 1.9 %collective-permute-done.15 = bf16[256,512]{1,0:T(8,128)(2,1)S(1)} collective-permute-done((bf16[256,512]{1,0:T(8,128)(2,1)S(1)}, bf16[256,512]{1,0:T(8,128)(2,1)S(1)}, u32[]{:S(2)}, u32[]{:S(2)}) %collective-permute-start.15) | collective-permute-done | bytes 262176 | tf_op jit(solution)/shard_map/ppermute | solution.py:34
  90.8 5.0 %collective-permute-done.16 = bf16[256,512]{1,0:T(8,128)(2,1)S(1)} collective-permute-done((bf16[256,512]{1,0:T(8,128)(2,1)S(1)}, bf16[256,512]{1,0:T(8,128)(2,1)S(1)}, u32[]{:S(2)}, u32[]{:S(2)}) %collective-permute-start.16) | collective-permute-done | bytes 262176 | tf_op jit(solution)/shard_map/ppermute | solution.py:34
  95.8 1.3 fusion.48
  97.1 26.4 %all_to_all.10.pieces_ref = bf16[32,8,512]{2,1,0:T(8,128)(2,1)S(1)} all-to-all(bf16[32,8,512]{2,1,0:T(8,128)(2,1)S(1)} %bitcast.56), channel_id=1, replica_groups=mesh['col'=32,'lo'=2,'hi'=4,'core'=2] {'col'}, dimensions={0} | all-to-all | bytes 524288 | tf_op jit(solution)/shard_map/all_to_all | solution.py:75
  123.5 1.3 turn.1
  124.7 5.3 %all-to-all-start.1 = ((bf16[32,8,512]{2,1,0:T(8,128)(2,1)}), bf16[32,8,512]{2,1,0:T(8,128)(2,1)S(1)}, u32[]{:S(2)}, u32[]{:S(2)}) async-start(bf16[32,8,512]{2,1,0:T(8,128)(2,1)} %turn.1), calls=%async_computation.1 | async-start | bytes 524288 | tf_op jit(solution)/shard_map/all_to_all | solution.py:96
  130.1 0.6 dynamic_slice.7
  132.6 8.5 %all-to-all-done.1 = bf16[32,8,512]{2,1,0:T(8,128)(2,1)S(1)} async-done(((bf16[32,8,512]{2,1,0:T(8,128)(2,1)}), bf16[32,8,512]{2,1,0:T(8,128)(2,1)S(1)}, u32[]{:S(2)}, u32[]{:S(2)}) %all-to-all-start.1) | async-done | bytes 262176 | tf_op jit(solution)/shard_map/all_to_all | solution.py:96
  141.2 0.9 fusion.21
  142.1 1.8 %fusion.25 = bf16[1,256,512]{2,1,0:T(8,128)(2,1)} fusion(f32[256,512]{1,0:T(8,128)S(1)} %get-tuple-element.37, bf16[32,256,512]{2,1,0:T(8,128)(2,1)} %all-gather.2.cloned.1.call-done, s32[]{:T(128)S(6)} %select_n.42, bf16[1,256,512]{2,1,0:T(8,128)(2,1)S(1)} %copy-done.2), kind=kLoop, calls=%fused_computation.42 | loop fusion | flops 786432 | bytes 1310724 | tf_op jit(solution)/shard_map/broadcast_in_dim | solution.py:185
  (29 shorter events, 1.1 us)
Async XLA Ops:
  7.2 134.9 %all-gather.2.cloned.1.call-start = ((), (), s32[]{:S(2)}) async-start(), calls=%async_computation.2 | async-start | bytes 8650752 | tf_op jit(solution)/shard_map/all_gather | solution.py:111
  7.9 29.7 %collective-permute-start.5 = (bf16[256,4096]{1,0:T(8,128)(2,1)}, bf16[256,4096]{1,0:T(8,128)(2,1)S(1)}, u32[]{:S(2)}, u32[]{:S(2)}) collective-permute-start(bf16[256,4096]{1,0:T(8,128)(2,1)} %bitcast.52), channel_id=1, source_target_pairs={{0,1},{1,0},{2,3},{3,2},{4,5},{5,4},{6,7},{7,6},{8,9},{9,8},{10,11... | collective-permute-start | bytes 6291464 | tf_op jit(solution)/shard_map/ppermute | solution.py:23
  9.8 11.1 %collective-permute-start.2 = (bf16[256,512]{1,0:T(8,128)(2,1)}, bf16[256,512]{1,0:T(8,128)(2,1)S(1)}, u32[]{:S(2)}, u32[]{:S(2)}) collective-permute-start(bf16[256,512]{1,0:T(8,128)(2,1)} %bitcast.54), channel_id=1, source_target_pairs={{0,15},{1,8},{8,1},{9,2},{2,9},{3,10},{10,3},{11,4},{4,11},{5,12},... | collective-permute-start | bytes 786440 | tf_op jit(solution)/shard_map/ppermute | solution.py:34
  15.3 9.7 %collective-permute-start = (bf16[256,512]{1,0:T(8,128)(2,1)}, bf16[256,512]{1,0:T(8,128)(2,1)S(1)}, u32[]{:S(2)}, u32[]{:S(2)}) collective-permute-start(bf16[256,512]{1,0:T(8,128)(2,1)} %bitcast.55), channel_id=1, source_target_pairs={{0,8},{1,15},{8,2},{9,1},{2,10},{3,9},{10,4},{11,3},{4,12},{5,11},... | collective-permute-start | bytes 786440 | tf_op jit(solution)/shard_map/ppermute | solution.py:34
  20.9 9.6 %collective-permute-start.3 = (bf16[256,512]{1,0:T(8,128)(2,1)S(1)}, bf16[256,512]{1,0:T(8,128)(2,1)}, u32[]{:S(2)}, u32[]{:S(2)}) collective-permute-start(bf16[256,512]{1,0:T(8,128)(2,1)S(1)} %collective-permute-done.2), channel_id=1, source_target_pairs={{0,8},{1,15},{8,2},{9,1},{2,10},{3,9},{10,4},{11,3},{4,12},{5,11},... | collective-permute-start | bytes 786440 | tf_op jit(solution)/shard_map/ppermute | solution.py:34
  25.0 15.0 %collective-permute-start.1 = (bf16[256,512]{1,0:T(8,128)(2,1)S(1)}, bf16[256,512]{1,0:T(8,128)(2,1)S(1)}, u32[]{:S(2)}, u32[]{:S(2)}) collective-permute-start(bf16[256,512]{1,0:T(8,128)(2,1)S(1)} %collective-permute-done), channel_id=1, source_target_pairs={{0,2},{1,7},{8,10},{9,15},{2,4},{3,1},{10,12},{11,9},{4,6},{5,3},{... | collective-permute-start | bytes 786440 | tf_op jit(solution)/shard_map/ppermute | solution.py:34
  30.5 9.5 %collective-permute-start.4 = (bf16[256,512]{1,0:T(8,128)(2,1)}, bf16[256,512]{1,0:T(8,128)(2,1)S(1)}, u32[]{:S(2)}, u32[]{:S(2)}) collective-permute-start(bf16[256,512]{1,0:T(8,128)(2,1)} %bitcast.57), channel_id=1, source_target_pairs={{0,1},{1,0},{2,3},{3,2},{4,5},{5,4},{6,7},{7,6},{8,9},{9,8},{10,11... | collective-permute-start | bytes 786440 | tf_op jit(solution)/shard_map/ppermute | solution.py:23
  33.1 12.9 %collective-permute-start.6 = (bf16[256,512]{1,0:T(8,128)(2,1)S(1)}, bf16[256,512]{1,0:T(8,128)(2,1)S(1)}, u32[]{:S(2)}, u32[]{:S(2)}) collective-permute-start(bf16[256,512]{1,0:T(8,128)(2,1)S(1)} %collective-permute-done), channel_id=1, source_target_pairs={{0,8},{1,15},{8,2},{9,1},{2,10},{3,9},{10,4},{11,3},{4,12},{5,11},... | collective-permute-start | bytes 786440 | tf_op jit(solution)/shard_map/ppermute | solution.py:34
  35.0 10.6 %collective-permute-start.7 = (bf16[256,512]{1,0:T(8,128)(2,1)}, bf16[256,512]{1,0:T(8,128)(2,1)S(1)}, u32[]{:S(2)}, u32[]{:S(2)}) collective-permute-start(bf16[256,512]{1,0:T(8,128)(2,1)} %collective-permute-done.3), channel_id=1, source_target_pairs={{0,8},{1,15},{8,2},{9,1},{2,10},{3,9},{10,4},{11,3},{4,12},{5,11},... | collective-permute-start | bytes 786440 | tf_op jit(solution)/shard_map/ppermute | solution.py:34
  37.6 1.6 %copy-start = (bf16[1,256,4096]{2,1,0:T(8,128)(2,1)S(1)}, bf16[1,256,4096]{2,1,0:T(8,128)(2,1)}, u32[]{:S(2)}) copy-start(bf16[1,256,4096]{2,1,0:T(8,128)(2,1)} %param.9) | copy-start | bytes 6291460
  39.2 4.6 %copy-start.2 = (bf16[1,256,512]{2,1,0:T(8,128)(2,1)S(1)}, bf16[1,256,512]{2,1,0:T(8,128)(2,1)}, u32[]{:S(2)}) copy-start(bf16[1,256,512]{2,1,0:T(8,128)(2,1)} %param.11) | copy-start | bytes 786436
  40.0 9.5 %collective-permute-start.8 = (bf16[256,512]{1,0:T(8,128)(2,1)S(1)}, bf16[256,512]{1,0:T(8,128)(2,1)S(1)}, u32[]{:S(2)}, u32[]{:S(2)}) collective-permute-start(bf16[256,512]{1,0:T(8,128)(2,1)S(1)} %collective-permute-done.1), channel_id=1, source_target_pairs={{0,8},{1,15},{8,2},{9,1},{2,10},{3,9},{10,4},{11,3},{4,12},{5,11},... | collective-permute-start | bytes 786440 | tf_op jit(solution)/shard_map/ppermute | solution.py:34
  50.2 4.1 %copy-start.3 = (bf16[1,256,512]{2,1,0:T(8,128)(2,1)S(1)}, bf16[1,256,512]{2,1,0:T(8,128)(2,1)}, u32[]{:S(2)}) copy-start(bf16[1,256,512]{2,1,0:T(8,128)(2,1)} %param.10) | copy-start | bytes 786436
  50.2 3.9 %collective-permute-start.9 = (bf16[512,512]{1,0:T(8,128)(2,1)S(1)}, bf16[512,512]{1,0:T(8,128)(2,1)S(1)}, u32[]{:S(2)}, u32[]{:S(2)}) collective-permute-start(bf16[512,512]{1,0:T(8,128)(2,1)S(1)} %get-tuple-element.56), channel_id=1, source_target_pairs={{0,1},{1,0},{2,3},{3,2},{4,5},{5,4},{6,7},{7,6},{8,9},{9,8},{10,11... | collective-permute-start | bytes 1572872 | tf_op jit(solution)/shard_map/ppermute | solution.py:23
  55.2 11.5 %collective-permute-start.11 = (bf16[256,512]{1,0:T(8,128)(2,1)S(1)}, bf16[256,512]{1,0:T(8,128)(2,1)S(1)}, u32[]{:S(2)}, u32[]{:S(2)}) collective-permute-start(bf16[256,512]{1,0:T(8,128)(2,1)S(1)} %get-tuple-element.29), channel_id=1, source_target_pairs={{0,14},{1,9},{8,0},{9,3},{2,8},{3,11},{10,2},{11,5},{4,10},{5,13},... | collective-permute-start | bytes 786440 | tf_op jit(solution)/shard_map/ppermute | solution.py:34
  58.5 8.3 %collective-permute-start.12 = (bf16[256,512]{1,0:T(8,128)(2,1)S(1)}, bf16[256,512]{1,0:T(8,128)(2,1)S(1)}, u32[]{:S(2)}, u32[]{:S(2)}) collective-permute-start(bf16[256,512]{1,0:T(8,128)(2,1)S(1)} %get-tuple-element.30), channel_id=1, source_target_pairs={{0,14},{1,9},{8,0},{9,3},{2,8},{3,11},{10,2},{11,5},{4,10},{5,13},... | collective-permute-start | bytes 786440 | tf_op jit(solution)/shard_map/ppermute | solution.py:34
  63.5 32.3 %copy-start.4 = (bf16[1,256,512]{2,1,0:T(8,128)(2,1)S(1)}, bf16[1,256,512]{2,1,0:T(8,128)(2,1)}, u32[]{:S(2)}) copy-start(bf16[1,256,512]{2,1,0:T(8,128)(2,1)} %param.13) | copy-start | bytes 786436
  63.5 32.3 %copy-start.5 = (bf16[1,256,512]{2,1,0:T(8,128)(2,1)S(1)}, bf16[1,256,512]{2,1,0:T(8,128)(2,1)}, u32[]{:S(2)}) copy-start(bf16[1,256,512]{2,1,0:T(8,128)(2,1)} %param.12) | copy-start | bytes 786436
  63.5 11.1 %collective-permute-start.10 = (bf16[256,512]{1,0:T(8,128)(2,1)S(1)}, bf16[256,512]{1,0:T(8,128)(2,1)S(1)}, u32[]{:S(2)}, u32[]{:S(2)}) collective-permute-start(bf16[256,512]{1,0:T(8,128)(2,1)S(1)} %slice.137), channel_id=1, source_target_pairs={{0,14},{1,9},{8,0},{9,3},{2,8},{3,11},{10,2},{11,5},{4,10},{5,13},... | collective-permute-start | bytes 786440 | tf_op jit(solution)/shard_map/ppermute | solution.py:34
  67.0 11.1 %collective-permute-start.13 = (bf16[256,512]{1,0:T(8,128)(2,1)S(1)}, bf16[256,512]{1,0:T(8,128)(2,1)S(1)}, u32[]{:S(2)}, u32[]{:S(2)}) collective-permute-start(bf16[256,512]{1,0:T(8,128)(2,1)S(1)} %get-tuple-element.31), channel_id=1, source_target_pairs={{0,6},{1,3},{8,14},{9,11},{2,0},{3,5},{10,8},{11,13},{4,2},{5,7},{... | collective-permute-start | bytes 786440 | tf_op jit(solution)/shard_map/ppermute | solution.py:34
  71.4 10.5 %collective-permute-start.14 = (bf16[256,512]{1,0:T(8,128)(2,1)S(1)}, bf16[256,512]{1,0:T(8,128)(2,1)S(1)}, u32[]{:S(2)}, u32[]{:S(2)}) collective-permute-start(bf16[256,512]{1,0:T(8,128)(2,1)S(1)} %get-tuple-element.32), channel_id=1, source_target_pairs={{0,14},{1,9},{8,0},{9,3},{2,8},{3,11},{10,2},{11,5},{4,10},{5,13},... | collective-permute-start | bytes 786440 | tf_op jit(solution)/shard_map/ppermute | solution.py:34
  82.2 41.3 %copy-start.1 = (s32[32]{0:T(128)S(1)}, s32[32]{0:T(128)}, u32[]{:S(2)}) copy-start(s32[32]{0:T(128)} %partner_ref.1) | copy-start | bytes 388
  82.2 59.0 %copy-start.6 = (bf16[1,256,512]{2,1,0:T(8,128)(2,1)S(1)}, bf16[1,256,512]{2,1,0:T(8,128)(2,1)}, u32[]{:S(2)}) copy-start(bf16[1,256,512]{2,1,0:T(8,128)(2,1)} %param.14) | copy-start | bytes 786436
  82.2 8.5 %collective-permute-start.15 = (bf16[256,512]{1,0:T(8,128)(2,1)S(1)}, bf16[256,512]{1,0:T(8,128)(2,1)S(1)}, u32[]{:S(2)}, u32[]{:S(2)}) collective-permute-start(bf16[256,512]{1,0:T(8,128)(2,1)S(1)} %get-tuple-element.33), channel_id=1, source_target_pairs={{0,14},{1,9},{8,0},{9,3},{2,8},{3,11},{10,2},{11,5},{4,10},{5,13},... | collective-permute-start | bytes 786440 | tf_op jit(solution)/shard_map/ppermute | solution.py:34
  86.9 8.9 %collective-permute-start.16 = (bf16[256,512]{1,0:T(8,128)(2,1)S(1)}, bf16[256,512]{1,0:T(8,128)(2,1)S(1)}, u32[]{:S(2)}, u32[]{:S(2)}) collective-permute-start(bf16[256,512]{1,0:T(8,128)(2,1)S(1)} %get-tuple-element.34), channel_id=1, source_target_pairs={{0,15},{1,8},{8,1},{9,2},{2,9},{3,10},{10,3},{11,4},{4,11},{5,12},... | collective-permute-start | bytes 786440 | tf_op jit(solution)/shard_map/ppermute | solution.py:34
  124.7 16.4 %all-to-all-start.1 = ((bf16[32,8,512]{2,1,0:T(8,128)(2,1)}), bf16[32,8,512]{2,1,0:T(8,128)(2,1)S(1)}, u32[]{:S(2)}, u32[]{:S(2)}) async-start(bf16[32,8,512]{2,1,0:T(8,128)(2,1)} %turn.1), calls=%async_computation.1 | async-start | bytes 524288 | tf_op jit(solution)/shard_map/all_to_all | solution.py:96
Sparse Core Ops, SparseCore 0:
  11.2 111.8 all-gather.1

commit v5 on v4

--- a/solution.py
+++ b/solution.py
@@ -112,8 +112,6 @@
     beside = swap_core(tokens[0])
     a1, b1 = hop(shard, ring, True), hop(shard, ring, True, cross=True)
     a3, b2, a2 = hop(a1, ring, True, chips=2), hop(b1, ring, True), hop(a1, ring, True)
-    b2, goals_own = lax.optimization_barrier((b2, targets[0]))
-    goals_beside = swap_core(goals_own)
 
     places = [(0, 0), (1, 0), (1, 1), (3, 0), (2, 1), (2, 0), (3, 1), (4, 0)]
     away = jnp.array([k for k, _ in places], jnp.int32)
@@ -122,8 +120,6 @@
     starts = ((source % 2 * half + source // 2) * 2 + (core + other) % 2) * rows
     inputs = arrange(tokens[0], beside, starts.astype(jnp.int32), rows)
 
-    a3, goals_beside, inputs = lax.optimization_barrier((a3, goals_beside, inputs))
-    goals = jnp.concatenate([targets[0], goals_beside], axis=0)
     blocks = [shard, a1, b1, a3, b2, a2, hop(b2, ring, True), hop(a3, ring, True)]
 
     part = None
@@ -132,10 +128,13 @@
         term = jnp.dot(columns, block, preferred_element_type=jnp.float32)
         part = term if part is None else part + term
     tokens_dev = part.shape[0] // 2
+    part = part * features ** (-0.5)
+    part = jnp.concatenate(
+        [part[:tokens_dev] - targets[0].astype(jnp.float32), part[tokens_dev:]], axis=0
+    )
     swapped = swap_core(part.astype(jnp.bfloat16)).astype(jnp.float32)
-    keys = part + jnp.concatenate([swapped[tokens_dev:], swapped[:tokens_dev]], axis=0)
-    keys = keys * features ** (-0.5)
-    residual = (keys - goals.astype(jnp.float32)).astype(jnp.bfloat16)
+    residual = part + jnp.concatenate([swapped[tokens_dev:], swapped[:tokens_dev]], axis=0)
+    residual = residual.astype(jnp.bfloat16)
 
     last = (ring - 2) * rows
     far_terms = contract_rows(inputs[:, last:], residual)
@@ -160,6 +159,10 @@
     four, three = both(term_of(3, 0) + four, term_of(2, 1) + three)
     four, three = send(four, chips=2), send(three)
     one, crossed = both(term_of(1, 0) + two + four, term_of(1, 1) + three)
+    facing = lax.dynamic_slice(
+        partner, (lax.axis_index("col"),), (1,), allow_negative_indices=False
+    )[0]
+    one, facing = lax.optimization_barrier((one, facing))
     from_one, crossed = send(one), send(crossed, cross=True)
     grad = (term_of(0, 0) + from_one + crossed) * norm_scale
 
@@ -175,14 +178,12 @@
     mean_delta = 0.5 * (delta + partner_delta.astype(jnp.float32))
     momentum = outer_momentum * outer_mom[0].astype(jnp.float32) + mean_delta
     moved = theta - outer_rate * (mean_delta + outer_momentum * momentum)
-    moved, new_mom, everyone = lax.optimization_barrier(
-        (moved, momentum.astype(jnp.bfloat16), everyone)
-    )
-    partner_anchor = lax.dynamic_index_in_dim(
-        everyone, partner[lax.axis_index("col")], 0, keepdims=False
-    )
+    partner_anchor = lax.dynamic_slice(
+        everyone, (facing, 0, 0), (1, *shard.shape), allow_negative_indices=False
+    )[0]
     moved = moved - pull_rate * 0.5 * (theta - partner_anchor.astype(jnp.float32))
-    return moved.astype(jnp.bfloat16)[None], new_m[None], new_v[None], new_mom[None]
+    moved, new_mom = moved.astype(jnp.bfloat16), momentum.astype(jnp.bfloat16)
+    return moved[None], new_m[None], new_v[None], new_mom[None]
 
 
 def solution(mesh):

time: 152 us -> 149 us (0.980)
  waiting for transfers between devices: 38.1 us -> 21.6 us
  blocking collectives: 26.4 us -> 42.4 us
  other arithmetic: 5.42 us -> 7.87 us
  between operations: 16.3 us -> 14.4 us
  starting transfers between devices: 55 us -> 53.1 us
    all_to_all x0 -> x1, blocking collectives: none -> 16.1 us  [deliver_pieces(): got = lax.all_to_all(turned, 'col', split_axis=0, concat_axis=0, tiled=True)]
    all_to_all x1 -> x0, waiting for transfers between devices: 8.52 us -> none  [deliver_pieces(): got = lax.all_to_all(turned, 'col', split_axis=0, concat_axis=0, tiled=True)]
    ppermute x14, waiting for transfers between devices: 27 us -> 19.1 us  [hop(): return lax.ppermute(value, REPLICA, pairs)]
    ppermute x14, starting transfers between devices: 43.8 us -> 49.2 us  [hop(): return lax.ppermute(value, REPLICA, pairs)]
    all_to_all x1 -> x0, starting transfers between devices: 5.34 us -> none  [deliver_pieces(): got = lax.all_to_all(turned, 'col', split_axis=0, concat_axis=0, tiled=True)]
    ppermute x3 -> x2, starting transfers between devices: 5.89 us -> 3.84 us  [swap_core(): return lax.ppermute(value, 'core', [(0, 1), (1, 0)])]
    convert_element_type x2, other arithmetic: 0.4 us -> 2.31 us  [both(): second.astype(jnp.bfloat16)]
  transfers between devices with their start and end apart: 19 -> 17, of which waited for: 11 -> 9; matrix products, arithmetic and copies ran while one was open for 6% -> 7% of each run, Pallas kernels for 1% -> 1%
where the time goes in v5:
time: 149 us; the launch traced here: 148 us
  starting transfers between devices  53.1 us (36%)
  blocking collectives  42.4 us (28%)
  waiting for transfers between devices  21.6 us (14%)
  between operations  14.4 us (10%)
  other arithmetic  7.87 us (5%)
  matrix products  3.95 us (3%)
  local copies, waits for them, and re-layouts  3.2 us (2%)
    ppermute x14, starting transfers between devices, hop(): return lax.ppermute(value, REPLICA, pairs)  49.2 us
    all_to_all x1, blocking collectives, scatter_pieces(): lax.all_to_all(pieces, 'col', split_axis=0, concat_axis=0, tiled=True)  26.3 us
    ppermute x14, waiting for transfers between devices, hop(): return lax.ppermute(value, REPLICA, pairs)  19.1 us
    all_to_all x1, blocking collectives, deliver_pieces(): got = lax.all_to_all(turned, 'col', split_axis=0, concat_axis=0, tiled=True)  16.1 us
    ppermute x2, starting transfers between devices, swap_core(): return lax.ppermute(value, 'core', [(0, 1), (1, 0)])  3.84 us
  transfers between devices with their start and end apart: 17, of which 9 were waited for; matrix products, arithmetic and copies ran while one was open for 7% of the time, Pallas kernels for 1%

profile of v5, /device:TPU:64, one launch (start us, length us, event | category | flops | bytes accessed | tf_op | source)
XLA Modules:
  0.0 147.9 jit_solution(13258196049941080977)
XLA Ops:
  7.2 0.7 all-gather.2.cloned.1.call-update
  7.9 1.9 %collective-permute-start = (bf16[256,4096]{1,0:T(8,128)(2,1)}, bf16[256,4096]{1,0:T(8,128)(2,1)S(1)}, u32[]{:S(2)}, u32[]{:S(2)}) collective-permute-start(bf16[256,4096]{1,0:T(8,128)(2,1)} %bitcast.62), channel_id=1, source_target_pairs={{0,1},{1,0},{2,3},{3,2},{4,5},{5,4},{6,7},{7,6},{8,9},{9,8},{10,11... | collective-permute-start | bytes 6291464 | tf_op jit(solution)/shard_map/ppermute | solution.py:23
  9.8 3.5 %collective-permute-start.1 = (bf16[256,512]{1,0:T(8,128)(2,1)}, bf16[256,512]{1,0:T(8,128)(2,1)S(1)}, u32[]{:S(2)}, u32[]{:S(2)}) collective-permute-start(bf16[256,512]{1,0:T(8,128)(2,1)} %bitcast.64), channel_id=1, source_target_pairs={{0,8},{1,15},{8,2},{9,1},{2,10},{3,9},{10,4},{11,3},{4,12},{5,11},... | collective-permute-start | bytes 786440 | tf_op jit(solution)/shard_map/ppermute | solution.py:34
  13.3 5.0 %collective-permute-start.2 = (bf16[256,512]{1,0:T(8,128)(2,1)}, bf16[256,512]{1,0:T(8,128)(2,1)S(1)}, u32[]{:S(2)}, u32[]{:S(2)}) collective-permute-start(bf16[256,512]{1,0:T(8,128)(2,1)} %bitcast.65), channel_id=1, source_target_pairs={{0,15},{1,8},{8,1},{9,2},{2,9},{3,10},{10,3},{11,4},{4,11},{5,12},... | collective-permute-start | bytes 786440 | tf_op jit(solution)/shard_map/ppermute | solution.py:34
  18.3 1.5 collective-permute-done.1
  19.8 3.0 %collective-permute-start.3 = (bf16[256,512]{1,0:T(8,128)(2,1)S(1)}, bf16[256,512]{1,0:T(8,128)(2,1)S(1)}, u32[]{:S(2)}, u32[]{:S(2)}) collective-permute-start(bf16[256,512]{1,0:T(8,128)(2,1)S(1)} %collective-permute-done.1), channel_id=1, source_target_pairs={{0,2},{1,7},{8,10},{9,15},{2,4},{3,1},{10,12},{11,9},{4,6},{5,3},{... | collective-permute-start | bytes 786440 | tf_op jit(solution)/shard_map/ppermute | solution.py:34
  22.8 4.6 %collective-permute-start.4 = (bf16[256,512]{1,0:T(8,128)(2,1)S(1)}, bf16[256,512]{1,0:T(8,128)(2,1)S(1)}, u32[]{:S(2)}, u32[]{:S(2)}) collective-permute-start(bf16[256,512]{1,0:T(8,128)(2,1)S(1)} %collective-permute-done.2), channel_id=1, source_target_pairs={{0,8},{1,15},{8,2},{9,1},{2,10},{3,9},{10,4},{11,3},{4,12},{5,11},... | collective-permute-start | bytes 786440 | tf_op jit(solution)/shard_map/ppermute | solution.py:34
  27.4 0.7 fusion.43.starts_ref
  28.1 5.5 %collective-permute-start.5 = (bf16[256,512]{1,0:T(8,128)(2,1)S(1)}, bf16[256,512]{1,0:T(8,128)(2,1)S(1)}, u32[]{:S(2)}, u32[]{:S(2)}) collective-permute-start(bf16[256,512]{1,0:T(8,128)(2,1)S(1)} %collective-permute-done.1), channel_id=1, source_target_pairs={{0,8},{1,15},{8,2},{9,1},{2,10},{3,9},{10,4},{11,3},{4,12},{5,11},... | collective-permute-start | bytes 786440 | tf_op jit(solution)/shard_map/ppermute | solution.py:34
  33.7 1.9 %collective-permute-start.7 = (bf16[256,512]{1,0:T(8,128)(2,1)S(1)}, bf16[256,512]{1,0:T(8,128)(2,1)S(1)}, u32[]{:S(2)}, u32[]{:S(2)}) collective-permute-start(bf16[256,512]{1,0:T(8,128)(2,1)S(1)} %collective-permute-done.3), channel_id=1, source_target_pairs={{0,8},{1,15},{8,2},{9,1},{2,10},{3,9},{10,4},{11,3},{4,12},{5,11},... | collective-permute-start | bytes 786440 | tf_op jit(solution)/shard_map/ppermute | solution.py:34
  35.6 2.6 %collective-permute-start.6 = (bf16[256,512]{1,0:T(8,128)(2,1)S(1)}, bf16[256,512]{1,0:T(8,128)(2,1)S(1)}, u32[]{:S(2)}, u32[]{:S(2)}) collective-permute-start(bf16[256,512]{1,0:T(8,128)(2,1)S(1)} %collective-permute-done.4), channel_id=1, source_target_pairs={{0,8},{1,15},{8,2},{9,1},{2,10},{3,9},{10,4},{11,3},{4,12},{5,11},... | collective-permute-start | bytes 786440 | tf_op jit(solution)/shard_map/ppermute | solution.py:34
  38.2 1.6 %copy-done = bf16[1,256,4096]{2,1,0:T(8,128)(2,1)S(1)} copy-done((bf16[1,256,4096]{2,1,0:T(8,128)(2,1)S(1)}, bf16[1,256,4096]{2,1,0:T(8,128)(2,1)}, u32[]{:S(2)}) %copy-start) | copy-done | bytes 2097176
  39.8 0.8 arrange.1
  40.7 0.3 fusion.36
  41.0 0.3 fusion.34
  41.3 0.3 fusion.31
  41.6 0.3 fusion.29
  41.9 0.3 fusion.4
  42.2 0.4 fusion.5
  42.6 0.5 collective-permute-done.7
  43.1 0.3 fusion.26
  43.5 2.5 %collective-permute-done.6 = bf16[256,512]{1,0:T(8,128)(2,1)S(1)} collective-permute-done((bf16[256,512]{1,0:T(8,128)(2,1)S(1)}, bf16[256,512]{1,0:T(8,128)(2,1)S(1)}, u32[]{:S(2)}, u32[]{:S(2)}) %collective-permute-start.6) | collective-permute-done | bytes 262176 | tf_op jit(solution)/shard_map/ppermute | solution.py:34
  45.9 0.3 fusion.6
  46.5 1.9 %collective-permute-start.8 = (bf16[512,512]{1,0:T(8,128)(2,1)S(1)}, bf16[512,512]{1,0:T(8,128)(2,1)S(1)}, u32[]{:S(2)}, u32[]{:S(2)}) collective-permute-start(bf16[512,512]{1,0:T(8,128)(2,1)S(1)} %fusion.8), channel_id=1, source_target_pairs={{0,1},{1,0},{2,3},{3,2},{4,5},{5,4},{6,7},{7,6},{8,9},{9,8},{10,11... | collective-permute-start | bytes 1572872 | tf_op jit(solution)/shard_map/ppermute | solution.py:23
  48.4 1.9 %collective-permute-done.8 = bf16[512,512]{1,0:T(8,128)(2,1)S(1)} collective-permute-done((bf16[512,512]{1,0:T(8,128)(2,1)S(1)}, bf16[512,512]{1,0:T(8,128)(2,1)S(1)}, u32[]{:S(2)}, u32[]{:S(2)}) %collective-permute-start.8) | collective-permute-done | bytes 524320 | tf_op jit(solution)/shard_map/ppermute | solution.py:23
  50.7 0.5 fusion.20
  51.2 3.1 %collective-permute-start.10 = (bf16[256,512]{1,0:T(8,128)(2,1)S(1)}, bf16[256,512]{1,0:T(8,128)(2,1)S(1)}, u32[]{:S(2)}, u32[]{:S(2)}) collective-permute-start(bf16[256,512]{1,0:T(8,128)(2,1)S(1)} %get-tuple-element.18), channel_id=1, source_target_pairs={{0,14},{1,9},{8,0},{9,3},{2,8},{3,11},{10,2},{11,5},{4,10},{5,13},... | collective-permute-start | bytes 786440 | tf_op jit(solution)/shard_map/ppermute | solution.py:34
  54.2 2.9 %collective-permute-start.11 = (bf16[256,512]{1,0:T(8,128)(2,1)S(1)}, bf16[256,512]{1,0:T(8,128)(2,1)S(1)}, u32[]{:S(2)}, u32[]{:S(2)}) collective-permute-start(bf16[256,512]{1,0:T(8,128)(2,1)S(1)} %get-tuple-element.19), channel_id=1, source_target_pairs={{0,14},{1,9},{8,0},{9,3},{2,8},{3,11},{10,2},{11,5},{4,10},{5,13},... | collective-permute-start | bytes 786440 | tf_op jit(solution)/shard_map/ppermute | solution.py:34
  57.2 1.0 fusion
  58.2 0.7 slice.158
  59.0 2.4 %collective-permute-start.9 = (bf16[256,512]{1,0:T(8,128)(2,1)}, bf16[256,512]{1,0:T(8,128)(2,1)}, u32[]{:S(2)}, u32[]{:S(2)}) collective-permute-start(bf16[256,512]{1,0:T(8,128)(2,1)} %slice.158), channel_id=1, source_target_pairs={{0,14},{1,9},{8,0},{9,3},{2,8},{3,11},{10,2},{11,5},{4,10},{5,13},... | collective-permute-start | bytes 786440 | tf_op jit(solution)/shard_map/ppermute | solution.py:34
  61.4 1.2 collective-permute-done.11
  62.5 1.0 fusion.15
  63.5 4.5 %collective-permute-start.12 = (bf16[256,512]{1,0:T(8,128)(2,1)}, bf16[256,512]{1,0:T(8,128)(2,1)}, u32[]{:S(2)}, u32[]{:S(2)}) collective-permute-start(bf16[256,512]{1,0:T(8,128)(2,1)} %get-tuple-element.20), channel_id=1, source_target_pairs={{0,6},{1,3},{8,14},{9,11},{2,0},{3,5},{10,8},{11,13},{4,2},{5,7},{... | collective-permute-start | bytes 786440 | tf_op jit(solution)/shard_map/ppermute | solution.py:34
  68.0 3.4 %collective-permute-start.13 = (bf16[256,512]{1,0:T(8,128)(2,1)}, bf16[256,512]{1,0:T(8,128)(2,1)}, u32[]{:S(2)}, u32[]{:S(2)}) collective-permute-start(bf16[256,512]{1,0:T(8,128)(2,1)} %get-tuple-element.21), channel_id=1, source_target_pairs={{0,14},{1,9},{8,0},{9,3},{2,8},{3,11},{10,2},{11,5},{4,10},{5,13},... | collective-permute-start | bytes 786440 | tf_op jit(solution)/shard_map/ppermute | solution.py:34
  71.5 0.7 dynamic_slice.6
  72.1 2.7 %collective-permute-done.12 = bf16[256,512]{1,0:T(8,128)(2,1)} collective-permute-done((bf16[256,512]{1,0:T(8,128)(2,1)}, bf16[256,512]{1,0:T(8,128)(2,1)}, u32[]{:S(2)}, u32[]{:S(2)}) %collective-permute-start.12) | collective-permute-done | bytes 262176 | tf_op jit(solution)/shard_map/ppermute | solution.py:34
  74.9 3.7 %collective-permute-done.13 = bf16[256,512]{1,0:T(8,128)(2,1)} collective-permute-done((bf16[256,512]{1,0:T(8,128)(2,1)}, bf16[256,512]{1,0:T(8,128)(2,1)}, u32[]{:S(2)}, u32[]{:S(2)}) %collective-permute-start.13) | collective-permute-done | bytes 262176 | tf_op jit(solution)/shard_map/ppermute | solution.py:34
  78.6 1.4 fusion.14
  80.0 4.8 %collective-permute-start.14 = (bf16[256,512]{1,0:T(8,128)(2,1)S(1)}, bf16[256,512]{1,0:T(8,128)(2,1)S(1)}, u32[]{:S(2)}, u32[]{:S(2)}) collective-permute-start(bf16[256,512]{1,0:T(8,128)(2,1)S(1)} %get-tuple-element.23), channel_id=1, source_target_pairs={{0,14},{1,9},{8,0},{9,3},{2,8},{3,11},{10,2},{11,5},{4,10},{5,13},... | collective-permute-start | bytes 786440 | tf_op jit(solution)/shard_map/ppermute | solution.py:34
  84.8 1.9 %collective-permute-start.15 = (bf16[256,512]{1,0:T(8,128)(2,1)S(1)}, bf16[256,512]{1,0:T(8,128)(2,1)S(1)}, u32[]{:S(2)}, u32[]{:S(2)}) collective-permute-start(bf16[256,512]{1,0:T(8,128)(2,1)S(1)} %get-tuple-element.24), channel_id=1, source_target_pairs={{0,15},{1,8},{8,1},{9,2},{2,9},{3,10},{10,3},{11,4},{4,11},{5,12},... | collective-permute-start | bytes 786440 | tf_op jit(solution)/shard_map/ppermute | solution.py:34
  86.7 1.9 %collective-permute-done.14 = bf16[256,512]{1,0:T(8,128)(2,1)S(1)} collective-permute-done((bf16[256,512]{1,0:T(8,128)(2,1)S(1)}, bf16[256,512]{1,0:T(8,128)(2,1)S(1)}, u32[]{:S(2)}, u32[]{:S(2)}) %collective-permute-start.14) | collective-permute-done | bytes 262176 | tf_op jit(solution)/shard_map/ppermute | solution.py:34
  88.7 5.0 %collective-permute-done.15 = bf16[256,512]{1,0:T(8,128)(2,1)S(1)} collective-permute-done((bf16[256,512]{1,0:T(8,128)(2,1)S(1)}, bf16[256,512]{1,0:T(8,128)(2,1)S(1)}, u32[]{:S(2)}, u32[]{:S(2)}) %collective-permute-start.15) | collective-permute-done | bytes 262176 | tf_op jit(solution)/shard_map/ppermute | solution.py:34
  93.7 1.5 fusion.49
  95.2 26.3 %all_to_all.10.pieces_ref = bf16[32,8,512]{2,1,0:T(8,128)(2,1)S(1)} all-to-all(bf16[32,8,512]{2,1,0:T(8,128)(2,1)S(1)} %bitcast.66), channel_id=1, replica_groups=mesh['col'=32,'lo'=2,'hi'=4,'core'=2] {'col'}, dimensions={0} | all-to-all | bytes 524288 | tf_op jit(solution)/shard_map/all_to_all | solution.py:75
  121.5 0.6 turn.1
  122.1 16.1 %all_to_all.11 = bf16[32,8,512]{2,1,0:T(8,128)(2,1)S(1)} all-to-all(bf16[32,8,512]{2,1,0:T(8,128)(2,1)S(1)} %turn.1), channel_id=1, replica_groups=mesh['col'=32,'lo'=2,'hi'=4,'core'=2] {'col'}, dimensions={0} | all-to-all | bytes 524288 | tf_op jit(solution)/shard_map/all_to_all | solution.py:96
  138.1 2.9 %fusion.25 = (bf16[1,256,512]{2,1,0:T(8,128)(2,1)}, bf16[1,256,512]{2,1,0:T(8,128)(2,1)}) fusion(f32[256,512]{1,0:T(8,128)} %get-tuple-element.25, bf16[1,256,512]{2,1,0:T(8,128)(2,1)} %param.14, bf16[32,8,512]{2,1,0:T(8,128)(2,1)S(1)} %all_to_all.11, bf16[32,256,512]{2,1,0:T(8,128)(2,1)} %all-gather.2.cloned.1.call-done, s32[]{:T(128)} %bitcast.4, ...), kind=kLoop, calls=%fused_computation.44 | loop fusion | flops 2228224 | bytes 2097156 | tf_op jit(solution)/shard_map/broadcast_in_dim | solution.py:186
  (25 shorter events, 0.7 us)
Async XLA Ops:
  7.2 130.9 %all-gather.2.cloned.1.call-start = ((), (), s32[]{:S(2)}) async-start(), calls=%async_computation.2 | async-start | bytes 8650752 | tf_op jit(solution)/shard_map/all_gather | solution.py:111
  7.9 30.3 %collective-permute-start = (bf16[256,4096]{1,0:T(8,128)(2,1)}, bf16[256,4096]{1,0:T(8,128)(2,1)S(1)}, u32[]{:S(2)}, u32[]{:S(2)}) collective-permute-start(bf16[256,4096]{1,0:T(8,128)(2,1)} %bitcast.62), channel_id=1, source_target_pairs={{0,1},{1,0},{2,3},{3,2},{4,5},{5,4},{6,7},{7,6},{8,9},{9,8},{10,11... | collective-permute-start | bytes 6291464 | tf_op jit(solution)/shard_map/ppermute | solution.py:23
  9.8 9.9 %collective-permute-start.1 = (bf16[256,512]{1,0:T(8,128)(2,1)}, bf16[256,512]{1,0:T(8,128)(2,1)S(1)}, u32[]{:S(2)}, u32[]{:S(2)}) collective-permute-start(bf16[256,512]{1,0:T(8,128)(2,1)} %bitcast.64), channel_id=1, source_target_pairs={{0,8},{1,15},{8,2},{9,1},{2,10},{3,9},{10,4},{11,3},{4,12},{5,11},... | collective-permute-start | bytes 786440 | tf_op jit(solution)/shard_map/ppermute | solution.py:34
  13.3 9.5 %collective-permute-start.2 = (bf16[256,512]{1,0:T(8,128)(2,1)}, bf16[256,512]{1,0:T(8,128)(2,1)S(1)}, u32[]{:S(2)}, u32[]{:S(2)}) collective-permute-start(bf16[256,512]{1,0:T(8,128)(2,1)} %bitcast.65), channel_id=1, source_target_pairs={{0,15},{1,8},{8,1},{9,2},{2,9},{3,10},{10,3},{11,4},{4,11},{5,12},... | collective-permute-start | bytes 786440 | tf_op jit(solution)/shard_map/ppermute | solution.py:34
  19.8 13.9 %collective-permute-start.3 = (bf16[256,512]{1,0:T(8,128)(2,1)S(1)}, bf16[256,512]{1,0:T(8,128)(2,1)S(1)}, u32[]{:S(2)}, u32[]{:S(2)}) collective-permute-start(bf16[256,512]{1,0:T(8,128)(2,1)S(1)} %collective-permute-done.1), channel_id=1, source_target_pairs={{0,2},{1,7},{8,10},{9,15},{2,4},{3,1},{10,12},{11,9},{4,6},{5,3},{... | collective-permute-start | bytes 786440 | tf_op jit(solution)/shard_map/ppermute | solution.py:34
  22.8 12.8 %collective-permute-start.4 = (bf16[256,512]{1,0:T(8,128)(2,1)S(1)}, bf16[256,512]{1,0:T(8,128)(2,1)S(1)}, u32[]{:S(2)}, u32[]{:S(2)}) collective-permute-start(bf16[256,512]{1,0:T(8,128)(2,1)S(1)} %collective-permute-done.2), channel_id=1, source_target_pairs={{0,8},{1,15},{8,2},{9,1},{2,10},{3,9},{10,4},{11,3},{4,12},{5,11},... | collective-permute-start | bytes 786440 | tf_op jit(solution)/shard_map/ppermute | solution.py:34
  28.1 13.4 %collective-permute-start.5 = (bf16[256,512]{1,0:T(8,128)(2,1)S(1)}, bf16[256,512]{1,0:T(8,128)(2,1)S(1)}, u32[]{:S(2)}, u32[]{:S(2)}) collective-permute-start(bf16[256,512]{1,0:T(8,128)(2,1)S(1)} %collective-permute-done.1), channel_id=1, source_target_pairs={{0,8},{1,15},{8,2},{9,1},{2,10},{3,9},{10,4},{11,3},{4,12},{5,11},... | collective-permute-start | bytes 786440 | tf_op jit(solution)/shard_map/ppermute | solution.py:34
  33.7 9.5 %collective-permute-start.7 = (bf16[256,512]{1,0:T(8,128)(2,1)S(1)}, bf16[256,512]{1,0:T(8,128)(2,1)S(1)}, u32[]{:S(2)}, u32[]{:S(2)}) collective-permute-start(bf16[256,512]{1,0:T(8,128)(2,1)S(1)} %collective-permute-done.3), channel_id=1, source_target_pairs={{0,8},{1,15},{8,2},{9,1},{2,10},{3,9},{10,4},{11,3},{4,12},{5,11},... | collective-permute-start | bytes 786440 | tf_op jit(solution)/shard_map/ppermute | solution.py:34
  35.6 10.3 %collective-permute-start.6 = (bf16[256,512]{1,0:T(8,128)(2,1)S(1)}, bf16[256,512]{1,0:T(8,128)(2,1)S(1)}, u32[]{:S(2)}, u32[]{:S(2)}) collective-permute-start(bf16[256,512]{1,0:T(8,128)(2,1)S(1)} %collective-permute-done.4), channel_id=1, source_target_pairs={{0,8},{1,15},{8,2},{9,1},{2,10},{3,9},{10,4},{11,3},{4,12},{5,11},... | collective-permute-start | bytes 786440 | tf_op jit(solution)/shard_map/ppermute | solution.py:34
  38.2 1.6 %copy-start = (bf16[1,256,4096]{2,1,0:T(8,128)(2,1)S(1)}, bf16[1,256,4096]{2,1,0:T(8,128)(2,1)}, u32[]{:S(2)}) copy-start(bf16[1,256,4096]{2,1,0:T(8,128)(2,1)} %param.9) | copy-start | bytes 6291460
  41.0 1.0 copy-start.2
  43.4 2.8 %copy-start.3 = (bf16[1,256,512]{2,1,0:T(8,128)(2,1)S(1)}, bf16[1,256,512]{2,1,0:T(8,128)(2,1)}, u32[]{:S(2)}) copy-start(bf16[1,256,512]{2,1,0:T(8,128)(2,1)} %param.10) | copy-start | bytes 786436
  46.5 3.8 %collective-permute-start.8 = (bf16[512,512]{1,0:T(8,128)(2,1)S(1)}, bf16[512,512]{1,0:T(8,128)(2,1)S(1)}, u32[]{:S(2)}, u32[]{:S(2)}) collective-permute-start(bf16[512,512]{1,0:T(8,128)(2,1)S(1)} %fusion.8), channel_id=1, source_target_pairs={{0,1},{1,0},{2,3},{3,2},{4,5},{5,4},{6,7},{7,6},{8,9},{9,8},{10,11... | collective-permute-start | bytes 1572872 | tf_op jit(solution)/shard_map/ppermute | solution.py:23
  51.2 10.2 %collective-permute-start.10 = (bf16[256,512]{1,0:T(8,128)(2,1)S(1)}, bf16[256,512]{1,0:T(8,128)(2,1)S(1)}, u32[]{:S(2)}, u32[]{:S(2)}) collective-permute-start(bf16[256,512]{1,0:T(8,128)(2,1)S(1)} %get-tuple-element.18), channel_id=1, source_target_pairs={{0,14},{1,9},{8,0},{9,3},{2,8},{3,11},{10,2},{11,5},{4,10},{5,13},... | collective-permute-start | bytes 786440 | tf_op jit(solution)/shard_map/ppermute | solution.py:34
  54.2 8.3 %collective-permute-start.11 = (bf16[256,512]{1,0:T(8,128)(2,1)S(1)}, bf16[256,512]{1,0:T(8,128)(2,1)S(1)}, u32[]{:S(2)}, u32[]{:S(2)}) collective-permute-start(bf16[256,512]{1,0:T(8,128)(2,1)S(1)} %get-tuple-element.19), channel_id=1, source_target_pairs={{0,14},{1,9},{8,0},{9,3},{2,8},{3,11},{10,2},{11,5},{4,10},{5,13},... | collective-permute-start | bytes 786440 | tf_op jit(solution)/shard_map/ppermute | solution.py:34
  58.2 13.2 %copy-start.1 = (s32[32]{0:T(128)S(1)}, s32[32]{0:T(128)}, u32[]{:S(2)}) copy-start(s32[32]{0:T(128)} %partner_ref.1) | copy-start | bytes 388
  59.0 13.2 %collective-permute-start.9 = (bf16[256,512]{1,0:T(8,128)(2,1)}, bf16[256,512]{1,0:T(8,128)(2,1)}, u32[]{:S(2)}, u32[]{:S(2)}) collective-permute-start(bf16[256,512]{1,0:T(8,128)(2,1)} %slice.158), channel_id=1, source_target_pairs={{0,14},{1,9},{8,0},{9,3},{2,8},{3,11},{10,2},{11,5},{4,10},{5,13},... | collective-permute-start | bytes 786440 | tf_op jit(solution)/shard_map/ppermute | solution.py:34
  63.5 11.4 %collective-permute-start.12 = (bf16[256,512]{1,0:T(8,128)(2,1)}, bf16[256,512]{1,0:T(8,128)(2,1)}, u32[]{:S(2)}, u32[]{:S(2)}) collective-permute-start(bf16[256,512]{1,0:T(8,128)(2,1)} %get-tuple-element.20), channel_id=1, source_target_pairs={{0,6},{1,3},{8,14},{9,11},{2,0},{3,5},{10,8},{11,13},{4,2},{5,7},{... | collective-permute-start | bytes 786440 | tf_op jit(solution)/shard_map/ppermute | solution.py:34
  68.0 10.6 %collective-permute-start.13 = (bf16[256,512]{1,0:T(8,128)(2,1)}, bf16[256,512]{1,0:T(8,128)(2,1)}, u32[]{:S(2)}, u32[]{:S(2)}) collective-permute-start(bf16[256,512]{1,0:T(8,128)(2,1)} %get-tuple-element.21), channel_id=1, source_target_pairs={{0,14},{1,9},{8,0},{9,3},{2,8},{3,11},{10,2},{11,5},{4,10},{5,13},... | collective-permute-start | bytes 786440 | tf_op jit(solution)/shard_map/ppermute | solution.py:34
  71.4 22.2 %copy-start.4 = (bf16[1,256,512]{2,1,0:T(8,128)(2,1)S(1)}, bf16[1,256,512]{2,1,0:T(8,128)(2,1)}, u32[]{:S(2)}) copy-start(bf16[1,256,512]{2,1,0:T(8,128)(2,1)} %param.13) | copy-start | bytes 786436
  71.5 22.2 %copy-start.5 = (bf16[1,256,512]{2,1,0:T(8,128)(2,1)S(1)}, bf16[1,256,512]{2,1,0:T(8,128)(2,1)}, u32[]{:S(2)}) copy-start(bf16[1,256,512]{2,1,0:T(8,128)(2,1)} %param.12) | copy-start | bytes 786436
  80.0 8.7 %collective-permute-start.14 = (bf16[256,512]{1,0:T(8,128)(2,1)S(1)}, bf16[256,512]{1,0:T(8,128)(2,1)S(1)}, u32[]{:S(2)}, u32[]{:S(2)}) collective-permute-start(bf16[256,512]{1,0:T(8,128)(2,1)S(1)} %get-tuple-element.23), channel_id=1, source_target_pairs={{0,14},{1,9},{8,0},{9,3},{2,8},{3,11},{10,2},{11,5},{4,10},{5,13},... | collective-permute-start | bytes 786440 | tf_op jit(solution)/shard_map/ppermute | solution.py:34
  84.8 8.9 %collective-permute-start.15 = (bf16[256,512]{1,0:T(8,128)(2,1)S(1)}, bf16[256,512]{1,0:T(8,128)(2,1)S(1)}, u32[]{:S(2)}, u32[]{:S(2)}) collective-permute-start(bf16[256,512]{1,0:T(8,128)(2,1)S(1)} %get-tuple-element.24), channel_id=1, source_target_pairs={{0,15},{1,8},{8,1},{9,2},{2,9},{3,10},{10,3},{11,4},{4,11},{5,12},... | collective-permute-start | bytes 786440 | tf_op jit(solution)/shard_map/ppermute | solution.py:34
Sparse Core Ops, SparseCore 0:
  11.2 112.0 all-gather.1

commit v6 on v5

--- a/solution.py
+++ b/solution.py
@@ -111,6 +111,10 @@
     everyone = lax.all_gather(shard, "col")
     beside = swap_core(tokens[0])
     a1, b1 = hop(shard, ring, True), hop(shard, ring, True, cross=True)
+    facing = lax.dynamic_slice(
+        partner, (lax.axis_index("col"),), (1,), allow_negative_indices=False
+    )[0]
+    b1, facing = lax.optimization_barrier((b1, facing))
     a3, b2, a2 = hop(a1, ring, True, chips=2), hop(b1, ring, True), hop(a1, ring, True)
 
     places = [(0, 0), (1, 0), (1, 1), (3, 0), (2, 1), (2, 0), (3, 1), (4, 0)]
@@ -136,7 +140,7 @@
     residual = part + jnp.concatenate([swapped[tokens_dev:], swapped[:tokens_dev]], axis=0)
     residual = residual.astype(jnp.bfloat16)
 
-    last = (ring - 2) * rows
+    last = (ring - 3) * rows
     far_terms = contract_rows(inputs[:, last:], residual)
     near_terms = contract_rows(
         inputs[:, :last], lax.optimization_barrier((residual, far_terms))[0]
@@ -150,19 +154,15 @@
     def send(value, **way):
         return hop(value, ring, False, **way).astype(jnp.float32)
 
-    def both(first, second):
-        return lax.optimization_barrier((first.astype(jnp.bfloat16), second.astype(jnp.bfloat16)))
-
-    four, three = both(term_of(4, 0), term_of(3, 1))
+    def ready(*sums):
+        return lax.optimization_barrier(tuple(part.astype(jnp.bfloat16) for part in sums))
+
+    four, three, two = ready(term_of(4, 0), term_of(3, 1), term_of(2, 0))
     four, three = send(four), send(three)
-    two = send(term_of(2, 0).astype(jnp.bfloat16))
-    four, three = both(term_of(3, 0) + four, term_of(2, 1) + three)
+    two = send(two)
+    four, three = ready(term_of(3, 0) + four, term_of(2, 1) + three)
     four, three = send(four, chips=2), send(three)
-    one, crossed = both(term_of(1, 0) + two + four, term_of(1, 1) + three)
-    facing = lax.dynamic_slice(
-        partner, (lax.axis_index("col"),), (1,), allow_negative_indices=False
-    )[0]
-    one, facing = lax.optimization_barrier((one, facing))
+    one, crossed = ready(term_of(1, 0) + two + four, term_of(1, 1) + three)
     from_one, crossed = send(one), send(crossed, cross=True)
     grad = (term_of(0, 0) + from_one + crossed) * norm_scale
 

time: 149 us -> 148 us (level)
  waiting for transfers between devices: 21.6 us -> 31.1 us
  starting transfers between devices: 53.1 us -> 44.4 us
  other arithmetic: 7.87 us -> 5.51 us
    ppermute x14, waiting for transfers between devices: 19.1 us -> 28.6 us  [hop(): return lax.ppermute(value, REPLICA, pairs)]
    ppermute x14, starting transfers between devices: 49.2 us -> 40.5 us  [hop(): return lax.ppermute(value, REPLICA, pairs)]
    convert_element_type x2, other arithmetic: 2.31 us -> 0.43 us  [ready(): part.astype(jnp.bfloat16)]
  transfers between devices with their start and end apart: 17 -> 17, of which waited for: 9 -> 11; matrix products, arithmetic and copies ran while one was open for 7% -> 6% of each run, Pallas kernels for 1% -> 1%
where the time goes in v6:
time: 148 us; the launch traced here: 147 us
  starting transfers between devices  44.4 us (30%)
  blocking collectives  42.9 us (29%)
  waiting for transfers between devices  31.1 us (21%)
  between operations  14.4 us (10%)
  other arithmetic  5.51 us (4%)
  matrix products  3.88 us (3%)
  local copies, waits for them, and re-layouts  3.12 us (2%)
    ppermute x14, starting transfers between devices, hop(): return lax.ppermute(value, REPLICA, pairs)  40.5 us
    ppermute x14, waiting for transfers between devices, hop(): return lax.ppermute(value, REPLICA, pairs)  28.6 us
    all_to_all x1, blocking collectives, scatter_pieces(): lax.all_to_all(pieces, 'col', split_axis=0, concat_axis=0, tiled=True)  26.8 us
    all_to_all x1, blocking collectives, deliver_pieces(): got = lax.all_to_all(turned, 'col', split_axis=0, concat_axis=0, tiled=True)  16.1 us
    ppermute x2, starting transfers between devices, swap_core(): return lax.ppermute(value, 'core', [(0, 1), (1, 0)])  3.84 us
  transfers between devices with their start and end apart: 17, of which 11 were waited for; matrix products, arithmetic and copies ran while one was open for 6% of the time, Pallas kernels for 1%

profile of v6, /device:TPU:64, one launch (start us, length us, event | category | flops | bytes accessed | tf_op | source)
XLA Modules:
  0.0 146.8 jit_solution(15298197240379325255)
XLA Ops:
  7.2 0.7 all-gather.2.cloned.1.call-update
  7.9 1.9 %collective-permute-start = (bf16[256,4096]{1,0:T(8,128)(2,1)}, bf16[256,4096]{1,0:T(8,128)(2,1)S(1)}, u32[]{:S(2)}, u32[]{:S(2)}) collective-permute-start(bf16[256,4096]{1,0:T(8,128)(2,1)} %bitcast.62), channel_id=1, source_target_pairs={{0,1},{1,0},{2,3},{3,2},{4,5},{5,4},{6,7},{7,6},{8,9},{9,8},{10,11... | collective-permute-start | bytes 6291464 | tf_op jit(solution)/shard_map/ppermute | solution.py:23
  9.8 5.5 %collective-permute-start.2 = (bf16[256,512]{1,0:T(8,128)(2,1)}, bf16[256,512]{1,0:T(8,128)(2,1)S(1)}, u32[]{:S(2)}, u32[]{:S(2)}) collective-permute-start(bf16[256,512]{1,0:T(8,128)(2,1)} %bitcast.64), channel_id=1, source_target_pairs={{0,15},{1,8},{8,1},{9,2},{2,9},{3,10},{10,3},{11,4},{4,11},{5,12},... | collective-permute-start | bytes 786440 | tf_op jit(solution)/shard_map/ppermute | solution.py:34
  15.3 1.9 %collective-permute-start.1 = (bf16[256,512]{1,0:T(8,128)(2,1)}, bf16[256,512]{1,0:T(8,128)(2,1)S(1)}, u32[]{:S(2)}, u32[]{:S(2)}) collective-permute-start(bf16[256,512]{1,0:T(8,128)(2,1)} %bitcast.65), channel_id=1, source_target_pairs={{0,8},{1,15},{8,2},{9,1},{2,10},{3,9},{10,4},{11,3},{4,12},{5,11},... | collective-permute-start | bytes 786440 | tf_op jit(solution)/shard_map/ppermute | solution.py:34
  17.3 1.3 dynamic_slice.6
  18.5 2.4 %collective-permute-done.2 = bf16[256,512]{1,0:T(8,128)(2,1)S(1)} collective-permute-done((bf16[256,512]{1,0:T(8,128)(2,1)}, bf16[256,512]{1,0:T(8,128)(2,1)S(1)}, u32[]{:S(2)}, u32[]{:S(2)}) %collective-permute-start.2) | collective-permute-done | bytes 262176 | tf_op jit(solution)/shard_map/ppermute | solution.py:34
  20.9 1.9 %collective-permute-start.4 = (bf16[256,512]{1,0:T(8,128)(2,1)S(1)}, bf16[256,512]{1,0:T(8,128)(2,1)S(1)}, u32[]{:S(2)}, u32[]{:S(2)}) collective-permute-start(bf16[256,512]{1,0:T(8,128)(2,1)S(1)} %collective-permute-done.2), channel_id=1, source_target_pairs={{0,8},{1,15},{8,2},{9,1},{2,10},{3,9},{10,4},{11,3},{4,12},{5,11},... | collective-permute-start | bytes 786440 | tf_op jit(solution)/shard_map/ppermute | solution.py:34
  22.8 2.2 %collective-permute-done.1 = bf16[256,512]{1,0:T(8,128)(2,1)S(1)} collective-permute-done((bf16[256,512]{1,0:T(8,128)(2,1)}, bf16[256,512]{1,0:T(8,128)(2,1)S(1)}, u32[]{:S(2)}, u32[]{:S(2)}) %collective-permute-start.1) | collective-permute-done | bytes 262176 | tf_op jit(solution)/shard_map/ppermute | solution.py:34
  25.0 1.9 %collective-permute-start.3 = (bf16[256,512]{1,0:T(8,128)(2,1)S(1)}, bf16[256,512]{1,0:T(8,128)(2,1)S(1)}, u32[]{:S(2)}, u32[]{:S(2)}) collective-permute-start(bf16[256,512]{1,0:T(8,128)(2,1)S(1)} %collective-permute-done.1), channel_id=1, source_target_pairs={{0,2},{1,7},{8,10},{9,15},{2,4},{3,1},{10,12},{11,9},{4,6},{5,3},{... | collective-permute-start | bytes 786440 | tf_op jit(solution)/shard_map/ppermute | solution.py:34
  26.9 0.7 fusion.41.starts_ref
  27.6 4.7 %collective-permute-start.5 = (bf16[256,512]{1,0:T(8,128)(2,1)S(1)}, bf16[256,512]{1,0:T(8,128)(2,1)S(1)}, u32[]{:S(2)}, u32[]{:S(2)}) collective-permute-start(bf16[256,512]{1,0:T(8,128)(2,1)S(1)} %collective-permute-done.1), channel_id=1, source_target_pairs={{0,8},{1,15},{8,2},{9,1},{2,10},{3,9},{10,4},{11,3},{4,12},{5,11},... | collective-permute-start | bytes 786440 | tf_op jit(solution)/shard_map/ppermute | solution.py:34
  32.4 3.0 %collective-permute-start.6 = (bf16[256,512]{1,0:T(8,128)(2,1)S(1)}, bf16[256,512]{1,0:T(8,128)(2,1)S(1)}, u32[]{:S(2)}, u32[]{:S(2)}) collective-permute-start(bf16[256,512]{1,0:T(8,128)(2,1)S(1)} %collective-permute-done.4), channel_id=1, source_target_pairs={{0,8},{1,15},{8,2},{9,1},{2,10},{3,9},{10,4},{11,3},{4,12},{5,11},... | collective-permute-start | bytes 786440 | tf_op jit(solution)/shard_map/ppermute | solution.py:34
  35.4 2.8 %collective-permute-done.3 = bf16[256,512]{1,0:T(8,128)(2,1)S(1)} collective-permute-done((bf16[256,512]{1,0:T(8,128)(2,1)S(1)}, bf16[256,512]{1,0:T(8,128)(2,1)S(1)}, u32[]{:S(2)}, u32[]{:S(2)}) %collective-permute-start.3) | collective-permute-done | bytes 262176 | tf_op jit(solution)/shard_map/ppermute | solution.py:34
  38.2 1.9 %collective-permute-start.7 = (bf16[256,512]{1,0:T(8,128)(2,1)S(1)}, bf16[256,512]{1,0:T(8,128)(2,1)S(1)}, u32[]{:S(2)}, u32[]{:S(2)}) collective-permute-start(bf16[256,512]{1,0:T(8,128)(2,1)S(1)} %collective-permute-done.3), channel_id=1, source_target_pairs={{0,8},{1,15},{8,2},{9,1},{2,10},{3,9},{10,4},{11,3},{4,12},{5,11},... | collective-permute-start | bytes 786440 | tf_op jit(solution)/shard_map/ppermute | solution.py:34
  40.2 1.6 %copy-done = bf16[1,256,4096]{2,1,0:T(8,128)(2,1)S(1)} copy-done((bf16[1,256,4096]{2,1,0:T(8,128)(2,1)S(1)}, bf16[1,256,4096]{2,1,0:T(8,128)(2,1)}, u32[]{:S(2)}) %copy-start) | copy-done | bytes 2097176
  41.8 0.8 arrange.1
  42.6 0.3 fusion.32
  42.9 0.3 fusion.34
  43.2 0.3 fusion.29
  43.6 0.3 fusion.3
  43.9 0.3 fusion.2
  44.2 0.3 fusion.26
  44.5 0.3 fusion.1
  44.8 2.9 %collective-permute-done.7 = bf16[256,512]{1,0:T(8,128)(2,1)S(1)} collective-permute-done((bf16[256,512]{1,0:T(8,128)(2,1)S(1)}, bf16[256,512]{1,0:T(8,128)(2,1)S(1)}, u32[]{:S(2)}, u32[]{:S(2)}) %collective-permute-start.7) | collective-permute-done | bytes 262176 | tf_op jit(solution)/shard_map/ppermute | solution.py:34
  47.7 0.3 fusion
  48.2 1.9 %collective-permute-start.8 = (bf16[512,512]{1,0:T(8,128)(2,1)S(1)}, bf16[512,512]{1,0:T(8,128)(2,1)S(1)}, u32[]{:S(2)}, u32[]{:S(2)}) collective-permute-start(bf16[512,512]{1,0:T(8,128)(2,1)S(1)} %fusion.7), channel_id=1, source_target_pairs={{0,1},{1,0},{2,3},{3,2},{4,5},{5,4},{6,7},{7,6},{8,9},{9,8},{10,11... | collective-permute-start | bytes 1572872 | tf_op jit(solution)/shard_map/ppermute | solution.py:23
  50.1 1.9 %collective-permute-done.8 = bf16[512,512]{1,0:T(8,128)(2,1)S(1)} collective-permute-done((bf16[512,512]{1,0:T(8,128)(2,1)S(1)}, bf16[512,512]{1,0:T(8,128)(2,1)S(1)}, u32[]{:S(2)}, u32[]{:S(2)}) %collective-permute-start.8) | collective-permute-done | bytes 524320 | tf_op jit(solution)/shard_map/ppermute | solution.py:23
  52.1 0.3 fusion.6
  52.4 0.6 fusion.8
  53.1 2.9 %collective-permute-start.10 = (bf16[256,512]{1,0:T(8,128)(2,1)S(1)}, bf16[256,512]{1,0:T(8,128)(2,1)S(1)}, u32[]{:S(2)}, u32[]{:S(2)}) collective-permute-start(bf16[256,512]{1,0:T(8,128)(2,1)S(1)} %get-tuple-element.21), channel_id=1, source_target_pairs={{0,14},{1,9},{8,0},{9,3},{2,8},{3,11},{10,2},{11,5},{4,10},{5,13},... | collective-permute-start | bytes 786440 | tf_op jit(solution)/shard_map/ppermute | solution.py:34
  56.0 1.9 %collective-permute-start.11 = (bf16[256,512]{1,0:T(8,128)(2,1)S(1)}, bf16[256,512]{1,0:T(8,128)(2,1)S(1)}, u32[]{:S(2)}, u32[]{:S(2)}) collective-permute-start(bf16[256,512]{1,0:T(8,128)(2,1)S(1)} %get-tuple-element.22), channel_id=1, source_target_pairs={{0,14},{1,9},{8,0},{9,3},{2,8},{3,11},{10,2},{11,5},{4,10},{5,13},... | collective-permute-start | bytes 786440 | tf_op jit(solution)/shard_map/ppermute | solution.py:34
  57.9 2.2 %collective-permute-start.9 = (bf16[256,512]{1,0:T(8,128)(2,1)S(1)}, bf16[256,512]{1,0:T(8,128)(2,1)S(1)}, u32[]{:S(2)}, u32[]{:S(2)}) collective-permute-start(bf16[256,512]{1,0:T(8,128)(2,1)S(1)} %get-tuple-element.20), channel_id=1, source_target_pairs={{0,14},{1,9},{8,0},{9,3},{2,8},{3,11},{10,2},{11,5},{4,10},{5,13},... | collective-permute-start | bytes 786440 | tf_op jit(solution)/shard_map/ppermute | solution.py:34
  60.1 0.9 fusion.4
  61.0 0.3 collective-permute-done.10
  61.3 2.9 %collective-permute-done.11 = bf16[256,512]{1,0:T(8,128)(2,1)S(1)} collective-permute-done((bf16[256,512]{1,0:T(8,128)(2,1)S(1)}, bf16[256,512]{1,0:T(8,128)(2,1)S(1)}, u32[]{:S(2)}, u32[]{:S(2)}) %collective-permute-start.11) | collective-permute-done | bytes 262176 | tf_op jit(solution)/shard_map/ppermute | solution.py:34
  64.4 2.4 %collective-permute-start.12 = (bf16[256,512]{1,0:T(8,128)(2,1)S(1)}, bf16[256,512]{1,0:T(8,128)(2,1)S(1)}, u32[]{:S(2)}, u32[]{:S(2)}) collective-permute-start(bf16[256,512]{1,0:T(8,128)(2,1)S(1)} %get-tuple-element.23), channel_id=1, source_target_pairs={{0,6},{1,3},{8,14},{9,11},{2,0},{3,5},{10,8},{11,13},{4,2},{5,7},{... | collective-permute-start | bytes 786440 | tf_op jit(solution)/shard_map/ppermute | solution.py:34
  66.8 4.4 %collective-permute-start.13 = (bf16[256,512]{1,0:T(8,128)(2,1)S(1)}, bf16[256,512]{1,0:T(8,128)(2,1)S(1)}, u32[]{:S(2)}, u32[]{:S(2)}) collective-permute-start(bf16[256,512]{1,0:T(8,128)(2,1)S(1)} %get-tuple-element.24), channel_id=1, source_target_pairs={{0,14},{1,9},{8,0},{9,3},{2,8},{3,11},{10,2},{11,5},{4,10},{5,13},... | collective-permute-start | bytes 786440 | tf_op jit(solution)/shard_map/ppermute | solution.py:34
  71.2 2.8 %collective-permute-done.12 = bf16[256,512]{1,0:T(8,128)(2,1)S(1)} collective-permute-done((bf16[256,512]{1,0:T(8,128)(2,1)S(1)}, bf16[256,512]{1,0:T(8,128)(2,1)S(1)}, u32[]{:S(2)}, u32[]{:S(2)}) %collective-permute-start.12) | collective-permute-done | bytes 262176 | tf_op jit(solution)/shard_map/ppermute | solution.py:34
  74.0 5.3 %collective-permute-done.13 = bf16[256,512]{1,0:T(8,128)(2,1)S(1)} collective-permute-done((bf16[256,512]{1,0:T(8,128)(2,1)S(1)}, bf16[256,512]{1,0:T(8,128)(2,1)S(1)}, u32[]{:S(2)}, u32[]{:S(2)}) %collective-permute-start.13) | collective-permute-done | bytes 262176 | tf_op jit(solution)/shard_map/ppermute | solution.py:34
  79.6 4.0 %collective-permute-start.14 = (bf16[256,512]{1,0:T(8,128)(2,1)S(1)}, bf16[256,512]{1,0:T(8,128)(2,1)S(1)}, u32[]{:S(2)}, u32[]{:S(2)}) collective-permute-start(bf16[256,512]{1,0:T(8,128)(2,1)S(1)} %get-tuple-element.25), channel_id=1, source_target_pairs={{0,14},{1,9},{8,0},{9,3},{2,8},{3,11},{10,2},{11,5},{4,10},{5,13},... | collective-permute-start | bytes 786440 | tf_op jit(solution)/shard_map/ppermute | solution.py:34
  83.6 1.9 %collective-permute-start.15 = (bf16[256,512]{1,0:T(8,128)(2,1)S(1)}, bf16[256,512]{1,0:T(8,128)(2,1)S(1)}, u32[]{:S(2)}, u32[]{:S(2)}) collective-permute-start(bf16[256,512]{1,0:T(8,128)(2,1)S(1)} %get-tuple-element.26), channel_id=1, source_target_pairs={{0,15},{1,8},{8,1},{9,2},{2,9},{3,10},{10,3},{11,4},{4,11},{5,12},... | collective-permute-start | bytes 786440 | tf_op jit(solution)/shard_map/ppermute | solution.py:34
  85.5 2.5 %collective-permute-done.14 = bf16[256,512]{1,0:T(8,128)(2,1)S(1)} collective-permute-done((bf16[256,512]{1,0:T(8,128)(2,1)S(1)}, bf16[256,512]{1,0:T(8,128)(2,1)S(1)}, u32[]{:S(2)}, u32[]{:S(2)}) %collective-permute-start.14) | collective-permute-done | bytes 262176 | tf_op jit(solution)/shard_map/ppermute | solution.py:34
  88.0 4.5 %collective-permute-done.15 = bf16[256,512]{1,0:T(8,128)(2,1)S(1)} collective-permute-done((bf16[256,512]{1,0:T(8,128)(2,1)S(1)}, bf16[256,512]{1,0:T(8,128)(2,1)S(1)}, u32[]{:S(2)}, u32[]{:S(2)}) %collective-permute-start.15) | collective-permute-done | bytes 262176 | tf_op jit(solution)/shard_map/ppermute | solution.py:34
  92.5 1.3 fusion.47
  93.8 26.8 %all_to_all.10.pieces_ref = bf16[32,8,512]{2,1,0:T(8,128)(2,1)S(1)} all-to-all(bf16[32,8,512]{2,1,0:T(8,128)(2,1)S(1)} %bitcast.66), channel_id=1, replica_groups=mesh['col'=32,'lo'=2,'hi'=4,'core'=2] {'col'}, dimensions={0} | all-to-all | bytes 524288 | tf_op jit(solution)/shard_map/all_to_all | solution.py:75
  120.6 0.6 turn.1
  121.2 16.1 %all_to_all.11 = bf16[32,8,512]{2,1,0:T(8,128)(2,1)S(1)} all-to-all(bf16[32,8,512]{2,1,0:T(8,128)(2,1)S(1)} %turn.1), channel_id=1, replica_groups=mesh['col'=32,'lo'=2,'hi'=4,'core'=2] {'col'}, dimensions={0} | all-to-all | bytes 524288 | tf_op jit(solution)/shard_map/all_to_all | solution.py:96
  137.3 2.6 %fusion.24 = (bf16[1,256,512]{2,1,0:T(8,128)(2,1)}, bf16[1,256,512]{2,1,0:T(8,128)(2,1)}) fusion(f32[256,512]{1,0:T(8,128)S(1)} %get-tuple-element.27, bf16[1,256,512]{2,1,0:T(8,128)(2,1)S(1)} %copy-done.6, bf16[32,8,512]{2,1,0:T(8,128)(2,1)S(1)} %all_to_all.11, bf16[32,256,512]{2,1,0:T(8,128)(2,1)} %all-gather.2.cloned.1.call-done, s32[]{:T(128)} %bitcast.3, ...), kind=kLoop, calls=%fused_computation.43 | loop fusion | flops 2228224 | bytes 2097156 | tf_op jit(solution)/shard_map/broadcast_in_dim | solution.py:186
  (26 shorter events, 0.9 us)
Async XLA Ops:
  7.2 130.1 %all-gather.2.cloned.1.call-start = ((), (), s32[]{:S(2)}) async-start(), calls=%async_computation.2 | async-start | bytes 8650752 | tf_op jit(solution)/shard_map/all_gather | solution.py:111
  7.9 32.3 %collective-permute-start = (bf16[256,4096]{1,0:T(8,128)(2,1)}, bf16[256,4096]{1,0:T(8,128)(2,1)S(1)}, u32[]{:S(2)}, u32[]{:S(2)}) collective-permute-start(bf16[256,4096]{1,0:T(8,128)(2,1)} %bitcast.62), channel_id=1, source_target_pairs={{0,1},{1,0},{2,3},{3,2},{4,5},{5,4},{6,7},{7,6},{8,9},{9,8},{10,11... | collective-permute-start | bytes 6291464 | tf_op jit(solution)/shard_map/ppermute | solution.py:23
  9.8 11.1 %collective-permute-start.2 = (bf16[256,512]{1,0:T(8,128)(2,1)}, bf16[256,512]{1,0:T(8,128)(2,1)S(1)}, u32[]{:S(2)}, u32[]{:S(2)}) collective-permute-start(bf16[256,512]{1,0:T(8,128)(2,1)} %bitcast.64), channel_id=1, source_target_pairs={{0,15},{1,8},{8,1},{9,2},{2,9},{3,10},{10,3},{11,4},{4,11},{5,12},... | collective-permute-start | bytes 786440 | tf_op jit(solution)/shard_map/ppermute | solution.py:34
  15.3 9.7 %collective-permute-start.1 = (bf16[256,512]{1,0:T(8,128)(2,1)}, bf16[256,512]{1,0:T(8,128)(2,1)S(1)}, u32[]{:S(2)}, u32[]{:S(2)}) collective-permute-start(bf16[256,512]{1,0:T(8,128)(2,1)} %bitcast.65), channel_id=1, source_target_pairs={{0,8},{1,15},{8,2},{9,1},{2,10},{3,9},{10,4},{11,3},{4,12},{5,11},... | collective-permute-start | bytes 786440 | tf_op jit(solution)/shard_map/ppermute | solution.py:34
  20.9 11.5 %collective-permute-start.4 = (bf16[256,512]{1,0:T(8,128)(2,1)S(1)}, bf16[256,512]{1,0:T(8,128)(2,1)S(1)}, u32[]{:S(2)}, u32[]{:S(2)}) collective-permute-start(bf16[256,512]{1,0:T(8,128)(2,1)S(1)} %collective-permute-done.2), channel_id=1, source_target_pairs={{0,8},{1,15},{8,2},{9,1},{2,10},{3,9},{10,4},{11,3},{4,12},{5,11},... | collective-permute-start | bytes 786440 | tf_op jit(solution)/shard_map/ppermute | solution.py:34
  25.0 13.2 %collective-permute-start.3 = (bf16[256,512]{1,0:T(8,128)(2,1)S(1)}, bf16[256,512]{1,0:T(8,128)(2,1)S(1)}, u32[]{:S(2)}, u32[]{:S(2)}) collective-permute-start(bf16[256,512]{1,0:T(8,128)(2,1)S(1)} %collective-permute-done.1), channel_id=1, source_target_pairs={{0,2},{1,7},{8,10},{9,15},{2,4},{3,1},{10,12},{11,9},{4,6},{5,3},{... | collective-permute-start | bytes 786440 | tf_op jit(solution)/shard_map/ppermute | solution.py:34
  27.6 16.8 %collective-permute-start.5 = (bf16[256,512]{1,0:T(8,128)(2,1)S(1)}, bf16[256,512]{1,0:T(8,128)(2,1)S(1)}, u32[]{:S(2)}, u32[]{:S(2)}) collective-permute-start(bf16[256,512]{1,0:T(8,128)(2,1)S(1)} %collective-permute-done.1), channel_id=1, source_target_pairs={{0,8},{1,15},{8,2},{9,1},{2,10},{3,9},{10,4},{11,3},{4,12},{5,11},... | collective-permute-start | bytes 786440 | tf_op jit(solution)/shard_map/ppermute | solution.py:34
  32.4 11.8 %collective-permute-start.6 = (bf16[256,512]{1,0:T(8,128)(2,1)S(1)}, bf16[256,512]{1,0:T(8,128)(2,1)S(1)}, u32[]{:S(2)}, u32[]{:S(2)}) collective-permute-start(bf16[256,512]{1,0:T(8,128)(2,1)S(1)} %collective-permute-done.4), channel_id=1, source_target_pairs={{0,8},{1,15},{8,2},{9,1},{2,10},{3,9},{10,4},{11,3},{4,12},{5,11},... | collective-permute-start | bytes 786440 | tf_op jit(solution)/shard_map/ppermute | solution.py:34
  38.2 9.5 %collective-permute-start.7 = (bf16[256,512]{1,0:T(8,128)(2,1)S(1)}, bf16[256,512]{1,0:T(8,128)(2,1)S(1)}, u32[]{:S(2)}, u32[]{:S(2)}) collective-permute-start(bf16[256,512]{1,0:T(8,128)(2,1)S(1)} %collective-permute-done.3), channel_id=1, source_target_pairs={{0,8},{1,15},{8,2},{9,1},{2,10},{3,9},{10,4},{11,3},{4,12},{5,11},... | collective-permute-start | bytes 786440 | tf_op jit(solution)/shard_map/ppermute | solution.py:34
  40.2 1.6 %copy-start = (bf16[1,256,4096]{2,1,0:T(8,128)(2,1)S(1)}, bf16[1,256,4096]{2,1,0:T(8,128)(2,1)}, u32[]{:S(2)}) copy-start(bf16[1,256,4096]{2,1,0:T(8,128)(2,1)} %param.9) | copy-start | bytes 6291460
  42.6 1.0 copy-start.2
  44.8 3.2 %copy-start.3 = (bf16[1,256,512]{2,1,0:T(8,128)(2,1)S(1)}, bf16[1,256,512]{2,1,0:T(8,128)(2,1)}, u32[]{:S(2)}) copy-start(bf16[1,256,512]{2,1,0:T(8,128)(2,1)} %param.10) | copy-start | bytes 786436
  48.2 3.8 %collective-permute-start.8 = (bf16[512,512]{1,0:T(8,128)(2,1)S(1)}, bf16[512,512]{1,0:T(8,128)(2,1)S(1)}, u32[]{:S(2)}, u32[]{:S(2)}) collective-permute-start(bf16[512,512]{1,0:T(8,128)(2,1)S(1)} %fusion.7), channel_id=1, source_target_pairs={{0,1},{1,0},{2,3},{3,2},{4,5},{5,4},{6,7},{7,6},{8,9},{9,8},{10,11... | collective-permute-start | bytes 1572872 | tf_op jit(solution)/shard_map/ppermute | solution.py:23
  53.1 8.3 %collective-permute-start.10 = (bf16[256,512]{1,0:T(8,128)(2,1)S(1)}, bf16[256,512]{1,0:T(8,128)(2,1)S(1)}, u32[]{:S(2)}, u32[]{:S(2)}) collective-permute-start(bf16[256,512]{1,0:T(8,128)(2,1)S(1)} %get-tuple-element.21), channel_id=1, source_target_pairs={{0,14},{1,9},{8,0},{9,3},{2,8},{3,11},{10,2},{11,5},{4,10},{5,13},... | collective-permute-start | bytes 786440 | tf_op jit(solution)/shard_map/ppermute | solution.py:34
  56.0 8.3 %collective-permute-start.11 = (bf16[256,512]{1,0:T(8,128)(2,1)S(1)}, bf16[256,512]{1,0:T(8,128)(2,1)S(1)}, u32[]{:S(2)}, u32[]{:S(2)}) collective-permute-start(bf16[256,512]{1,0:T(8,128)(2,1)S(1)} %get-tuple-element.22), channel_id=1, source_target_pairs={{0,14},{1,9},{8,0},{9,3},{2,8},{3,11},{10,2},{11,5},{4,10},{5,13},... | collective-permute-start | bytes 786440 | tf_op jit(solution)/shard_map/ppermute | solution.py:34
  57.9 13.3 %collective-permute-start.9 = (bf16[256,512]{1,0:T(8,128)(2,1)S(1)}, bf16[256,512]{1,0:T(8,128)(2,1)S(1)}, u32[]{:S(2)}, u32[]{:S(2)}) collective-permute-start(bf16[256,512]{1,0:T(8,128)(2,1)S(1)} %get-tuple-element.20), channel_id=1, source_target_pairs={{0,14},{1,9},{8,0},{9,3},{2,8},{3,11},{10,2},{11,5},{4,10},{5,13},... | collective-permute-start | bytes 786440 | tf_op jit(solution)/shard_map/ppermute | solution.py:34
  61.0 31.5 %copy-start.4 = (bf16[1,256,512]{2,1,0:T(8,128)(2,1)S(1)}, bf16[1,256,512]{2,1,0:T(8,128)(2,1)}, u32[]{:S(2)}) copy-start(bf16[1,256,512]{2,1,0:T(8,128)(2,1)} %param.13) | copy-start | bytes 786436
  61.0 31.5 %copy-start.5 = (bf16[1,256,512]{2,1,0:T(8,128)(2,1)S(1)}, bf16[1,256,512]{2,1,0:T(8,128)(2,1)}, u32[]{:S(2)}) copy-start(bf16[1,256,512]{2,1,0:T(8,128)(2,1)} %param.12) | copy-start | bytes 786436
  64.4 9.6 %collective-permute-start.12 = (bf16[256,512]{1,0:T(8,128)(2,1)S(1)}, bf16[256,512]{1,0:T(8,128)(2,1)S(1)}, u32[]{:S(2)}, u32[]{:S(2)}) collective-permute-start(bf16[256,512]{1,0:T(8,128)(2,1)S(1)} %get-tuple-element.23), channel_id=1, source_target_pairs={{0,6},{1,3},{8,14},{9,11},{2,0},{3,5},{10,8},{11,13},{4,2},{5,7},{... | collective-permute-start | bytes 786440 | tf_op jit(solution)/shard_map/ppermute | solution.py:34
  66.8 12.5 %collective-permute-start.13 = (bf16[256,512]{1,0:T(8,128)(2,1)S(1)}, bf16[256,512]{1,0:T(8,128)(2,1)S(1)}, u32[]{:S(2)}, u32[]{:S(2)}) collective-permute-start(bf16[256,512]{1,0:T(8,128)(2,1)S(1)} %get-tuple-element.24), channel_id=1, source_target_pairs={{0,14},{1,9},{8,0},{9,3},{2,8},{3,11},{10,2},{11,5},{4,10},{5,13},... | collective-permute-start | bytes 786440 | tf_op jit(solution)/shard_map/ppermute | solution.py:34
  79.6 41.0 %copy-start.1 = (s32[32]{0:T(128)S(1)}, s32[32]{0:T(128)}, u32[]{:S(2)}) copy-start(s32[32]{0:T(128)} %partner_ref.1) | copy-start | bytes 388
  79.6 57.7 %copy-start.6 = (bf16[1,256,512]{2,1,0:T(8,128)(2,1)S(1)}, bf16[1,256,512]{2,1,0:T(8,128)(2,1)}, u32[]{:S(2)}) copy-start(bf16[1,256,512]{2,1,0:T(8,128)(2,1)} %param.14) | copy-start | bytes 786436
  79.6 8.4 %collective-permute-start.14 = (bf16[256,512]{1,0:T(8,128)(2,1)S(1)}, bf16[256,512]{1,0:T(8,128)(2,1)S(1)}, u32[]{:S(2)}, u32[]{:S(2)}) collective-permute-start(bf16[256,512]{1,0:T(8,128)(2,1)S(1)} %get-tuple-element.25), channel_id=1, source_target_pairs={{0,14},{1,9},{8,0},{9,3},{2,8},{3,11},{10,2},{11,5},{4,10},{5,13},... | collective-permute-start | bytes 786440 | tf_op jit(solution)/shard_map/ppermute | solution.py:34
  83.6 8.9 %collective-permute-start.15 = (bf16[256,512]{1,0:T(8,128)(2,1)S(1)}, bf16[256,512]{1,0:T(8,128)(2,1)S(1)}, u32[]{:S(2)}, u32[]{:S(2)}) collective-permute-start(bf16[256,512]{1,0:T(8,128)(2,1)S(1)} %get-tuple-element.26), channel_id=1, source_target_pairs={{0,15},{1,8},{8,1},{9,2},{2,9},{3,10},{10,3},{11,4},{4,11},{5,12},... | collective-permute-start | bytes 786440 | tf_op jit(solution)/shard_map/ppermute | solution.py:34
Sparse Core Ops, SparseCore 0:
  11.2 112.2 all-gather.1

commit v7 on v6

--- a/solution.py
+++ b/solution.py
@@ -181,6 +181,7 @@
     partner_anchor = lax.dynamic_slice(
         everyone, (facing, 0, 0), (1, *shard.shape), allow_negative_indices=False
     )[0]
+    partner_anchor = lax.optimization_barrier(partner_anchor)
     moved = moved - pull_rate * 0.5 * (theta - partner_anchor.astype(jnp.float32))
     moved, new_mom = moved.astype(jnp.bfloat16), momentum.astype(jnp.bfloat16)
     return moved[None], new_m[None], new_v[None], new_mom[None]

time: 148 us -> 150 us (1.014)
  blocking collectives: 42.9 us -> 26.6 us
  waiting for transfers between devices: 31.1 us -> 43.3 us
  starting transfers between devices: 44.4 us -> 50.2 us
  local copies, waits for them, and re-layouts: 3.12 us -> 4.69 us
  other arithmetic: 5.51 us -> 3.94 us
    all_to_all x1 -> x0, blocking collectives: 16.1 us -> none  [deliver_pieces(): got = lax.all_to_all(turned, 'col', split_axis=0, concat_axis=0, tiled=True)]
    all_to_all x0 -> x1, waiting for transfers between devices: none -> 9.4 us  [deliver_pieces(): got = lax.all_to_all(turned, 'col', split_axis=0, concat_axis=0, tiled=True)]
    all_to_all x0 -> x1, starting transfers between devices: none -> 5.26 us  [deliver_pieces(): got = lax.all_to_all(turned, 'col', split_axis=0, concat_axis=0, tiled=True)]
    ppermute x14, waiting for transfers between devices: 28.6 us -> 31.3 us  [hop(): return lax.ppermute(value, REPLICA, pairs)]
    squeeze x0 -> x1, local copies, waits for them, and re-layouts: none -> 1.62 us  [shards(): lax.dynamic_slice(everyone, (facing, 0, 0), (1, *shard.shape), allow_nega...]
    broadcast_in_dim x1, other arithmetic: 2.64 us -> 1.07 us  [shards(): return (moved[None], new_m[None], new_v[None], new_mom[None])]
  transfers between devices with their start and end apart: 17 -> 18, of which waited for: 11 -> 12; matrix products, arithmetic and copies ran while one was open for 6% -> 7% of each run, Pallas kernels for 1% -> 1%
where the time goes in v7:
time: 150 us; the launch traced here: 149 us
  starting transfers between devices  50.2 us (33%)
  waiting for transfers between devices  43.3 us (29%)
  blocking collectives  26.6 us (18%)
  between operations  14.4 us (10%)
  local copies, waits for them, and re-layouts  4.69 us (3%)
  other arithmetic  3.94 us (3%)
  matrix products  3.88 us (3%)
  Pallas kernels  2.11 us (1%)
    ppermute x14, starting transfers between devices, hop(): return lax.ppermute(value, REPLICA, pairs)  41 us
    ppermute x14, waiting for transfers between devices, hop(): return lax.ppermute(value, REPLICA, pairs)  31.3 us
    all_to_all x1, blocking collectives, scatter_pieces(): lax.all_to_all(pieces, 'col', split_axis=0, concat_axis=0, tiled=True)  26.6 us
    all_to_all x1, waiting for transfers between devices, deliver_pieces(): got = lax.all_to_all(turned, 'col', split_axis=0, concat_axis=0, tiled=True)  9.4 us
    all_to_all x1, starting transfers between devices, deliver_pieces(): got = lax.all_to_all(turned, 'col', split_axis=0, concat_axis=0, tiled=True)  5.26 us
    ppermute x2, starting transfers between devices, swap_core(): return lax.ppermute(value, 'core', [(0, 1), (1, 0)])  3.84 us
  transfers between devices with their start and end apart: 18, of which 12 were waited for; matrix products, arithmetic and copies ran while one was open for 7% of the time, Pallas kernels for 1%

profile of v7, /device:TPU:64, one launch (start us, length us, event | category | flops | bytes accessed | tf_op | source)
XLA Modules:
  0.0 149.0 jit_solution(8327244262793892136)
XLA Ops:
  7.2 0.7 all-gather.2.cloned.1.call-update
  7.9 1.9 %collective-permute-start = (bf16[256,4096]{1,0:T(8,128)(2,1)}, bf16[256,4096]{1,0:T(8,128)(2,1)S(1)}, u32[]{:S(2)}, u32[]{:S(2)}) collective-permute-start(bf16[256,4096]{1,0:T(8,128)(2,1)} %bitcast.59), channel_id=1, source_target_pairs={{0,1},{1,0},{2,3},{3,2},{4,5},{5,4},{6,7},{7,6},{8,9},{9,8},{10,11... | collective-permute-start | bytes 6291464 | tf_op jit(solution)/shard_map/ppermute | solution.py:23
  9.8 5.5 %collective-permute-start.2 = (bf16[256,512]{1,0:T(8,128)(2,1)}, bf16[256,512]{1,0:T(8,128)(2,1)S(1)}, u32[]{:S(2)}, u32[]{:S(2)}) collective-permute-start(bf16[256,512]{1,0:T(8,128)(2,1)} %bitcast.61), channel_id=1, source_target_pairs={{0,15},{1,8},{8,1},{9,2},{2,9},{3,10},{10,3},{11,4},{4,11},{5,12},... | collective-permute-start | bytes 786440 | tf_op jit(solution)/shard_map/ppermute | solution.py:34
  15.3 1.9 %collective-permute-start.1 = (bf16[256,512]{1,0:T(8,128)(2,1)}, bf16[256,512]{1,0:T(8,128)(2,1)S(1)}, u32[]{:S(2)}, u32[]{:S(2)}) collective-permute-start(bf16[256,512]{1,0:T(8,128)(2,1)} %bitcast.62), channel_id=1, source_target_pairs={{0,8},{1,15},{8,2},{9,1},{2,10},{3,9},{10,4},{11,3},{4,12},{5,11},... | collective-permute-start | bytes 786440 | tf_op jit(solution)/shard_map/ppermute | solution.py:34
  17.3 1.2 dynamic_slice.6
  18.5 2.4 %collective-permute-done.2 = bf16[256,512]{1,0:T(8,128)(2,1)S(1)} collective-permute-done((bf16[256,512]{1,0:T(8,128)(2,1)}, bf16[256,512]{1,0:T(8,128)(2,1)S(1)}, u32[]{:S(2)}, u32[]{:S(2)}) %collective-permute-start.2) | collective-permute-done | bytes 262176 | tf_op jit(solution)/shard_map/ppermute | solution.py:34
  20.9 1.9 %collective-permute-start.4 = (bf16[256,512]{1,0:T(8,128)(2,1)S(1)}, bf16[256,512]{1,0:T(8,128)(2,1)S(1)}, u32[]{:S(2)}, u32[]{:S(2)}) collective-permute-start(bf16[256,512]{1,0:T(8,128)(2,1)S(1)} %collective-permute-done.2), channel_id=1, source_target_pairs={{0,8},{1,15},{8,2},{9,1},{2,10},{3,9},{10,4},{11,3},{4,12},{5,11},... | collective-permute-start | bytes 786440 | tf_op jit(solution)/shard_map/ppermute | solution.py:34
  22.8 2.2 %collective-permute-done.1 = bf16[256,512]{1,0:T(8,128)(2,1)S(1)} collective-permute-done((bf16[256,512]{1,0:T(8,128)(2,1)}, bf16[256,512]{1,0:T(8,128)(2,1)S(1)}, u32[]{:S(2)}, u32[]{:S(2)}) %collective-permute-start.1) | collective-permute-done | bytes 262176 | tf_op jit(solution)/shard_map/ppermute | solution.py:34
  25.0 1.9 %collective-permute-start.3 = (bf16[256,512]{1,0:T(8,128)(2,1)S(1)}, bf16[256,512]{1,0:T(8,128)(2,1)S(1)}, u32[]{:S(2)}, u32[]{:S(2)}) collective-permute-start(bf16[256,512]{1,0:T(8,128)(2,1)S(1)} %collective-permute-done.1), channel_id=1, source_target_pairs={{0,2},{1,7},{8,10},{9,15},{2,4},{3,1},{10,12},{11,9},{4,6},{5,3},{... | collective-permute-start | bytes 786440 | tf_op jit(solution)/shard_map/ppermute | solution.py:34
  26.9 0.7 fusion.41.starts_ref
  27.6 4.7 %collective-permute-start.5 = (bf16[256,512]{1,0:T(8,128)(2,1)S(1)}, bf16[256,512]{1,0:T(8,128)(2,1)S(1)}, u32[]{:S(2)}, u32[]{:S(2)}) collective-permute-start(bf16[256,512]{1,0:T(8,128)(2,1)S(1)} %collective-permute-done.1), channel_id=1, source_target_pairs={{0,8},{1,15},{8,2},{9,1},{2,10},{3,9},{10,4},{11,3},{4,12},{5,11},... | collective-permute-start | bytes 786440 | tf_op jit(solution)/shard_map/ppermute | solution.py:34
  32.4 3.0 %collective-permute-start.6 = (bf16[256,512]{1,0:T(8,128)(2,1)S(1)}, bf16[256,512]{1,0:T(8,128)(2,1)S(1)}, u32[]{:S(2)}, u32[]{:S(2)}) collective-permute-start(bf16[256,512]{1,0:T(8,128)(2,1)S(1)} %collective-permute-done.4), channel_id=1, source_target_pairs={{0,8},{1,15},{8,2},{9,1},{2,10},{3,9},{10,4},{11,3},{4,12},{5,11},... | collective-permute-start | bytes 786440 | tf_op jit(solution)/shard_map/ppermute | solution.py:34
  35.4 2.8 %collective-permute-done.3 = bf16[256,512]{1,0:T(8,128)(2,1)S(1)} collective-permute-done((bf16[256,512]{1,0:T(8,128)(2,1)S(1)}, bf16[256,512]{1,0:T(8,128)(2,1)S(1)}, u32[]{:S(2)}, u32[]{:S(2)}) %collective-permute-start.3) | collective-permute-done | bytes 262176 | tf_op jit(solution)/shard_map/ppermute | solution.py:34
  38.2 1.9 %collective-permute-start.7 = (bf16[256,512]{1,0:T(8,128)(2,1)S(1)}, bf16[256,512]{1,0:T(8,128)(2,1)S(1)}, u32[]{:S(2)}, u32[]{:S(2)}) collective-permute-start(bf16[256,512]{1,0:T(8,128)(2,1)S(1)} %collective-permute-done.3), channel_id=1, source_target_pairs={{0,8},{1,15},{8,2},{9,1},{2,10},{3,9},{10,4},{11,3},{4,12},{5,11},... | collective-permute-start | bytes 786440 | tf_op jit(solution)/shard_map/ppermute | solution.py:34
  40.2 1.6 %copy-done = bf16[1,256,4096]{2,1,0:T(8,128)(2,1)S(1)} copy-done((bf16[1,256,4096]{2,1,0:T(8,128)(2,1)S(1)}, bf16[1,256,4096]{2,1,0:T(8,128)(2,1)}, u32[]{:S(2)}) %copy-start) | copy-done | bytes 2097176
  41.8 0.8 arrange.1
  42.6 0.3 fusion.32
  42.9 0.3 fusion.29
  43.2 0.3 fusion.34
  43.9 0.3 fusion.2
  44.2 0.3 fusion.26
  44.5 0.3 fusion.1
  44.8 2.9 %collective-permute-done.7 = bf16[256,512]{1,0:T(8,128)(2,1)S(1)} collective-permute-done((bf16[256,512]{1,0:T(8,128)(2,1)S(1)}, bf16[256,512]{1,0:T(8,128)(2,1)S(1)}, u32[]{:S(2)}, u32[]{:S(2)}) %collective-permute-start.7) | collective-permute-done | bytes 262176 | tf_op jit(solution)/shard_map/ppermute | solution.py:34
  47.7 0.3 fusion
  48.2 1.9 %collective-permute-start.8 = (bf16[512,512]{1,0:T(8,128)(2,1)S(1)}, bf16[512,512]{1,0:T(8,128)(2,1)S(1)}, u32[]{:S(2)}, u32[]{:S(2)}) collective-permute-start(bf16[512,512]{1,0:T(8,128)(2,1)S(1)} %fusion.7), channel_id=1, source_target_pairs={{0,1},{1,0},{2,3},{3,2},{4,5},{5,4},{6,7},{7,6},{8,9},{9,8},{10,11... | collective-permute-start | bytes 1572872 | tf_op jit(solution)/shard_map/ppermute | solution.py:23
  50.1 1.9 %collective-permute-done.8 = bf16[512,512]{1,0:T(8,128)(2,1)S(1)} collective-permute-done((bf16[512,512]{1,0:T(8,128)(2,1)S(1)}, bf16[512,512]{1,0:T(8,128)(2,1)S(1)}, u32[]{:S(2)}, u32[]{:S(2)}) %collective-permute-start.8) | collective-permute-done | bytes 524320 | tf_op jit(solution)/shard_map/ppermute | solution.py:23
  52.4 0.6 fusion.8
  53.1 2.9 %collective-permute-start.9 = (bf16[256,512]{1,0:T(8,128)(2,1)S(1)}, bf16[256,512]{1,0:T(8,128)(2,1)S(1)}, u32[]{:S(2)}, u32[]{:S(2)}) collective-permute-start(bf16[256,512]{1,0:T(8,128)(2,1)S(1)} %get-tuple-element.20), channel_id=1, source_target_pairs={{0,14},{1,9},{8,0},{9,3},{2,8},{3,11},{10,2},{11,5},{4,10},{5,13},... | collective-permute-start | bytes 786440 | tf_op jit(solution)/shard_map/ppermute | solution.py:34
  56.0 1.9 %collective-permute-start.10 = (bf16[256,512]{1,0:T(8,128)(2,1)S(1)}, bf16[256,512]{1,0:T(8,128)(2,1)S(1)}, u32[]{:S(2)}, u32[]{:S(2)}) collective-permute-start(bf16[256,512]{1,0:T(8,128)(2,1)S(1)} %get-tuple-element.21), channel_id=1, source_target_pairs={{0,14},{1,9},{8,0},{9,3},{2,8},{3,11},{10,2},{11,5},{4,10},{5,13},... | collective-permute-start | bytes 786440 | tf_op jit(solution)/shard_map/ppermute | solution.py:34
  57.9 2.2 %collective-permute-start.11 = (bf16[256,512]{1,0:T(8,128)(2,1)S(1)}, bf16[256,512]{1,0:T(8,128)(2,1)S(1)}, u32[]{:S(2)}, u32[]{:S(2)}) collective-permute-start(bf16[256,512]{1,0:T(8,128)(2,1)S(1)} %get-tuple-element.22), channel_id=1, source_target_pairs={{0,14},{1,9},{8,0},{9,3},{2,8},{3,11},{10,2},{11,5},{4,10},{5,13},... | collective-permute-start | bytes 786440 | tf_op jit(solution)/shard_map/ppermute | solution.py:34
  60.1 0.9 fusion.4
  61.0 3.2 %collective-permute-done.10 = bf16[256,512]{1,0:T(8,128)(2,1)S(1)} collective-permute-done((bf16[256,512]{1,0:T(8,128)(2,1)S(1)}, bf16[256,512]{1,0:T(8,128)(2,1)S(1)}, u32[]{:S(2)}, u32[]{:S(2)}) %collective-permute-start.10) | collective-permute-done | bytes 262176 | tf_op jit(solution)/shard_map/ppermute | solution.py:34
  64.2 2.8 %collective-permute-done.11 = bf16[256,512]{1,0:T(8,128)(2,1)S(1)} collective-permute-done((bf16[256,512]{1,0:T(8,128)(2,1)S(1)}, bf16[256,512]{1,0:T(8,128)(2,1)S(1)}, u32[]{:S(2)}, u32[]{:S(2)}) %collective-permute-start.11) | collective-permute-done | bytes 262176 | tf_op jit(solution)/shard_map/ppermute | solution.py:34
  67.2 4.0 %collective-permute-start.12 = (bf16[256,512]{1,0:T(8,128)(2,1)S(1)}, bf16[256,512]{1,0:T(8,128)(2,1)S(1)}, u32[]{:S(2)}, u32[]{:S(2)}) collective-permute-start(bf16[256,512]{1,0:T(8,128)(2,1)S(1)} %get-tuple-element.23), channel_id=1, source_target_pairs={{0,6},{1,3},{8,14},{9,11},{2,0},{3,5},{10,8},{11,13},{4,2},{5,7},{... | collective-permute-start | bytes 786440 | tf_op jit(solution)/shard_map/ppermute | solution.py:34
  71.2 2.9 %collective-permute-start.13 = (bf16[256,512]{1,0:T(8,128)(2,1)S(1)}, bf16[256,512]{1,0:T(8,128)(2,1)S(1)}, u32[]{:S(2)}, u32[]{:S(2)}) collective-permute-start(bf16[256,512]{1,0:T(8,128)(2,1)S(1)} %get-tuple-element.24), channel_id=1, source_target_pairs={{0,14},{1,9},{8,0},{9,3},{2,8},{3,11},{10,2},{11,5},{4,10},{5,13},... | collective-permute-start | bytes 786440 | tf_op jit(solution)/shard_map/ppermute | solution.py:34
  74.1 5.2 %collective-permute-done.12 = bf16[256,512]{1,0:T(8,128)(2,1)S(1)} collective-permute-done((bf16[256,512]{1,0:T(8,128)(2,1)S(1)}, bf16[256,512]{1,0:T(8,128)(2,1)S(1)}, u32[]{:S(2)}, u32[]{:S(2)}) %collective-permute-start.12) | collective-permute-done | bytes 262176 | tf_op jit(solution)/shard_map/ppermute | solution.py:34
  79.3 2.8 %collective-permute-done.13 = bf16[256,512]{1,0:T(8,128)(2,1)S(1)} collective-permute-done((bf16[256,512]{1,0:T(8,128)(2,1)S(1)}, bf16[256,512]{1,0:T(8,128)(2,1)S(1)}, u32[]{:S(2)}, u32[]{:S(2)}) %collective-permute-start.13) | collective-permute-done | bytes 262176 | tf_op jit(solution)/shard_map/ppermute | solution.py:34
  82.4 4.4 %collective-permute-start.14 = (bf16[256,512]{1,0:T(8,128)(2,1)S(1)}, bf16[256,512]{1,0:T(8,128)(2,1)S(1)}, u32[]{:S(2)}, u32[]{:S(2)}) collective-permute-start(bf16[256,512]{1,0:T(8,128)(2,1)S(1)} %get-tuple-element.25), channel_id=1, source_target_pairs={{0,14},{1,9},{8,0},{9,3},{2,8},{3,11},{10,2},{11,5},{4,10},{5,13},... | collective-permute-start | bytes 786440 | tf_op jit(solution)/shard_map/ppermute | solution.py:34
  86.7 1.9 %collective-permute-start.15 = (bf16[256,512]{1,0:T(8,128)(2,1)S(1)}, bf16[256,512]{1,0:T(8,128)(2,1)S(1)}, u32[]{:S(2)}, u32[]{:S(2)}) collective-permute-start(bf16[256,512]{1,0:T(8,128)(2,1)S(1)} %get-tuple-element.26), channel_id=1, source_target_pairs={{0,15},{1,8},{8,1},{9,2},{2,9},{3,10},{10,3},{11,4},{4,11},{5,12},... | collective-permute-start | bytes 786440 | tf_op jit(solution)/shard_map/ppermute | solution.py:34
  88.7 2.1 %collective-permute-done.14 = bf16[256,512]{1,0:T(8,128)(2,1)S(1)} collective-permute-done((bf16[256,512]{1,0:T(8,128)(2,1)S(1)}, bf16[256,512]{1,0:T(8,128)(2,1)S(1)}, u32[]{:S(2)}, u32[]{:S(2)}) %collective-permute-start.14) | collective-permute-done | bytes 262176 | tf_op jit(solution)/shard_map/ppermute | solution.py:34
  90.8 4.9 %collective-permute-done.15 = bf16[256,512]{1,0:T(8,128)(2,1)S(1)} collective-permute-done((bf16[256,512]{1,0:T(8,128)(2,1)S(1)}, bf16[256,512]{1,0:T(8,128)(2,1)S(1)}, u32[]{:S(2)}, u32[]{:S(2)}) %collective-permute-start.15) | collective-permute-done | bytes 262176 | tf_op jit(solution)/shard_map/ppermute | solution.py:34
  95.6 1.3 fusion.47
  96.9 26.6 %all_to_all.10.pieces_ref = bf16[32,8,512]{2,1,0:T(8,128)(2,1)S(1)} all-to-all(bf16[32,8,512]{2,1,0:T(8,128)(2,1)S(1)} %bitcast.63), channel_id=1, replica_groups=mesh['col'=32,'lo'=2,'hi'=4,'core'=2] {'col'}, dimensions={0} | all-to-all | bytes 524288 | tf_op jit(solution)/shard_map/all_to_all | solution.py:75
  123.5 1.3 turn.1
  124.8 5.3 %all-to-all-start.1 = ((bf16[32,8,512]{2,1,0:T(8,128)(2,1)}), bf16[32,8,512]{2,1,0:T(8,128)(2,1)S(1)}, u32[]{:S(2)}, u32[]{:S(2)}) async-start(bf16[32,8,512]{2,1,0:T(8,128)(2,1)} %turn.1), calls=%async_computation.1 | async-start | bytes 524288 | tf_op jit(solution)/shard_map/all_to_all | solution.py:96
  130.1 1.6 %dynamic-slice_bitcast_fusion = bf16[256,512]{1,0:T(8,128)(2,1)S(1)} fusion(bf16[32,256,512]{2,1,0:T(8,128)(2,1)} %all-gather.2.cloned.1.call-done, s32[]{:T(128)} %bitcast.3), kind=kLoop, calls=%fused_computation.56 | loop fusion | bytes 524292 | tf_op jit(solution)/shard_map/squeeze | solution.py:181
  131.7 9.4 %all-to-all-done.1 = bf16[32,8,512]{2,1,0:T(8,128)(2,1)S(1)} async-done(((bf16[32,8,512]{2,1,0:T(8,128)(2,1)}), bf16[32,8,512]{2,1,0:T(8,128)(2,1)S(1)}, u32[]{:S(2)}, u32[]{:S(2)}) %all-to-all-start.1) | async-done | bytes 262176 | tf_op jit(solution)/shard_map/all_to_all | solution.py:96
  141.1 1.1 fusion.24
  (28 shorter events, 1.5 us)
Async XLA Ops:
  7.2 122.9 %all-gather.2.cloned.1.call-start = ((), (), s32[]{:S(2)}) async-start(), calls=%async_computation.2 | async-start | bytes 8650752 | tf_op jit(solution)/shard_map/all_gather | solution.py:111
  7.9 32.3 %collective-permute-start = (bf16[256,4096]{1,0:T(8,128)(2,1)}, bf16[256,4096]{1,0:T(8,128)(2,1)S(1)}, u32[]{:S(2)}, u32[]{:S(2)}) collective-permute-start(bf16[256,4096]{1,0:T(8,128)(2,1)} %bitcast.59), channel_id=1, source_target_pairs={{0,1},{1,0},{2,3},{3,2},{4,5},{5,4},{6,7},{7,6},{8,9},{9,8},{10,11... | collective-permute-start | bytes 6291464 | tf_op jit(solution)/shard_map/ppermute | solution.py:23
  9.8 11.1 %collective-permute-start.2 = (bf16[256,512]{1,0:T(8,128)(2,1)}, bf16[256,512]{1,0:T(8,128)(2,1)S(1)}, u32[]{:S(2)}, u32[]{:S(2)}) collective-permute-start(bf16[256,512]{1,0:T(8,128)(2,1)} %bitcast.61), channel_id=1, source_target_pairs={{0,15},{1,8},{8,1},{9,2},{2,9},{3,10},{10,3},{11,4},{4,11},{5,12},... | collective-permute-start | bytes 786440 | tf_op jit(solution)/shard_map/ppermute | solution.py:34
  15.3 9.7 %collective-permute-start.1 = (bf16[256,512]{1,0:T(8,128)(2,1)}, bf16[256,512]{1,0:T(8,128)(2,1)S(1)}, u32[]{:S(2)}, u32[]{:S(2)}) collective-permute-start(bf16[256,512]{1,0:T(8,128)(2,1)} %bitcast.62), channel_id=1, source_target_pairs={{0,8},{1,15},{8,2},{9,1},{2,10},{3,9},{10,4},{11,3},{4,12},{5,11},... | collective-permute-start | bytes 786440 | tf_op jit(solution)/shard_map/ppermute | solution.py:34
  20.9 11.5 %collective-permute-start.4 = (bf16[256,512]{1,0:T(8,128)(2,1)S(1)}, bf16[256,512]{1,0:T(8,128)(2,1)S(1)}, u32[]{:S(2)}, u32[]{:S(2)}) collective-permute-start(bf16[256,512]{1,0:T(8,128)(2,1)S(1)} %collective-permute-done.2), channel_id=1, source_target_pairs={{0,8},{1,15},{8,2},{9,1},{2,10},{3,9},{10,4},{11,3},{4,12},{5,11},... | collective-permute-start | bytes 786440 | tf_op jit(solution)/shard_map/ppermute | solution.py:34
  25.0 13.2 %collective-permute-start.3 = (bf16[256,512]{1,0:T(8,128)(2,1)S(1)}, bf16[256,512]{1,0:T(8,128)(2,1)S(1)}, u32[]{:S(2)}, u32[]{:S(2)}) collective-permute-start(bf16[256,512]{1,0:T(8,128)(2,1)S(1)} %collective-permute-done.1), channel_id=1, source_target_pairs={{0,2},{1,7},{8,10},{9,15},{2,4},{3,1},{10,12},{11,9},{4,6},{5,3},{... | collective-permute-start | bytes 786440 | tf_op jit(solution)/shard_map/ppermute | solution.py:34
  27.6 16.8 %collective-permute-start.5 = (bf16[256,512]{1,0:T(8,128)(2,1)S(1)}, bf16[256,512]{1,0:T(8,128)(2,1)S(1)}, u32[]{:S(2)}, u32[]{:S(2)}) collective-permute-start(bf16[256,512]{1,0:T(8,128)(2,1)S(1)} %collective-permute-done.1), channel_id=1, source_target_pairs={{0,8},{1,15},{8,2},{9,1},{2,10},{3,9},{10,4},{11,3},{4,12},{5,11},... | collective-permute-start | bytes 786440 | tf_op jit(solution)/shard_map/ppermute | solution.py:34
  32.4 11.8 %collective-permute-start.6 = (bf16[256,512]{1,0:T(8,128)(2,1)S(1)}, bf16[256,512]{1,0:T(8,128)(2,1)S(1)}, u32[]{:S(2)}, u32[]{:S(2)}) collective-permute-start(bf16[256,512]{1,0:T(8,128)(2,1)S(1)} %collective-permute-done.4), channel_id=1, source_target_pairs={{0,8},{1,15},{8,2},{9,1},{2,10},{3,9},{10,4},{11,3},{4,12},{5,11},... | collective-permute-start | bytes 786440 | tf_op jit(solution)/shard_map/ppermute | solution.py:34
  38.2 9.5 %collective-permute-start.7 = (bf16[256,512]{1,0:T(8,128)(2,1)S(1)}, bf16[256,512]{1,0:T(8,128)(2,1)S(1)}, u32[]{:S(2)}, u32[]{:S(2)}) collective-permute-start(bf16[256,512]{1,0:T(8,128)(2,1)S(1)} %collective-permute-done.3), channel_id=1, source_target_pairs={{0,8},{1,15},{8,2},{9,1},{2,10},{3,9},{10,4},{11,3},{4,12},{5,11},... | collective-permute-start | bytes 786440 | tf_op jit(solution)/shard_map/ppermute | solution.py:34
  40.2 1.6 %copy-start = (bf16[1,256,4096]{2,1,0:T(8,128)(2,1)S(1)}, bf16[1,256,4096]{2,1,0:T(8,128)(2,1)}, u32[]{:S(2)}) copy-start(bf16[1,256,4096]{2,1,0:T(8,128)(2,1)} %param.9) | copy-start | bytes 6291460
  42.6 1.0 copy-start.2
  44.8 3.2 %copy-start.3 = (bf16[1,256,512]{2,1,0:T(8,128)(2,1)S(1)}, bf16[1,256,512]{2,1,0:T(8,128)(2,1)}, u32[]{:S(2)}) copy-start(bf16[1,256,512]{2,1,0:T(8,128)(2,1)} %param.10) | copy-start | bytes 786436
  48.2 3.8 %collective-permute-start.8 = (bf16[512,512]{1,0:T(8,128)(2,1)S(1)}, bf16[512,512]{1,0:T(8,128)(2,1)S(1)}, u32[]{:S(2)}, u32[]{:S(2)}) collective-permute-start(bf16[512,512]{1,0:T(8,128)(2,1)S(1)} %fusion.7), channel_id=1, source_target_pairs={{0,1},{1,0},{2,3},{3,2},{4,5},{5,4},{6,7},{7,6},{8,9},{9,8},{10,11... | collective-permute-start | bytes 1572872 | tf_op jit(solution)/shard_map/ppermute | solution.py:23
  53.1 21.0 %collective-permute-start.9 = (bf16[256,512]{1,0:T(8,128)(2,1)S(1)}, bf16[256,512]{1,0:T(8,128)(2,1)S(1)}, u32[]{:S(2)}, u32[]{:S(2)}) collective-permute-start(bf16[256,512]{1,0:T(8,128)(2,1)S(1)} %get-tuple-element.20), channel_id=1, source_target_pairs={{0,14},{1,9},{8,0},{9,3},{2,8},{3,11},{10,2},{11,5},{4,10},{5,13},... | collective-permute-start | bytes 786440 | tf_op jit(solution)/shard_map/ppermute | solution.py:34
  56.0 8.3 %collective-permute-start.10 = (bf16[256,512]{1,0:T(8,128)(2,1)S(1)}, bf16[256,512]{1,0:T(8,128)(2,1)S(1)}, u32[]{:S(2)}, u32[]{:S(2)}) collective-permute-start(bf16[256,512]{1,0:T(8,128)(2,1)S(1)} %get-tuple-element.21), channel_id=1, source_target_pairs={{0,14},{1,9},{8,0},{9,3},{2,8},{3,11},{10,2},{11,5},{4,10},{5,13},... | collective-permute-start | bytes 786440 | tf_op jit(solution)/shard_map/ppermute | solution.py:34
  57.9 9.1 %collective-permute-start.11 = (bf16[256,512]{1,0:T(8,128)(2,1)S(1)}, bf16[256,512]{1,0:T(8,128)(2,1)S(1)}, u32[]{:S(2)}, u32[]{:S(2)}) collective-permute-start(bf16[256,512]{1,0:T(8,128)(2,1)S(1)} %get-tuple-element.22), channel_id=1, source_target_pairs={{0,14},{1,9},{8,0},{9,3},{2,8},{3,11},{10,2},{11,5},{4,10},{5,13},... | collective-permute-start | bytes 786440 | tf_op jit(solution)/shard_map/ppermute | solution.py:34
  61.0 34.6 %copy-start.4 = (bf16[1,256,512]{2,1,0:T(8,128)(2,1)S(1)}, bf16[1,256,512]{2,1,0:T(8,128)(2,1)}, u32[]{:S(2)}) copy-start(bf16[1,256,512]{2,1,0:T(8,128)(2,1)} %param.13) | copy-start | bytes 786436
  61.0 34.6 %copy-start.5 = (bf16[1,256,512]{2,1,0:T(8,128)(2,1)S(1)}, bf16[1,256,512]{2,1,0:T(8,128)(2,1)}, u32[]{:S(2)}) copy-start(bf16[1,256,512]{2,1,0:T(8,128)(2,1)} %param.12) | copy-start | bytes 786436
  67.2 12.1 %collective-permute-start.12 = (bf16[256,512]{1,0:T(8,128)(2,1)S(1)}, bf16[256,512]{1,0:T(8,128)(2,1)S(1)}, u32[]{:S(2)}, u32[]{:S(2)}) collective-permute-start(bf16[256,512]{1,0:T(8,128)(2,1)S(1)} %get-tuple-element.23), channel_id=1, source_target_pairs={{0,6},{1,3},{8,14},{9,11},{2,0},{3,5},{10,8},{11,13},{4,2},{5,7},{... | collective-permute-start | bytes 786440 | tf_op jit(solution)/shard_map/ppermute | solution.py:34
  71.2 10.9 %collective-permute-start.13 = (bf16[256,512]{1,0:T(8,128)(2,1)S(1)}, bf16[256,512]{1,0:T(8,128)(2,1)S(1)}, u32[]{:S(2)}, u32[]{:S(2)}) collective-permute-start(bf16[256,512]{1,0:T(8,128)(2,1)S(1)} %get-tuple-element.24), channel_id=1, source_target_pairs={{0,14},{1,9},{8,0},{9,3},{2,8},{3,11},{10,2},{11,5},{4,10},{5,13},... | collective-permute-start | bytes 786440 | tf_op jit(solution)/shard_map/ppermute | solution.py:34
  82.3 41.2 %copy-start.1 = (s32[32]{0:T(128)S(1)}, s32[32]{0:T(128)}, u32[]{:S(2)}) copy-start(s32[32]{0:T(128)} %partner_ref.1) | copy-start | bytes 388
  82.3 58.8 %copy-start.6 = (bf16[1,256,512]{2,1,0:T(8,128)(2,1)S(1)}, bf16[1,256,512]{2,1,0:T(8,128)(2,1)}, u32[]{:S(2)}) copy-start(bf16[1,256,512]{2,1,0:T(8,128)(2,1)} %param.14) | copy-start | bytes 786436
  82.4 8.4 %collective-permute-start.14 = (bf16[256,512]{1,0:T(8,128)(2,1)S(1)}, bf16[256,512]{1,0:T(8,128)(2,1)S(1)}, u32[]{:S(2)}, u32[]{:S(2)}) collective-permute-start(bf16[256,512]{1,0:T(8,128)(2,1)S(1)} %get-tuple-element.25), channel_id=1, source_target_pairs={{0,14},{1,9},{8,0},{9,3},{2,8},{3,11},{10,2},{11,5},{4,10},{5,13},... | collective-permute-start | bytes 786440 | tf_op jit(solution)/shard_map/ppermute | solution.py:34
  86.7 8.9 %collective-permute-start.15 = (bf16[256,512]{1,0:T(8,128)(2,1)S(1)}, bf16[256,512]{1,0:T(8,128)(2,1)S(1)}, u32[]{:S(2)}, u32[]{:S(2)}) collective-permute-start(bf16[256,512]{1,0:T(8,128)(2,1)S(1)} %get-tuple-element.26), channel_id=1, source_target_pairs={{0,15},{1,8},{8,1},{9,2},{2,9},{3,10},{10,3},{11,4},{4,11},{5,12},... | collective-permute-start | bytes 786440 | tf_op jit(solution)/shard_map/ppermute | solution.py:34
  124.8 16.3 %all-to-all-start.1 = ((bf16[32,8,512]{2,1,0:T(8,128)(2,1)}), bf16[32,8,512]{2,1,0:T(8,128)(2,1)S(1)}, u32[]{:S(2)}, u32[]{:S(2)}) async-start(bf16[32,8,512]{2,1,0:T(8,128)(2,1)} %turn.1), calls=%async_computation.1 | async-start | bytes 524288 | tf_op jit(solution)/shard_map/all_to_all | solution.py:96
Sparse Core Ops, SparseCore 0:
  11.2 111.7 all-gather.1

commit v8 on v6

--- a/solution.py
+++ b/solution.py
@@ -109,12 +109,13 @@
     norm_scale = (2 * ring * tokens.shape[1]) ** (-0.5)
 
     everyone = lax.all_gather(shard, "col")
-    beside = swap_core(tokens[0])
     a1, b1 = hop(shard, ring, True), hop(shard, ring, True, cross=True)
     facing = lax.dynamic_slice(
         partner, (lax.axis_index("col"),), (1,), allow_negative_indices=False
     )[0]
     b1, facing = lax.optimization_barrier((b1, facing))
+    own, _, _ = lax.optimization_barrier((tokens[0], a1, b1))
+    beside = swap_core(own)
     a3, b2, a2 = hop(a1, ring, True, chips=2), hop(b1, ring, True), hop(a1, ring, True)
 
     places = [(0, 0), (1, 0), (1, 1), (3, 0), (2, 1), (2, 0), (3, 1), (4, 0)]
@@ -122,7 +123,7 @@
     other = jnp.array([o for _, o in places], jnp.int32)
     source = (chip + jnp.where(core == 0, -away, away)) % ring
     starts = ((source % 2 * half + source // 2) * 2 + (core + other) % 2) * rows
-    inputs = arrange(tokens[0], beside, starts.astype(jnp.int32), rows)
+    inputs = arrange(own, beside, starts.astype(jnp.int32), rows)
 
     blocks = [shard, a1, b1, a3, b2, a2, hop(b2, ring, True), hop(a3, ring, True)]
 

time: 148 us -> 148 us (level)
  starting transfers between devices: 44.4 us -> 52 us
  waiting for transfers between devices: 31.1 us -> 24.4 us
    ppermute x14, starting transfers between devices: 40.5 us -> 48.1 us  [hop(): return lax.ppermute(value, REPLICA, pairs)]
    ppermute x14, waiting for transfers between devices: 28.6 us -> 21.8 us  [hop(): return lax.ppermute(value, REPLICA, pairs)]
  transfers between devices with their start and end apart: 17 -> 17, of which waited for: 11 -> 9; matrix products, arithmetic and copies ran while one was open for 6% -> 6% of each run, Pallas kernels for 1% -> 1%
where the time goes in v8:
time: 148 us
  starting transfers between devices  52 us (35%)
  blocking collectives  42.5 us (29%)
  waiting for transfers between devices  24.4 us (16%)
  between operations  14.4 us (10%)
  other arithmetic  5.52 us (4%)
  matrix products  3.88 us (3%)
  local copies, waits for them, and re-layouts  3.49 us (2%)
    ppermute x14, starting transfers between devices, hop(): return lax.ppermute(value, REPLICA, pairs)  48.1 us
    all_to_all x1, blocking collectives, scatter_pieces(): lax.all_to_all(pieces, 'col', split_axis=0, concat_axis=0, tiled=True)  26.4 us
    ppermute x14, waiting for transfers between devices, hop(): return lax.ppermute(value, REPLICA, pairs)  21.8 us
    all_to_all x1, blocking collectives, deliver_pieces(): got = lax.all_to_all(turned, 'col', split_axis=0, concat_axis=0, tiled=True)  16.1 us
    ppermute x2, starting transfers between devices, swap_core(): return lax.ppermute(value, 'core', [(0, 1), (1, 0)])  3.83 us
  transfers between devices with their start and end apart: 17, of which 9 were waited for; matrix products, arithmetic and copies ran while one was open for 6% of the time, Pallas kernels for 1%

profile of v8, /device:TPU:64, one launch (start us, length us, event | category | flops | bytes accessed | tf_op | source)
XLA Modules:
  0.0 147.6 jit_solution(15285592993619156143)
XLA Ops:
  7.2 0.7 all-gather.2.cloned.1.call-update
  7.9 4.8 %collective-permute-start.1 = (bf16[256,512]{1,0:T(8,128)(2,1)}, bf16[256,512]{1,0:T(8,128)(2,1)S(1)}, u32[]{:S(2)}, u32[]{:S(2)}) collective-permute-start(bf16[256,512]{1,0:T(8,128)(2,1)} %bitcast.64), channel_id=1, source_target_pairs={{0,15},{1,8},{8,1},{9,2},{2,9},{3,10},{10,3},{11,4},{4,11},{5,12},... | collective-permute-start | bytes 786440 | tf_op jit(solution)/shard_map/ppermute | solution.py:34
  12.7 1.9 %collective-permute-start = (bf16[256,512]{1,0:T(8,128)(2,1)}, bf16[256,512]{1,0:T(8,128)(2,1)S(1)}, u32[]{:S(2)}, u32[]{:S(2)}) collective-permute-start(bf16[256,512]{1,0:T(8,128)(2,1)} %bitcast.65), channel_id=1, source_target_pairs={{0,8},{1,15},{8,2},{9,1},{2,10},{3,9},{10,4},{11,3},{4,12},{5,11},... | collective-permute-start | bytes 786440 | tf_op jit(solution)/shard_map/ppermute | solution.py:34
  14.7 1.3 dynamic_slice.6
  16.0 2.3 %collective-permute-done.1 = bf16[256,512]{1,0:T(8,128)(2,1)S(1)} collective-permute-done((bf16[256,512]{1,0:T(8,128)(2,1)}, bf16[256,512]{1,0:T(8,128)(2,1)S(1)}, u32[]{:S(2)}, u32[]{:S(2)}) %collective-permute-start.1) | collective-permute-done | bytes 262176 | tf_op jit(solution)/shard_map/ppermute | solution.py:34
  18.3 4.1 %collective-permute-done = bf16[256,512]{1,0:T(8,128)(2,1)S(1)} collective-permute-done((bf16[256,512]{1,0:T(8,128)(2,1)}, bf16[256,512]{1,0:T(8,128)(2,1)S(1)}, u32[]{:S(2)}, u32[]{:S(2)}) %collective-permute-start) | collective-permute-done | bytes 262176 | tf_op jit(solution)/shard_map/ppermute | solution.py:34
  22.4 1.9 %collective-permute-start.2 = (bf16[256,4096]{1,0:T(8,128)(2,1)}, bf16[256,4096]{1,0:T(8,128)(2,1)S(1)}, u32[]{:S(2)}, u32[]{:S(2)}) collective-permute-start(bf16[256,4096]{1,0:T(8,128)(2,1)} %bitcast.62), channel_id=1, source_target_pairs={{0,1},{1,0},{2,3},{3,2},{4,5},{5,4},{6,7},{7,6},{8,9},{9,8},{10,11... | collective-permute-start | bytes 6291464 | tf_op jit(solution)/shard_map/ppermute | solution.py:23
  24.3 1.9 %collective-permute-start.4 = (bf16[256,512]{1,0:T(8,128)(2,1)S(1)}, bf16[256,512]{1,0:T(8,128)(2,1)S(1)}, u32[]{:S(2)}, u32[]{:S(2)}) collective-permute-start(bf16[256,512]{1,0:T(8,128)(2,1)S(1)} %collective-permute-done.1), channel_id=1, source_target_pairs={{0,8},{1,15},{8,2},{9,1},{2,10},{3,9},{10,4},{11,3},{4,12},{5,11},... | collective-permute-start | bytes 786440 | tf_op jit(solution)/shard_map/ppermute | solution.py:34
  26.3 4.9 %collective-permute-start.3 = (bf16[256,512]{1,0:T(8,128)(2,1)S(1)}, bf16[256,512]{1,0:T(8,128)(2,1)S(1)}, u32[]{:S(2)}, u32[]{:S(2)}) collective-permute-start(bf16[256,512]{1,0:T(8,128)(2,1)S(1)} %collective-permute-done), channel_id=1, source_target_pairs={{0,2},{1,7},{8,10},{9,15},{2,4},{3,1},{10,12},{11,9},{4,6},{5,3},{... | collective-permute-start | bytes 786440 | tf_op jit(solution)/shard_map/ppermute | solution.py:34
  31.2 0.7 fusion.41.starts_ref
  31.9 3.3 %collective-permute-start.5 = (bf16[256,512]{1,0:T(8,128)(2,1)S(1)}, bf16[256,512]{1,0:T(8,128)(2,1)S(1)}, u32[]{:S(2)}, u32[]{:S(2)}) collective-permute-start(bf16[256,512]{1,0:T(8,128)(2,1)S(1)} %collective-permute-done), channel_id=1, source_target_pairs={{0,8},{1,15},{8,2},{9,1},{2,10},{3,9},{10,4},{11,3},{4,12},{5,11},... | collective-permute-start | bytes 786440 | tf_op jit(solution)/shard_map/ppermute | solution.py:34
  35.2 1.9 %collective-permute-start.6 = (bf16[256,512]{1,0:T(8,128)(2,1)S(1)}, bf16[256,512]{1,0:T(8,128)(2,1)S(1)}, u32[]{:S(2)}, u32[]{:S(2)}) collective-permute-start(bf16[256,512]{1,0:T(8,128)(2,1)S(1)} %collective-permute-done.4), channel_id=1, source_target_pairs={{0,8},{1,15},{8,2},{9,1},{2,10},{3,9},{10,4},{11,3},{4,12},{5,11},... | collective-permute-start | bytes 786440 | tf_op jit(solution)/shard_map/ppermute | solution.py:34
  37.1 5.8 %collective-permute-start.7 = (bf16[256,512]{1,0:T(8,128)(2,1)S(1)}, bf16[256,512]{1,0:T(8,128)(2,1)S(1)}, u32[]{:S(2)}, u32[]{:S(2)}) collective-permute-start(bf16[256,512]{1,0:T(8,128)(2,1)S(1)} %collective-permute-done.3), channel_id=1, source_target_pairs={{0,8},{1,15},{8,2},{9,1},{2,10},{3,9},{10,4},{11,3},{4,12},{5,11},... | collective-permute-start | bytes 786440 | tf_op jit(solution)/shard_map/ppermute | solution.py:34
  42.9 1.6 %copy-done = bf16[1,256,4096]{2,1,0:T(8,128)(2,1)S(1)} copy-done((bf16[1,256,4096]{2,1,0:T(8,128)(2,1)S(1)}, bf16[1,256,4096]{2,1,0:T(8,128)(2,1)}, u32[]{:S(2)}) %copy-start) | copy-done | bytes 2097176
  44.5 0.8 arrange.1
  45.4 0.3 fusion.32
  45.7 0.3 fusion.34
  46.0 0.3 fusion.29
  46.3 0.3 fusion.3
  46.6 0.3 fusion.2
  46.9 0.3 fusion.26
  47.3 0.3 fusion.1
  47.6 0.3 collective-permute-done.7
  47.9 0.3 fusion
  48.2 0.4 copy-done.3
  48.7 1.9 %collective-permute-start.8 = (bf16[512,512]{1,0:T(8,128)(2,1)S(1)}, bf16[512,512]{1,0:T(8,128)(2,1)S(1)}, u32[]{:S(2)}, u32[]{:S(2)}) collective-permute-start(bf16[512,512]{1,0:T(8,128)(2,1)S(1)} %fusion.7), channel_id=1, source_target_pairs={{0,1},{1,0},{2,3},{3,2},{4,5},{5,4},{6,7},{7,6},{8,9},{9,8},{10,11... | collective-permute-start | bytes 1572872 | tf_op jit(solution)/shard_map/ppermute | solution.py:23
  50.6 1.9 %collective-permute-done.8 = bf16[512,512]{1,0:T(8,128)(2,1)S(1)} collective-permute-done((bf16[512,512]{1,0:T(8,128)(2,1)S(1)}, bf16[512,512]{1,0:T(8,128)(2,1)S(1)}, u32[]{:S(2)}, u32[]{:S(2)}) %collective-permute-start.8) | collective-permute-done | bytes 524320 | tf_op jit(solution)/shard_map/ppermute | solution.py:23
  52.6 0.3 fusion.6
  52.9 0.6 fusion.8
  53.6 2.4 %collective-permute-start.10 = (bf16[256,512]{1,0:T(8,128)(2,1)S(1)}, bf16[256,512]{1,0:T(8,128)(2,1)S(1)}, u32[]{:S(2)}, u32[]{:S(2)}) collective-permute-start(bf16[256,512]{1,0:T(8,128)(2,1)S(1)} %get-tuple-element.23), channel_id=1, source_target_pairs={{0,14},{1,9},{8,0},{9,3},{2,8},{3,11},{10,2},{11,5},{4,10},{5,13},... | collective-permute-start | bytes 786440 | tf_op jit(solution)/shard_map/ppermute | solution.py:34
  56.0 3.3 %collective-permute-start.11 = (bf16[256,512]{1,0:T(8,128)(2,1)S(1)}, bf16[256,512]{1,0:T(8,128)(2,1)S(1)}, u32[]{:S(2)}, u32[]{:S(2)}) collective-permute-start(bf16[256,512]{1,0:T(8,128)(2,1)S(1)} %get-tuple-element.24), channel_id=1, source_target_pairs={{0,14},{1,9},{8,0},{9,3},{2,8},{3,11},{10,2},{11,5},{4,10},{5,13},... | collective-permute-start | bytes 786440 | tf_op jit(solution)/shard_map/ppermute | solution.py:34
  59.4 3.9 %collective-permute-start.9 = (bf16[256,512]{1,0:T(8,128)(2,1)S(1)}, bf16[256,512]{1,0:T(8,128)(2,1)S(1)}, u32[]{:S(2)}, u32[]{:S(2)}) collective-permute-start(bf16[256,512]{1,0:T(8,128)(2,1)S(1)} %get-tuple-element.22), channel_id=1, source_target_pairs={{0,14},{1,9},{8,0},{9,3},{2,8},{3,11},{10,2},{11,5},{4,10},{5,13},... | collective-permute-start | bytes 786440 | tf_op jit(solution)/shard_map/ppermute | solution.py:34
  63.3 0.9 fusion.4
  64.2 0.5 collective-permute-done.11
  64.9 4.4 %collective-permute-start.12 = (bf16[256,512]{1,0:T(8,128)(2,1)S(1)}, bf16[256,512]{1,0:T(8,128)(2,1)S(1)}, u32[]{:S(2)}, u32[]{:S(2)}) collective-permute-start(bf16[256,512]{1,0:T(8,128)(2,1)S(1)} %get-tuple-element.25), channel_id=1, source_target_pairs={{0,6},{1,3},{8,14},{9,11},{2,0},{3,5},{10,8},{11,13},{4,2},{5,7},{... | collective-permute-start | bytes 786440 | tf_op jit(solution)/shard_map/ppermute | solution.py:34
  69.3 2.9 %collective-permute-start.13 = (bf16[256,512]{1,0:T(8,128)(2,1)S(1)}, bf16[256,512]{1,0:T(8,128)(2,1)S(1)}, u32[]{:S(2)}, u32[]{:S(2)}) collective-permute-start(bf16[256,512]{1,0:T(8,128)(2,1)S(1)} %get-tuple-element.26), channel_id=1, source_target_pairs={{0,14},{1,9},{8,0},{9,3},{2,8},{3,11},{10,2},{11,5},{4,10},{5,13},... | collective-permute-start | bytes 786440 | tf_op jit(solution)/shard_map/ppermute | solution.py:34
  72.2 4.8 %collective-permute-done.12 = bf16[256,512]{1,0:T(8,128)(2,1)S(1)} collective-permute-done((bf16[256,512]{1,0:T(8,128)(2,1)S(1)}, bf16[256,512]{1,0:T(8,128)(2,1)S(1)}, u32[]{:S(2)}, u32[]{:S(2)}) %collective-permute-start.12) | collective-permute-done | bytes 262176 | tf_op jit(solution)/shard_map/ppermute | solution.py:34
  77.0 2.8 %collective-permute-done.13 = bf16[256,512]{1,0:T(8,128)(2,1)S(1)} collective-permute-done((bf16[256,512]{1,0:T(8,128)(2,1)S(1)}, bf16[256,512]{1,0:T(8,128)(2,1)S(1)}, u32[]{:S(2)}, u32[]{:S(2)}) %collective-permute-start.13) | collective-permute-done | bytes 262176 | tf_op jit(solution)/shard_map/ppermute | solution.py:34
  79.8 0.2 fusion.15
  80.0 4.7 %collective-permute-start.14 = (bf16[256,512]{1,0:T(8,128)(2,1)S(1)}, bf16[256,512]{1,0:T(8,128)(2,1)S(1)}, u32[]{:S(2)}, u32[]{:S(2)}) collective-permute-start(bf16[256,512]{1,0:T(8,128)(2,1)S(1)} %get-tuple-element.27), channel_id=1, source_target_pairs={{0,14},{1,9},{8,0},{9,3},{2,8},{3,11},{10,2},{11,5},{4,10},{5,13},... | collective-permute-start | bytes 786440 | tf_op jit(solution)/shard_map/ppermute | solution.py:34
  84.8 1.9 %collective-permute-start.15 = (bf16[256,512]{1,0:T(8,128)(2,1)S(1)}, bf16[256,512]{1,0:T(8,128)(2,1)S(1)}, u32[]{:S(2)}, u32[]{:S(2)}) collective-permute-start(bf16[256,512]{1,0:T(8,128)(2,1)S(1)} %get-tuple-element.28), channel_id=1, source_target_pairs={{0,15},{1,8},{8,1},{9,2},{2,9},{3,10},{10,3},{11,4},{4,11},{5,12},... | collective-permute-start | bytes 786440 | tf_op jit(solution)/shard_map/ppermute | solution.py:34
  86.7 1.9 %collective-permute-done.14 = bf16[256,512]{1,0:T(8,128)(2,1)S(1)} collective-permute-done((bf16[256,512]{1,0:T(8,128)(2,1)S(1)}, bf16[256,512]{1,0:T(8,128)(2,1)S(1)}, u32[]{:S(2)}, u32[]{:S(2)}) %collective-permute-start.14) | collective-permute-done | bytes 262176 | tf_op jit(solution)/shard_map/ppermute | solution.py:34
  88.6 5.0 %collective-permute-done.15 = bf16[256,512]{1,0:T(8,128)(2,1)S(1)} collective-permute-done((bf16[256,512]{1,0:T(8,128)(2,1)S(1)}, bf16[256,512]{1,0:T(8,128)(2,1)S(1)}, u32[]{:S(2)}, u32[]{:S(2)}) %collective-permute-start.15) | collective-permute-done | bytes 262176 | tf_op jit(solution)/shard_map/ppermute | solution.py:34
  93.7 1.3 fusion.47
  95.0 26.4 %all_to_all.10.pieces_ref = bf16[32,8,512]{2,1,0:T(8,128)(2,1)S(1)} all-to-all(bf16[32,8,512]{2,1,0:T(8,128)(2,1)S(1)} %bitcast.66), channel_id=1, replica_groups=mesh['col'=32,'lo'=2,'hi'=4,'core'=2] {'col'}, dimensions={0} | all-to-all | bytes 524288 | tf_op jit(solution)/shard_map/all_to_all | solution.py:75
  121.4 0.6 turn.1
  122.0 16.1 %all_to_all.11 = bf16[32,8,512]{2,1,0:T(8,128)(2,1)S(1)} all-to-all(bf16[32,8,512]{2,1,0:T(8,128)(2,1)S(1)} %turn.1), channel_id=1, replica_groups=mesh['col'=32,'lo'=2,'hi'=4,'core'=2] {'col'}, dimensions={0} | all-to-all | bytes 524288 | tf_op jit(solution)/shard_map/all_to_all | solution.py:96
  138.1 2.6 %fusion.24 = (bf16[1,256,512]{2,1,0:T(8,128)(2,1)}, bf16[1,256,512]{2,1,0:T(8,128)(2,1)}) fusion(f32[256,512]{1,0:T(8,128)S(1)} %get-tuple-element.29, bf16[1,256,512]{2,1,0:T(8,128)(2,1)S(1)} %copy-done.6, bf16[32,8,512]{2,1,0:T(8,128)(2,1)S(1)} %all_to_all.11, bf16[32,256,512]{2,1,0:T(8,128)(2,1)} %all-gather.2.cloned.1.call-done, s32[]{:T(128)} %bitcast.3, ...), kind=kLoop, calls=%fused_computation.43 | loop fusion | flops 2228224 | bytes 2097156 | tf_op jit(solution)/shard_map/broadcast_in_dim | solution.py:187
  (26 shorter events, 0.7 us)
Async XLA Ops:
  7.2 130.9 %all-gather.2.cloned.1.call-start = ((), (), s32[]{:S(2)}) async-start(), calls=%async_computation.2 | async-start | bytes 8650752 | tf_op jit(solution)/shard_map/all_gather | solution.py:111
  7.9 10.4 %collective-permute-start.1 = (bf16[256,512]{1,0:T(8,128)(2,1)}, bf16[256,512]{1,0:T(8,128)(2,1)S(1)}, u32[]{:S(2)}, u32[]{:S(2)}) collective-permute-start(bf16[256,512]{1,0:T(8,128)(2,1)} %bitcast.64), channel_id=1, source_target_pairs={{0,15},{1,8},{8,1},{9,2},{2,9},{3,10},{10,3},{11,4},{4,11},{5,12},... | collective-permute-start | bytes 786440 | tf_op jit(solution)/shard_map/ppermute | solution.py:34
  12.7 9.7 %collective-permute-start = (bf16[256,512]{1,0:T(8,128)(2,1)}, bf16[256,512]{1,0:T(8,128)(2,1)S(1)}, u32[]{:S(2)}, u32[]{:S(2)}) collective-permute-start(bf16[256,512]{1,0:T(8,128)(2,1)} %bitcast.65), channel_id=1, source_target_pairs={{0,8},{1,15},{8,2},{9,1},{2,10},{3,9},{10,4},{11,3},{4,12},{5,11},... | collective-permute-start | bytes 786440 | tf_op jit(solution)/shard_map/ppermute | solution.py:34
  22.4 20.5 %collective-permute-start.2 = (bf16[256,4096]{1,0:T(8,128)(2,1)}, bf16[256,4096]{1,0:T(8,128)(2,1)S(1)}, u32[]{:S(2)}, u32[]{:S(2)}) collective-permute-start(bf16[256,4096]{1,0:T(8,128)(2,1)} %bitcast.62), channel_id=1, source_target_pairs={{0,1},{1,0},{2,3},{3,2},{4,5},{5,4},{6,7},{7,6},{8,9},{9,8},{10,11... | collective-permute-start | bytes 6291464 | tf_op jit(solution)/shard_map/ppermute | solution.py:23
  24.3 10.8 %collective-permute-start.4 = (bf16[256,512]{1,0:T(8,128)(2,1)S(1)}, bf16[256,512]{1,0:T(8,128)(2,1)S(1)}, u32[]{:S(2)}, u32[]{:S(2)}) collective-permute-start(bf16[256,512]{1,0:T(8,128)(2,1)S(1)} %collective-permute-done.1), channel_id=1, source_target_pairs={{0,8},{1,15},{8,2},{9,1},{2,10},{3,9},{10,4},{11,3},{4,12},{5,11},... | collective-permute-start | bytes 786440 | tf_op jit(solution)/shard_map/ppermute | solution.py:34
  26.3 10.8 %collective-permute-start.3 = (bf16[256,512]{1,0:T(8,128)(2,1)S(1)}, bf16[256,512]{1,0:T(8,128)(2,1)S(1)}, u32[]{:S(2)}, u32[]{:S(2)}) collective-permute-start(bf16[256,512]{1,0:T(8,128)(2,1)S(1)} %collective-permute-done), channel_id=1, source_target_pairs={{0,2},{1,7},{8,10},{9,15},{2,4},{3,1},{10,12},{11,9},{4,6},{5,3},{... | collective-permute-start | bytes 786440 | tf_op jit(solution)/shard_map/ppermute | solution.py:34
  31.9 15.4 %collective-permute-start.5 = (bf16[256,512]{1,0:T(8,128)(2,1)S(1)}, bf16[256,512]{1,0:T(8,128)(2,1)S(1)}, u32[]{:S(2)}, u32[]{:S(2)}) collective-permute-start(bf16[256,512]{1,0:T(8,128)(2,1)S(1)} %collective-permute-done), channel_id=1, source_target_pairs={{0,8},{1,15},{8,2},{9,1},{2,10},{3,9},{10,4},{11,3},{4,12},{5,11},... | collective-permute-start | bytes 786440 | tf_op jit(solution)/shard_map/ppermute | solution.py:34
  35.2 11.8 %collective-permute-start.6 = (bf16[256,512]{1,0:T(8,128)(2,1)S(1)}, bf16[256,512]{1,0:T(8,128)(2,1)S(1)}, u32[]{:S(2)}, u32[]{:S(2)}) collective-permute-start(bf16[256,512]{1,0:T(8,128)(2,1)S(1)} %collective-permute-done.4), channel_id=1, source_target_pairs={{0,8},{1,15},{8,2},{9,1},{2,10},{3,9},{10,4},{11,3},{4,12},{5,11},... | collective-permute-start | bytes 786440 | tf_op jit(solution)/shard_map/ppermute | solution.py:34
  37.1 10.7 %collective-permute-start.7 = (bf16[256,512]{1,0:T(8,128)(2,1)S(1)}, bf16[256,512]{1,0:T(8,128)(2,1)S(1)}, u32[]{:S(2)}, u32[]{:S(2)}) collective-permute-start(bf16[256,512]{1,0:T(8,128)(2,1)S(1)} %collective-permute-done.3), channel_id=1, source_target_pairs={{0,8},{1,15},{8,2},{9,1},{2,10},{3,9},{10,4},{11,3},{4,12},{5,11},... | collective-permute-start | bytes 786440 | tf_op jit(solution)/shard_map/ppermute | solution.py:34
  42.9 1.6 %copy-start = (bf16[1,256,4096]{2,1,0:T(8,128)(2,1)S(1)}, bf16[1,256,4096]{2,1,0:T(8,128)(2,1)}, u32[]{:S(2)}) copy-start(bf16[1,256,4096]{2,1,0:T(8,128)(2,1)} %param.9) | copy-start | bytes 6291460
  45.4 1.0 copy-start.2
  47.6 1.0 copy-start.3
  48.7 3.8 %collective-permute-start.8 = (bf16[512,512]{1,0:T(8,128)(2,1)S(1)}, bf16[512,512]{1,0:T(8,128)(2,1)S(1)}, u32[]{:S(2)}, u32[]{:S(2)}) collective-permute-start(bf16[512,512]{1,0:T(8,128)(2,1)S(1)} %fusion.7), channel_id=1, source_target_pairs={{0,1},{1,0},{2,3},{3,2},{4,5},{5,4},{6,7},{7,6},{8,9},{9,8},{10,11... | collective-permute-start | bytes 1572872 | tf_op jit(solution)/shard_map/ppermute | solution.py:23
  53.6 10.6 %collective-permute-start.10 = (bf16[256,512]{1,0:T(8,128)(2,1)S(1)}, bf16[256,512]{1,0:T(8,128)(2,1)S(1)}, u32[]{:S(2)}, u32[]{:S(2)}) collective-permute-start(bf16[256,512]{1,0:T(8,128)(2,1)S(1)} %get-tuple-element.23), channel_id=1, source_target_pairs={{0,14},{1,9},{8,0},{9,3},{2,8},{3,11},{10,2},{11,5},{4,10},{5,13},... | collective-permute-start | bytes 786440 | tf_op jit(solution)/shard_map/ppermute | solution.py:34
  56.0 8.7 %collective-permute-start.11 = (bf16[256,512]{1,0:T(8,128)(2,1)S(1)}, bf16[256,512]{1,0:T(8,128)(2,1)S(1)}, u32[]{:S(2)}, u32[]{:S(2)}) collective-permute-start(bf16[256,512]{1,0:T(8,128)(2,1)S(1)} %get-tuple-element.24), channel_id=1, source_target_pairs={{0,14},{1,9},{8,0},{9,3},{2,8},{3,11},{10,2},{11,5},{4,10},{5,13},... | collective-permute-start | bytes 786440 | tf_op jit(solution)/shard_map/ppermute | solution.py:34
  59.4 12.8 %collective-permute-start.9 = (bf16[256,512]{1,0:T(8,128)(2,1)S(1)}, bf16[256,512]{1,0:T(8,128)(2,1)S(1)}, u32[]{:S(2)}, u32[]{:S(2)}) collective-permute-start(bf16[256,512]{1,0:T(8,128)(2,1)S(1)} %get-tuple-element.22), channel_id=1, source_target_pairs={{0,14},{1,9},{8,0},{9,3},{2,8},{3,11},{10,2},{11,5},{4,10},{5,13},... | collective-permute-start | bytes 786440 | tf_op jit(solution)/shard_map/ppermute | solution.py:34
  64.2 29.5 %copy-start.4 = (bf16[1,256,512]{2,1,0:T(8,128)(2,1)S(1)}, bf16[1,256,512]{2,1,0:T(8,128)(2,1)}, u32[]{:S(2)}) copy-start(bf16[1,256,512]{2,1,0:T(8,128)(2,1)} %param.13) | copy-start | bytes 786436
  64.2 29.5 %copy-start.5 = (bf16[1,256,512]{2,1,0:T(8,128)(2,1)S(1)}, bf16[1,256,512]{2,1,0:T(8,128)(2,1)}, u32[]{:S(2)}) copy-start(bf16[1,256,512]{2,1,0:T(8,128)(2,1)} %param.12) | copy-start | bytes 786436
  64.9 12.1 %collective-permute-start.12 = (bf16[256,512]{1,0:T(8,128)(2,1)S(1)}, bf16[256,512]{1,0:T(8,128)(2,1)S(1)}, u32[]{:S(2)}, u32[]{:S(2)}) collective-permute-start(bf16[256,512]{1,0:T(8,128)(2,1)S(1)} %get-tuple-element.25), channel_id=1, source_target_pairs={{0,6},{1,3},{8,14},{9,11},{2,0},{3,5},{10,8},{11,13},{4,2},{5,7},{... | collective-permute-start | bytes 786440 | tf_op jit(solution)/shard_map/ppermute | solution.py:34
  69.3 10.5 %collective-permute-start.13 = (bf16[256,512]{1,0:T(8,128)(2,1)S(1)}, bf16[256,512]{1,0:T(8,128)(2,1)S(1)}, u32[]{:S(2)}, u32[]{:S(2)}) collective-permute-start(bf16[256,512]{1,0:T(8,128)(2,1)S(1)} %get-tuple-element.26), channel_id=1, source_target_pairs={{0,14},{1,9},{8,0},{9,3},{2,8},{3,11},{10,2},{11,5},{4,10},{5,13},... | collective-permute-start | bytes 786440 | tf_op jit(solution)/shard_map/ppermute | solution.py:34
  80.0 41.4 %copy-start.1 = (s32[32]{0:T(128)S(1)}, s32[32]{0:T(128)}, u32[]{:S(2)}) copy-start(s32[32]{0:T(128)} %partner_ref.1) | copy-start | bytes 388
  80.0 58.0 %copy-start.6 = (bf16[1,256,512]{2,1,0:T(8,128)(2,1)S(1)}, bf16[1,256,512]{2,1,0:T(8,128)(2,1)}, u32[]{:S(2)}) copy-start(bf16[1,256,512]{2,1,0:T(8,128)(2,1)} %param.14) | copy-start | bytes 786436
  80.0 8.6 %collective-permute-start.14 = (bf16[256,512]{1,0:T(8,128)(2,1)S(1)}, bf16[256,512]{1,0:T(8,128)(2,1)S(1)}, u32[]{:S(2)}, u32[]{:S(2)}) collective-permute-start(bf16[256,512]{1,0:T(8,128)(2,1)S(1)} %get-tuple-element.27), channel_id=1, source_target_pairs={{0,14},{1,9},{8,0},{9,3},{2,8},{3,11},{10,2},{11,5},{4,10},{5,13},... | collective-permute-start | bytes 786440 | tf_op jit(solution)/shard_map/ppermute | solution.py:34
  84.8 8.9 %collective-permute-start.15 = (bf16[256,512]{1,0:T(8,128)(2,1)S(1)}, bf16[256,512]{1,0:T(8,128)(2,1)S(1)}, u32[]{:S(2)}, u32[]{:S(2)}) collective-permute-start(bf16[256,512]{1,0:T(8,128)(2,1)S(1)} %get-tuple-element.28), channel_id=1, source_target_pairs={{0,15},{1,8},{8,1},{9,2},{2,9},{3,10},{10,3},{11,4},{4,11},{5,12},... | collective-permute-start | bytes 786440 | tf_op jit(solution)/shard_map/ppermute | solution.py:34
Sparse Core Ops, SparseCore 0:
  11.2 112.3 all-gather.1
